TPU v7x, 32 devices: a whole 2x2x4 slice. The times are simulated.
32 devices in a mesh: fsdp: 8 (over z, y), expert: 4 (over x, core).
Axes of the slice: x: 2, y: 2, z: 4, core: 2. Of those that a mesh axis runs over, the one named last changes fastest.
Arguments:
- tokens: bfloat16 [32768, 768], P(('fsdp', 'expert')), may hold values from -6 to 6
- cotangent: bfloat16 [32768, 768], P(('fsdp', 'expert')), may hold values from -6 to 6
- prev_logits: bfloat16 [32768, 12], P(('fsdp', 'expert')), may hold values from -3 to 3
- routes: int32 [32768, 2], P(('fsdp', 'expert')), may hold values from 0 to 11, all different within a row
- capacity: int32 [8], replicated, may hold values from 64 to 128
- segments: int32 [32768], P(('fsdp', 'expert')), may hold values from 0 to 63, as said below
- positions: int32 [32768], P(('fsdp', 'expert')), may hold values from 0 to 511, as said below
- w_qkv: bfloat16 [768, 2304], P('fsdp'), may hold values from -0.21875 to 0.21875
- w_out: bfloat16 [768, 768], P('fsdp'), may hold values from -0.625 to 0.625
- gate_matrix: bfloat16 [768, 16], P('fsdp'), may hold values from -0.109375 to 0.109375
- const_values: bfloat16 [768, 2], P('fsdp'), may hold values from -5 to 5
- attn_gain: bfloat16 [768], P('fsdp'), may hold values from 0.5 to 1.5
- moe_gain: bfloat16 [768], P('fsdp'), may hold values from 0.5 to 1.5
- w_gate_up: bfloat16 [8, 768, 4096], P('expert', 'fsdp'), may hold values from -0.21875 to 0.21875
- w_down: bfloat16 [8, 2048, 768], P('expert', 'fsdp'), may hold values from -0.125 to 0.125
Outputs:
- output: bfloat16 [32768, 768], P(('fsdp', 'expert'))
- input_grad: float32 [32768, 768], P(('fsdp', 'expert'))
- prev_logits_grad: float32 [32768, 12], P(('fsdp', 'expert'))
- w_qkv_grad: float32 [768, 2304], P('fsdp')
- w_out_grad: float32 [768, 768], P('fsdp')
- gate_matrix_grad: float32 [768, 16], P('fsdp')
- const_values_grad: float32 [768, 2], P('fsdp')
- attn_gain_grad: float32 [768], P('fsdp')
- moe_gain_grad: float32 [768], P('fsdp')
- w_gate_up_grad: float32 [8, 768, 4096], P('expert', 'fsdp')
- w_down_grad: float32 [8, 2048, 768], P('expert', 'fsdp')
Inputs may be any that keep to these rules, and one draw needn't show every extreme that they name: The two routes of a token differ; 0 to 7 are SwiGLU experts, 8 the zero expert, 9 the copy expert, 10 and 11 the constant experts. `segments`: within each aligned block of 512 tokens the numbers start at 0 and rise by one at each new document; documents start only at multiples of 8 within the block; the first block is one document, and in the second block a document starts at every multiple of 8. `positions`: 0 at a document's first token, rising by one along it.
All inputs are finite; a program needn't handle non-finite values.
Results may differ from a plain program's by a relative error of at most 0.02.
Values may be sent and summed in bfloat16 or wider, within the bound.
No kernel may reach another device: no remote copies, remote signals or barrier semaphores. Data moves between devices by JAX's collectives and lax.ppermute only.
A program may use at most 160 MiB of HBM per device.

v0:
```python
import math

import jax
import jax.numpy as jnp
from jax import lax
from jax.sharding import PartitionSpec as P

D = 768
HEADS = 12
HEAD_DIM = 64
FF = 2048
EXPERTS = 8
SEQ = 512
MB = 2
CAP = 128


EPSILON = 1e-05
ROPE_BASE = 10000.0
FLOOR_SCORE = -1e30
HIGHEST = lax.Precision.HIGHEST


def pair_tables(route, capacity):
    choice_ids = jnp.arange(EXPERTS + 4, dtype=jnp.int32)
    flat_routes = route.reshape(-1)
    route_flags = (flat_routes[:, None] == choice_ids[None, :]).astype(jnp.int32)
    earlier = jnp.cumsum(route_flags, axis=0, dtype=jnp.int32) - route_flags
    slot_rank = jnp.sum(earlier * route_flags, axis=1, dtype=jnp.int32)
    cap_limit = jnp.sum(route_flags[:, :EXPERTS] * capacity[None, :], axis=1, dtype=jnp.int32)
    kept_pairs = (flat_routes < EXPERTS) & (slot_rank < cap_limit)
    slot_index = jnp.where(kept_pairs, flat_routes * CAP + slot_rank, -1).reshape(route.shape)
    route_hot = route_flags.reshape(route.shape[0], 2, EXPERTS + 4).astype(jnp.float32)
    copy_mask = route_hot[:, :, EXPERTS + 1]
    const_mask = route_hot[:, :, EXPERTS + 2 :]
    return (slot_index, route_hot, copy_mask, const_mask)


def rope_tables(position, head_dim):
    half_dim = head_dim // 2
    frequency = jnp.exp(
        jnp.arange(half_dim, dtype=jnp.float32) * (-2.0 * math.log(ROPE_BASE) / head_dim)
    )
    angles = position.astype(jnp.float32)[:, None] * frequency[None, :]
    return (jnp.cos(angles)[:, None, :], jnp.sin(angles)[:, None, :])


def rotate(values, cosine, sine_part):
    half_dim = values.shape[-1] // 2
    first_half, second_half = (values[..., :half_dim], values[..., half_dim:])
    return jnp.concatenate(
        [
            first_half * cosine - second_half * sine_part,
            first_half * sine_part + second_half * cosine,
        ],
        axis=-1,
    )


def rotate_back(grads_in, cosine, sine_part):
    half_dim = grads_in.shape[-1] // 2
    first_half, second_half = (grads_in[..., :half_dim], grads_in[..., half_dim:])
    return jnp.concatenate(
        [
            first_half * cosine + second_half * sine_part,
            second_half * cosine - first_half * sine_part,
        ],
        axis=-1,
    )


def norm_forward(inputs, gain):
    inverse = lax.rsqrt(jnp.mean(inputs * inputs, axis=-1, keepdims=True) + EPSILON)
    return (inputs * inverse * gain, inverse)


def norm_backward(inputs, inverse, gain, grad_in):
    scaled = grad_in * gain
    gain_grad = jnp.sum(grad_in * inputs * inverse, axis=0)
    inner_mean = jnp.mean(scaled * inputs, axis=-1, keepdims=True)
    return (inverse * scaled - inputs * inverse * inverse * inverse * inner_mean, gain_grad)


def masked_scores(query_rot, key_rot, allowed, score_scale):
    scores = (
        jnp.einsum("qhd,khd->hqk", query_rot, key_rot, preferred_element_type=jnp.float32)
        * score_scale
    )
    return jnp.where(allowed[None], scores, FLOOR_SCORE)


def micro_step(
    inputs_low, cot_low, prev_low, route, capacity, segment, position, mixer_now, expert_now
):
    w_qkv, w_out, gate_matrix, const_values, attn_gain, moe_gain = mixer_now
    w_gate_up, w_down = expert_now
    owners = lax.axis_size("expert")
    local_count = w_gate_up.shape[0]
    choices_count = EXPERTS + 4
    score_scale = 1.0 / math.sqrt(HEAD_DIM)
    inputs = inputs_low.astype(jnp.float32)
    gain_one = attn_gain.astype(jnp.float32)
    gain_two = moe_gain.astype(jnp.float32)
    normed_one, inverse_one = norm_forward(inputs, gain_one)
    act_one = normed_one.astype(jnp.bfloat16)
    qkv = jnp.dot(act_one, w_qkv, preferred_element_type=jnp.float32)
    cosine, sine_part = rope_tables(position, HEAD_DIM)
    query_rot = rotate(qkv[:, :D].reshape(SEQ, HEADS, HEAD_DIM), cosine, sine_part).astype(
        jnp.bfloat16
    )
    key_rot = rotate(qkv[:, D : 2 * D].reshape(SEQ, HEADS, HEAD_DIM), cosine, sine_part).astype(
        jnp.bfloat16
    )
    value_low = qkv[:, 2 * D :].reshape(SEQ, HEADS, HEAD_DIM).astype(jnp.bfloat16)
    seq_index = jnp.arange(SEQ, dtype=jnp.int32)
    allowed = (seq_index[:, None] >= seq_index[None, :]) & (segment[:, None] == segment[None, :])
    scores = masked_scores(query_rot, key_rot, allowed, score_scale)
    row_max = jnp.max(scores, axis=-1, keepdims=True)
    log_total = row_max + jnp.log(jnp.sum(jnp.exp(scores - row_max), axis=-1, keepdims=True))
    prob_low = jnp.exp(scores - log_total).astype(jnp.bfloat16)
    attended = jnp.einsum("hqk,khd->qhd", prob_low, value_low, preferred_element_type=jnp.float32)
    attended_low = attended.reshape(SEQ, D).astype(jnp.bfloat16)
    residual = inputs + jnp.dot(attended_low, w_out, preferred_element_type=jnp.float32)
    normed_two, inverse_two = norm_forward(residual, gain_two)
    act_two = normed_two.astype(jnp.bfloat16)
    logits_all = jnp.dot(act_two, gate_matrix, preferred_element_type=jnp.float32)
    router = logits_all[:, :choices_count] + prev_low.astype(jnp.float32)
    slot_index, route_hot, copy_mask, const_mask = pair_tables(route, capacity)
    gates = jax.nn.softmax(jnp.sum(router[:, None, :] * route_hot, axis=-1), axis=1)
    const_gates = jax.nn.softmax(logits_all[:, choices_count:].reshape(SEQ, 2, 2), axis=-1)
    const_vec = const_values.astype(jnp.float32)
    slot_ids = jnp.arange(EXPERTS * CAP, dtype=jnp.int32)
    pick_table = (slot_index[None, :, :] == slot_ids[:, None, None]).astype(jnp.bfloat16)
    carry_low = jnp.sum(pick_table, axis=2)
    send_rows = jnp.dot(carry_low, act_two, preferred_element_type=jnp.float32).astype(jnp.bfloat16)
    received = lax.all_to_all(
        send_rows.reshape(owners, local_count, CAP, D),
        "expert",
        split_axis=0,
        concat_axis=0,
        tiled=True,
    )
    gate_up = jnp.einsum("slcd,ldf->slcf", received, w_gate_up, preferred_element_type=jnp.float32)
    gate_part = gate_up[..., :FF]
    up_part = gate_up[..., FF:]
    gate_sigmoid = jax.nn.sigmoid(gate_part)
    activated = gate_part * gate_sigmoid
    hidden_low = (activated * up_part).astype(jnp.bfloat16)
    produced = jnp.einsum(
        "slcf,lfd->slcd", hidden_low, w_down, preferred_element_type=jnp.float32
    ).astype(jnp.bfloat16)
    returned = lax.all_to_all(produced, "expert", split_axis=0, concat_axis=0, tiled=True).reshape(
        EXPERTS * CAP, D
    )
    combined = jnp.einsum("esk,ed->skd", pick_table, returned, preferred_element_type=jnp.float32)
    const_out = (
        const_gates[..., 0:1] * normed_two[:, None, :]
        + const_gates[..., 1:2] * const_vec.T[None, :, :]
    )
    term = combined + copy_mask[..., None] * normed_two[:, None, :]
    term = (
        term
        + const_mask[:, :, 0, None] * const_out[:, None, 0, :]
        + const_mask[:, :, 1, None] * const_out[:, None, 1, :]
    )
    output = residual + jnp.sum(gates[..., None] * term, axis=1)
    grad_out = cot_low.astype(jnp.float32)
    gate_grad = jnp.sum(grad_out[:, None, :] * term, axis=-1)
    term_grad = gates[..., None] * grad_out[:, None, :]
    term_grad_low = term_grad.astype(jnp.bfloat16)
    slot_grad = jnp.einsum(
        "esk,skd->ed", pick_table, term_grad_low, preferred_element_type=jnp.float32
    ).astype(jnp.bfloat16)
    grad_rows = lax.all_to_all(
        slot_grad.reshape(owners, local_count, CAP, D),
        "expert",
        split_axis=0,
        concat_axis=0,
        tiled=True,
    )
    hidden_grad = jnp.einsum(
        "slcd,lfd->slcf", grad_rows, w_down, preferred_element_type=jnp.float32
    ).astype(jnp.bfloat16)
    down_wgrad = jnp.einsum(
        "slcf,slcd->lfd", hidden_low, grad_rows, preferred_element_type=jnp.float32
    )
    hidden_wide = hidden_grad.astype(jnp.float32)
    gate_part_grad = hidden_wide * up_part * gate_sigmoid * (1.0 + gate_part * (1.0 - gate_sigmoid))
    up_part_grad = hidden_wide * activated
    gate_up_grad = jnp.concatenate([gate_part_grad, up_part_grad], axis=-1).astype(jnp.bfloat16)
    gate_up_wgrad = jnp.einsum(
        "slcd,slcf->ldf", received, gate_up_grad, preferred_element_type=jnp.float32
    )
    row_grad = jnp.einsum(
        "slcf,ldf->slcd", gate_up_grad, w_gate_up, preferred_element_type=jnp.float32
    ).astype(jnp.bfloat16)
    back_rows = lax.all_to_all(row_grad, "expert", split_axis=0, concat_axis=0, tiled=True).reshape(
        EXPERTS * CAP, D
    )
    dispatch_grad = jnp.einsum(
        "es,ed->sd", carry_low, back_rows, preferred_element_type=jnp.float32
    )
    direct_weight = (
        copy_mask
        + const_mask[:, :, 0] * const_gates[:, None, 0, 0]
        + const_mask[:, :, 1] * const_gates[:, None, 1, 0]
    )
    direct_grad = jnp.sum(direct_weight[..., None] * term_grad, axis=1)
    along_normed = jnp.sum(term_grad * normed_two[:, None, :], axis=-1)
    along_vector = jnp.einsum("skd,dc->skc", term_grad, const_vec, precision=HIGHEST)
    in_normed = jnp.sum(const_mask * along_normed[..., None], axis=1)
    in_vector = jnp.sum(const_mask * along_vector, axis=1)
    const_in_grad = jnp.stack([in_normed, in_vector], axis=-1)
    const_logit_grad = const_gates * (
        const_in_grad - jnp.sum(const_gates * const_in_grad, axis=-1, keepdims=True)
    )
    vector_wgrad = jnp.einsum(
        "skc,skd->dc", const_mask * const_gates[:, None, :, 1], term_grad, precision=HIGHEST
    )
    picked_grad = gates * (gate_grad - jnp.sum(gates * gate_grad, axis=1, keepdims=True))
    router_grad = jnp.sum(picked_grad[..., None] * route_hot, axis=1)
    logit_grad = jnp.concatenate([router_grad, const_logit_grad.reshape(SEQ, 4)], axis=1).astype(
        jnp.bfloat16
    )
    gate_wgrad = jnp.dot(act_two.T, logit_grad, preferred_element_type=jnp.float32)
    router_back = jnp.dot(logit_grad, gate_matrix.T, preferred_element_type=jnp.float32)
    normed_grad = router_back + dispatch_grad + direct_grad
    residual_norm_grad, gain_two_grad = norm_backward(residual, inverse_two, gain_two, normed_grad)
    residual_grad = grad_out + residual_norm_grad
    out_grad_low = residual_grad.astype(jnp.bfloat16)
    out_wgrad = jnp.dot(attended_low.T, out_grad_low, preferred_element_type=jnp.float32)
    attended_grad = (
        jnp.dot(out_grad_low, w_out.T, preferred_element_type=jnp.float32)
        .astype(jnp.bfloat16)
        .reshape(SEQ, HEADS, HEAD_DIM)
    )
    prob_full = jnp.exp(masked_scores(query_rot, key_rot, allowed, score_scale) - log_total)
    prob_grad = jnp.einsum(
        "qhd,khd->hqk", attended_grad, value_low, preferred_element_type=jnp.float32
    )
    row_inner = jnp.sum(prob_full * prob_grad, axis=-1, keepdims=True)
    score_grad = (prob_full * (prob_grad - row_inner)).astype(jnp.bfloat16)
    query_grad = (
        jnp.einsum("hqk,khd->qhd", score_grad, key_rot, preferred_element_type=jnp.float32)
        * score_scale
    )
    key_grad = (
        jnp.einsum("hqk,qhd->khd", score_grad, query_rot, preferred_element_type=jnp.float32)
        * score_scale
    )
    value_grad = jnp.einsum(
        "hqk,qhd->khd", prob_low, attended_grad, preferred_element_type=jnp.float32
    )
    qkv_grad = jnp.concatenate(
        [
            rotate_back(query_grad, cosine, sine_part).reshape(SEQ, D),
            rotate_back(key_grad, cosine, sine_part).reshape(SEQ, D),
            value_grad.reshape(SEQ, D),
        ],
        axis=1,
    ).astype(jnp.bfloat16)
    qkv_wgrad = jnp.dot(act_one.T, qkv_grad, preferred_element_type=jnp.float32)
    act_one_grad = jnp.dot(qkv_grad, w_qkv.T, preferred_element_type=jnp.float32)
    input_norm_grad, gain_one_grad = norm_backward(inputs, inverse_one, gain_one, act_one_grad)
    input_grad = residual_grad + input_norm_grad
    mixer_grads_now = (qkv_wgrad, out_wgrad, gate_wgrad, vector_wgrad, gain_one_grad, gain_two_grad)
    expert_grads_now = (gate_up_wgrad, down_wgrad)
    return (output.astype(jnp.bfloat16), input_grad, router_grad, mixer_grads_now, expert_grads_now)


def on_device(
    tokens,
    cotangent,
    prev_logits,
    routes,
    capacity,
    segments,
    positions,
    w_qkv,
    w_out,
    gate_matrix,
    const_values,
    attn_gain,
    moe_gain,
    w_gate_up,
    w_down,
):
    output_parts = []
    input_parts = []
    router_parts = []
    mixer_sums = None
    expert_sums = None
    for micro_index in range(MB):
        mixer_now = (
            lax.all_gather(w_qkv, "fsdp", axis=0, tiled=True),
            lax.all_gather(w_out, "fsdp", axis=0, tiled=True),
            lax.all_gather(gate_matrix, "fsdp", axis=0, tiled=True),
            lax.all_gather(const_values, "fsdp", axis=0, tiled=True),
            lax.all_gather(attn_gain, "fsdp", axis=0, tiled=True),
            lax.all_gather(moe_gain, "fsdp", axis=0, tiled=True),
        )
        expert_now = (
            lax.all_gather(w_gate_up, "fsdp", axis=1, tiled=True),
            lax.all_gather(w_down, "fsdp", axis=1, tiled=True),
        )
        row_span = slice(micro_index * SEQ, (micro_index + 1) * SEQ)
        result = micro_step(
            tokens[row_span],
            cotangent[row_span],
            prev_logits[row_span],
            routes[row_span],
            capacity,
            segments[row_span],
            positions[row_span],
            mixer_now,
            expert_now,
        )
        output_parts.append(result[0])
        input_parts.append(result[1])
        router_parts.append(result[2])
        if micro_index == 0:
            mixer_sums = result[3]
            expert_sums = result[4]
        else:
            mixer_sums = jax.tree.map(jnp.add, mixer_sums, result[3])
            expert_sums = jax.tree.map(jnp.add, expert_sums, result[4])
    shared = (
        lax.psum_scatter(
            mixer_sums[0].astype(jnp.bfloat16), "fsdp", scatter_dimension=0, tiled=True
        ).astype(jnp.float32),
        lax.psum_scatter(
            mixer_sums[1].astype(jnp.bfloat16), "fsdp", scatter_dimension=0, tiled=True
        ).astype(jnp.float32),
        lax.psum_scatter(
            mixer_sums[2].astype(jnp.bfloat16), "fsdp", scatter_dimension=0, tiled=True
        ).astype(jnp.float32),
        lax.psum_scatter(
            mixer_sums[3].astype(jnp.bfloat16), "fsdp", scatter_dimension=0, tiled=True
        ).astype(jnp.float32),
        lax.psum_scatter(
            mixer_sums[4].astype(jnp.bfloat16), "fsdp", scatter_dimension=0, tiled=True
        ).astype(jnp.float32),
        lax.psum_scatter(
            mixer_sums[5].astype(jnp.bfloat16), "fsdp", scatter_dimension=0, tiled=True
        ).astype(jnp.float32),
    )
    shared = (
        lax.psum(shared[0].astype(jnp.bfloat16), "expert").astype(jnp.float32),
        lax.psum(shared[1].astype(jnp.bfloat16), "expert").astype(jnp.float32),
        lax.psum(shared[2].astype(jnp.bfloat16), "expert").astype(jnp.float32),
        lax.psum(shared[3].astype(jnp.bfloat16), "expert").astype(jnp.float32),
        lax.psum(shared[4].astype(jnp.bfloat16), "expert").astype(jnp.float32),
        lax.psum(shared[5].astype(jnp.bfloat16), "expert").astype(jnp.float32),
    )
    expert_total = (
        lax.psum_scatter(
            expert_sums[0].astype(jnp.bfloat16), "fsdp", scatter_dimension=1, tiled=True
        ).astype(jnp.float32),
        lax.psum_scatter(
            expert_sums[1].astype(jnp.bfloat16), "fsdp", scatter_dimension=1, tiled=True
        ).astype(jnp.float32),
    )
    return (
        jnp.concatenate(output_parts, axis=0),
        jnp.concatenate(input_parts, axis=0),
        jnp.concatenate(router_parts, axis=0),
        shared[0],
        shared[1],
        shared[2],
        shared[3],
        shared[4],
        shared[5],
        expert_total[0],
        expert_total[1],
    )


def solution(mesh):
    return jax.shard_map(
        on_device,
        mesh=mesh,
        in_specs=(
            P(("fsdp", "expert"), None),
            P(("fsdp", "expert"), None),
            P(("fsdp", "expert"), None),
            P(("fsdp", "expert"), None),
            P(),
            P(("fsdp", "expert")),
            P(("fsdp", "expert")),
            P("fsdp", None),
            P("fsdp", None),
            P("fsdp", None),
            P("fsdp", None),
            P("fsdp"),
            P("fsdp"),
            P("expert", "fsdp", None),
            P("expert", "fsdp", None),
        ),
        out_specs=(
            P(("fsdp", "expert"), None),
            P(("fsdp", "expert"), None),
            P(("fsdp", "expert"), None),
            P("fsdp", None),
            P("fsdp", None),
            P("fsdp", None),
            P("fsdp", None),
            P("fsdp"),
            P("fsdp"),
            P("expert", "fsdp", None),
            P("expert", "fsdp", None),
        ),
        check_vma=False,
    )
```

profile of v0, /device:TPU:1, one launch (start us, length us, event | category | flops | bytes accessed | tf_op | source)
XLA Modules:
  0.0 1294.3 jit_solution(7311858620719880376)
XLA Ops:
  10.6 18.0 %all-gather.1 = bf16[8,96,2]{1,2,0:T(2,128)(2,1)S(1)} all-gather(bf16[1,96,2]{1,2,0:T(2,128)(2,1)} %bitcast.360), channel_id=1, replica_groups=mesh['fsdp'=8,'expert'=4] {'fsdp'}, dimensions={0}, use_global_device_ids=true | all-gather | bytes 3456 | tf_op jit(solution)/shard_map/all_gather | solution.py:298
  33.0 13.8 %all-reduce.5 = (bf16[768]{0:T(1024)(128)(2,1)S(1)}, bf16[768]{0:T(1024)(128)(2,1)S(1)}) all-reduce(bf16[768]{0:T(1024)(128)(2,1)S(1)} %dynamic-update-slice, bf16[768]{0:T(1024)(128)(2,1)S(1)} %dynamic-update-slice.1), channel_id=1, replica_groups=mesh['fsdp'=8,'expert'=4] {'fsdp'}, use_global_device_ids=true, to_apply=%add | all-reduce | flops 1536 | bytes 6144
  50.1 24.6 %all-gather = bf16[8,96,16]{1,2,0:T(8,128)(2,1)S(1)} all-gather(bf16[1,96,16]{1,2,0:T(8,128)(2,1)S(1)} %bitcast.351), channel_id=1, replica_groups=mesh['fsdp'=8,'expert'=4] {'fsdp'}, dimensions={0}, use_global_device_ids=true | all-gather | bytes 27648 | tf_op jit(solution)/shard_map/all_gather | solution.py:297
  171.4 18.1 %all-to-all-start.2 = ((bf16[4,2,128,768]{3,2,1,0:T(8,128)(2,1)}), bf16[4,2,128,768]{3,2,1,0:T(8,128)(2,1)}, u32[]{:S(2)}, u32[]{:S(2)}) async-start(bf16[4,2,128,768]{3,2,1,0:T(8,128)(2,1)} %bitcast.318), calls=%async_computation.2 | async-start | bytes 3145728 | tf_op jit(solution)/shard_map/all_to_all | solution.py:136
  217.7 79.2 %all-gather.11.cloned.1.call-done = bf16[2,768,4096]{2,1,0:T(8,128)(2,1)} async-done(((bf16[2,96,4096]{2,1,0:T(8,128)(2,1)}), bf16[2,768,4096]{2,1,0:T(8,128)(2,1)}) %all-gather.11.cloned.1.call-update) | async-done | bytes 12582928 | tf_op jit(solution)/shard_map/all_gather | solution.py:303
  296.9 15.0 %fusion.24 = f32[4,2,128,4096]{3,2,0,1:T(8,128)} fusion(bf16[2,768,4096]{2,1,0:T(8,128)(2,1)} %all-gather.11.cloned.1.call-done, bf16[4,2,128,768]{3,2,1,0:T(8,128)(2,1)} %all-to-all-done.2), kind=kOutput, calls=%fused_computation.40 | convolution fusion | flops 6442450944 | bytes 30932992 | tf_op jit(solution)/shard_map/slcd,ldf->slcf/dot_general | solution.py:143
  317.5 78.6 %all-gather.13.cloned.1.call-done = bf16[2,2048,768]{2,1,0:T(8,128)(2,1)} async-done(((bf16[2,256,768]{2,1,0:T(8,128)(2,1)}), bf16[2,2048,768]{2,1,0:T(8,128)(2,1)}) %all-gather.13.cloned.1.call-update) | async-done | bytes 6291472 | tf_op jit(solution)/shard_map/all_gather | solution.py:304
  396.1 14.0 %fusion.29 = (bf16[4,2,128,2048]{3,2,0,1:T(8,128)(2,1)}, bf16[4,2,128,2048]{3,2,0,1:T(8,128)(2,1)}, bf16[4,2,128,2048]{3,2,0,1:T(8,128)(2,1)}) fusion(f32[4,2,128,4096]{3,2,0,1:T(8,128)} %fusion.24, bf16[2,2048,768]{2,1,0:T(8,128)(2,1)} %all-gather.13.cloned.1.call-done, bf16[4,2,128,768]{3,2,1,0:T(8,128)(2,1)} %all-to-all-done.6), kind=kOutput, calls=%fused_computation.47 | convolution fusion | flops 3256877056 | bytes 37224448 | tf_op jit(solution)/shard_map/slcd,lfd->slcf/dot_general | solution.py:181
  424.3 15.0 %fusion.21 = f32[4,2,128,4096]{3,2,0,1:T(8,128)} fusion(bf16[2,768,4096]{2,1,0:T(8,128)(2,1)} %all-gather.11.cloned.1.call-done, bf16[4,2,128,768]{3,2,1,0:T(8,128)(2,1)} %all-to-all-done), kind=kOutput, calls=%fused_computation.39 | convolution fusion | flops 6442450944 | bytes 30932992 | tf_op jit(solution)/shard_map/slcd,ldf->slcf/dot_general | solution.py:143
  449.2 14.0 %fusion.33 = (bf16[4,2,128,2048]{3,2,0,1:T(8,128)(2,1)}, bf16[4,2,128,2048]{3,2,0,1:T(8,128)(2,1)}, bf16[4,2,128,2048]{3,2,0,1:T(8,128)(2,1)}) fusion(f32[4,2,128,4096]{3,2,0,1:T(8,128)} %fusion.21, bf16[2,2048,768]{2,1,0:T(8,128)(2,1)} %all-gather.13.cloned.1.call-done, bf16[4,2,128,768]{3,2,1,0:T(8,128)(2,1)} %all-to-all-done.4), kind=kOutput, calls=%fused_computation.53 | convolution fusion | flops 3256877056 | bytes 37224448 | tf_op jit(solution)/shard_map/slcd,lfd->slcf/dot_general | solution.py:181
  472.0 13.7 %fusion.120 = bf16[4,2,128,768]{3,2,0,1:T(8,128)(2,1)} fusion(bf16[2,768,4096]{2,1,0:T(8,128)(2,1)} %all-gather.11.cloned.1.call-done, bf16[4,2,128,2048]{3,2,0,1:T(8,128)(2,1)} %get-tuple-element.46, bf16[4,2,128,2048]{3,2,0,1:T(8,128)(2,1)} %get-tuple-element.45), kind=kOutput, calls=%fused_computation.184 | convolution fusion | flops 6460014592 | bytes 22544384 | tf_op jit(solution)/shard_map/slcf,ldf->slcd/dot_general | solution.py:194
  490.2 13.7 %fusion.123 = bf16[4,2,128,768]{3,2,0,1:T(8,128)(2,1)} fusion(bf16[2,768,4096]{2,1,0:T(8,128)(2,1)} %all-gather.11.cloned.1.call-done, bf16[4,2,128,2048]{3,2,0,1:T(8,128)(2,1)} %get-tuple-element.44, bf16[4,2,128,2048]{3,2,0,1:T(8,128)(2,1)} %get-tuple-element.43), kind=kOutput, calls=%fused_computation.185 | convolution fusion | flops 6460014592 | bytes 22544384 | tf_op jit(solution)/shard_map/slcf,ldf->slcd/dot_general | solution.py:194
  549.0 15.0 %all-to-all-done.5 = bf16[4,2,128,768]{3,2,1,0:T(8,128)(2,1)} async-done(((bf16[4,2,128,768]{3,2,1,0:T(8,128)(2,1)}), bf16[4,2,128,768]{3,2,1,0:T(8,128)(2,1)}, u32[]{:S(2)}, u32[]{:S(2)}) %all-to-all-start.5) | async-done | bytes 1572896 | tf_op jit(solution)/shard_map/all_to_all | solution.py:197
  579.1 13.6 %multiply_reduce_fusion = (f32[12,512]{1,0:T(8,128)S(1)}, f32[12,512,512]{1,2,0:T(8,128)}) fusion(f32[12,512,512]{1,2,0:T(8,128)} %copy-done, f32[12,512]{1,0:T(8,128)S(1)} %copy-done.83, pred[512,512]{0,1:T(8,128)(4,1)S(1)} %copy-done.24, bf16[512,12,64]{0,2,1:T(8,128)(2,1)} %bitcast.314, bf16[512,12,64]{0,2,1:T(8,128)(2,1)} %bitcast.312), kind=kOutput, calls=%fused_computation.14 | convolution fusion | flops 418375680 | bytes 27049984 | tf_op jit(solution)/shard_map/qhd,khd->hqk/dot_general | solution.py:238
  691.3 14.3 %reduce-scatter.13.cloned.1.call-done = bf16[96,768]{1,0:T(8,128)(2,1)} async-done(((bf16[768,768]{1,0:T(8,128)(2,1)}), bf16[96,768]{1,0:T(8,128)(2,1)}) %reduce-scatter.13.cloned.1.call-update) | async-done | bytes 147472 | tf_op jit(solution)/shard_map/reduce_scatter | solution.py:331
  705.6 82.8 %reduce-scatter.11.cloned.1.call-done = bf16[96,2304]{1,0:T(8,128)(2,1)} async-done(((bf16[768,2304]{1,0:T(8,128)(2,1)}), bf16[96,2304]{1,0:T(8,128)(2,1)}) %reduce-scatter.11.cloned.1.call-update) | async-done | bytes 442384 | tf_op jit(solution)/shard_map/reduce_scatter | solution.py:328
  788.5 12.4 fusion.2
  801.2 19.1 %fusion.36 = f32[2,768,4096,1]{2,1,0,3:T(8,128)} fusion(bf16[4,2,128,768]{3,2,1,0:T(8,128)(2,1)} %all-to-all-done, bf16[4,2,128,2048]{3,2,0,1:T(8,128)(2,1)} %get-tuple-element.44, bf16[4,2,128,2048]{3,2,0,1:T(8,128)(2,1)} %get-tuple-element.43), kind=kOutput, calls=%fused_computation.56 | convolution fusion | flops 6459228160 | bytes 35127296 | tf_op jit(solution)/shard_map/slcd,slcf->ldf/dot_general | solution.py:191
  820.3 19.9 %fusion.1 = bf16[2,768,4096]{2,1,0:T(8,128)(2,1)} fusion(f32[2,768,4096,1]{2,1,0,3:T(8,128)} %fusion.36, bf16[4,2,128,768]{3,2,1,0:T(8,128)(2,1)} %all-to-all-done.2, bf16[4,2,128,2048]{3,2,0,1:T(8,128)(2,1)} %get-tuple-element.46, bf16[4,2,128,2048]{3,2,0,1:T(8,128)(2,1)} %get-tuple-element.45), kind=kOutput, calls=%fused_computation.2 | convolution fusion | flops 6471811072 | bytes 47710208 | tf_op jit(solution)/shard_map/slcd,slcf->ldf/dot_general | solution.py:191
  860.4 16.3 %all-reduce.4 = (bf16[768]{0:T(1024)(128)(2,1)S(1)}, bf16[768]{0:T(1024)(128)(2,1)S(1)}) all-reduce(bf16[768]{0:T(1024)(128)(2,1)S(1)} %add_convert_fusion.13, bf16[768]{0:T(1024)(128)(2,1)S(1)} %add_convert_fusion.12), channel_id=6, replica_groups=mesh['fsdp'=8,'expert'=4] {'fsdp'}, use_global_device_ids=true, to_apply=%region_62.63.clone | all-reduce | flops 1536 | bytes 6144
  884.9 30.3 %reduce-scatter.19.cloned.1.call-done = bf16[96,16]{1,0:T(8,128)(2,1)} async-done(((bf16[768,16]{1,0:T(8,128)(2,1)}), bf16[96,16]{1,0:T(8,128)(2,1)}) %reduce-scatter.19.cloned.1.call-update) | async-done | bytes 3088
  926.0 25.0 %all-reduce.10.cloned.1.call-done = (bf16[96,2304]{1,0:T(8,128)(2,1)}, bf16[96,768]{1,0:T(8,128)(2,1)}) async-done(((bf16[96,2304]{1,0:T(8,128)(2,1)}, bf16[96,768]{1,0:T(8,128)(2,1)}), (bf16[96,2304]{1,0:T(8,128)(2,1)}, bf16[96,768]{1,0:T(8,128)(2,1)})) %all-reduce.10.cloned.1.call-update) | async-done | bytes 589840 | tf_op jit(solution)/shard_map/psum | solution.py:348
  954.6 118.4 %reduce-scatter.17.cloned.1.call-done = bf16[2,256,768]{2,1,0:T(8,128)(2,1)} async-done(((bf16[2,2048,768]{2,1,0:T(8,128)(2,1)}), bf16[2,256,768]{2,1,0:T(8,128)(2,1)}) %reduce-scatter.17.cloned.1.call-update) | async-done | bytes 786448 | tf_op jit(solution)/shard_map/reduce_scatter | solution.py:359
  1075.3 208.5 %reduce-scatter.15.cloned.1.call-done = bf16[2,96,4096]{2,1,0:T(8,128)(2,1)} async-done(((bf16[2,768,4096]{2,1,0:T(8,128)(2,1)}), bf16[2,96,4096]{2,1,0:T(8,128)(2,1)}) %reduce-scatter.15.cloned.1.call-update) | async-done | bytes 1572880 | tf_op jit(solution)/shard_map/reduce_scatter | solution.py:356
  (566 shorter events, 383.2 us)
Async XLA Ops:
  7.3 96.0 %all-gather.7.cloned.1.call-start = ((), (), s32[]{:S(2)}) async-start(), calls=%async_computation.14 | async-start | bytes 3981312 | tf_op jit(solution)/shard_map/all_gather | solution.py:295
  8.0 146.2 %all-gather.9.cloned.1.call-start = ((), (), s32[]{:S(2)}) async-start(), calls=%async_computation.15 | async-start | bytes 1327104 | tf_op jit(solution)/shard_map/all_gather | solution.py:296
  8.7 288.1 %all-gather.11.cloned.1.call-start = ((), (), s32[]{:S(2)}) async-start(), calls=%async_computation.16 | async-start | bytes 14155776 | tf_op jit(solution)/shard_map/all_gather | solution.py:303
  9.5 386.6 %all-gather.13.cloned.1.call-start = ((), (), s32[]{:S(2)}) async-start(), calls=%async_computation.17 | async-start | bytes 7077888 | tf_op jit(solution)/shard_map/all_gather | solution.py:304
  29.7 53.5 %copy-start.27 = (s32[512,2]{1,0:T(8,128)}, s32[512,2]{1,0:T(8,128)S(1)}, u32[]{:S(2)}) copy-start(s32[512,2]{1,0:T(8,128)S(1)} %copy.195) | copy-start | bytes 12292
  47.4 118.5 %copy-start.89 = (f32[768]{0:T(1024)}, f32[768]{0:T(1024)S(1)}, u32[]{:S(2)}) copy-start(f32[768]{0:T(1024)S(1)} %convert_element_type.285) | copy-start | bytes 9220
  102.1 54.5 %copy-start.23 = (pred[512,512]{0,1:T(8,128)(4,1)}, pred[512,512]{0,1:T(8,128)(4,1)S(1)}, u32[]{:S(2)}) copy-start(pred[512,512]{0,1:T(8,128)(4,1)S(1)} %get-tuple-element.143) | copy-start | bytes 786436
  171.4 42.0 %all-to-all-start.2 = ((bf16[4,2,128,768]{3,2,1,0:T(8,128)(2,1)}), bf16[4,2,128,768]{3,2,1,0:T(8,128)(2,1)}, u32[]{:S(2)}, u32[]{:S(2)}) async-start(bf16[4,2,128,768]{3,2,1,0:T(8,128)(2,1)} %bitcast.318), calls=%async_computation.2 | async-start | bytes 3145728 | tf_op jit(solution)/shard_map/all_to_all | solution.py:136
  189.6 330.6 %copy-start.95 = (f32[512,2]{0,1:T(2,128)}, f32[512,2]{0,1:T(2,128)S(1)}, u32[]{:S(2)}) copy-start(f32[512,2]{0,1:T(2,128)S(1)} %fusion.206) | copy-start | bytes 12292
  193.3 314.7 %copy-start.97 = (f32[512,2]{0,1:T(2,128)}, f32[512,2]{0,1:T(2,128)S(1)}, u32[]{:S(2)}) copy-start(f32[512,2]{0,1:T(2,128)S(1)} %fusion.208) | copy-start | bytes 12292
  213.4 98.5 %all-to-all-start.6 = ((bf16[4,2,128,768]{3,2,1,0:T(8,128)(2,1)}), bf16[4,2,128,768]{3,2,1,0:T(8,128)(2,1)}, u32[]{:S(2)}, u32[]{:S(2)}) async-start(bf16[4,2,128,768]{3,2,1,0:T(8,128)(2,1)} %bitcast.321), calls=%async_computation.6 | async-start | bytes 3145728 | tf_op jit(solution)/shard_map/all_to_all | solution.py:174
  311.9 107.0 %all-to-all-start = ((bf16[4,2,128,768]{3,2,1,0:T(8,128)(2,1)}), bf16[4,2,128,768]{3,2,1,0:T(8,128)(2,1)}, u32[]{:S(2)}, u32[]{:S(2)}) async-start(bf16[4,2,128,768]{3,2,1,0:T(8,128)(2,1)} %bitcast.319), calls=%async_computation | async-start | bytes 3145728 | tf_op jit(solution)/shard_map/all_to_all | solution.py:136
  418.8 24.8 %all-to-all-start.4 = ((bf16[4,2,128,768]{3,2,1,0:T(8,128)(2,1)}), bf16[4,2,128,768]{3,2,1,0:T(8,128)(2,1)}, u32[]{:S(2)}, u32[]{:S(2)}) async-start(bf16[4,2,128,768]{3,2,1,0:T(8,128)(2,1)} %bitcast.320), calls=%async_computation.4 | async-start | bytes 3145728 | tf_op jit(solution)/shard_map/all_to_all | solution.py:174
  443.6 42.0 %all-to-all-start.3 = ((bf16[4,2,128,768]{3,2,1,0:T(8,128)(2,1)}), bf16[4,2,128,768]{3,2,1,0:T(8,128)(2,1)}, u32[]{:S(2)}, u32[]{:S(2)}) async-start(bf16[4,2,128,768]{3,2,1,0:T(8,128)(2,1)} %copy.137), calls=%async_computation.3 | async-start | bytes 3145728 | tf_op jit(solution)/shard_map/all_to_all | solution.py:152
  485.6 30.1 %all-to-all-start.1 = ((bf16[4,2,128,768]{3,2,1,0:T(8,128)(2,1)}), bf16[4,2,128,768]{3,2,1,0:T(8,128)(2,1)}, u32[]{:S(2)}, u32[]{:S(2)}) async-start(bf16[4,2,128,768]{3,2,1,0:T(8,128)(2,1)} %copy.124), calls=%async_computation.1 | async-start | bytes 3145728 | tf_op jit(solution)/shard_map/all_to_all | solution.py:152
  515.7 23.7 %all-to-all-start.7 = ((bf16[4,2,128,768]{3,2,1,0:T(8,128)(2,1)}), bf16[4,2,128,768]{3,2,1,0:T(8,128)(2,1)}, u32[]{:S(2)}, u32[]{:S(2)}) async-start(bf16[4,2,128,768]{3,2,1,0:T(8,128)(2,1)} %copy.150), calls=%async_computation.7 | async-start | bytes 3145728 | tf_op jit(solution)/shard_map/all_to_all | solution.py:197
  539.4 24.5 %all-to-all-start.5 = ((bf16[4,2,128,768]{3,2,1,0:T(8,128)(2,1)}), bf16[4,2,128,768]{3,2,1,0:T(8,128)(2,1)}, u32[]{:S(2)}, u32[]{:S(2)}) async-start(bf16[4,2,128,768]{3,2,1,0:T(8,128)(2,1)} %copy.141), calls=%async_computation.5 | async-start | bytes 3145728 | tf_op jit(solution)/shard_map/all_to_all | solution.py:197
  544.6 161.0 %reduce-scatter.13.cloned.1.call-start = ((), (), s32[]{:S(2)}) async-start(), calls=%async_computation.19 | async-start | bytes 1327104 | tf_op jit(solution)/shard_map/reduce_scatter | solution.py:331
  645.6 142.8 %reduce-scatter.11.cloned.1.call-start = ((), (), s32[]{:S(2)}) async-start(), calls=%async_computation.18 | async-start | bytes 3981312 | tf_op jit(solution)/shard_map/reduce_scatter | solution.py:328
  670.7 180.6 %reduce-scatter.21.cloned.1.call-start = ((), (), s32[]{:S(2)}) async-start(), calls=%async_computation.23 | async-start | bytes 221184
  678.9 236.3 %reduce-scatter.19.cloned.1.call-start = ((), (), s32[]{:S(2)}) async-start(), calls=%async_computation.22 | async-start | bytes 221184
  680.3 270.7 %all-reduce.10.cloned.1.call-start = ((), (), s32[]{:S(2)}) async-start(), calls=%async_computation.24 | async-start | bytes 1179648 | tf_op jit(solution)/shard_map/psum | solution.py:348
  788.4 284.6 %reduce-scatter.17.cloned.1.call-start = ((), (), s32[]{:S(2)}) async-start(), calls=%async_computation.21 | async-start | bytes 7077888 | tf_op jit(solution)/shard_map/reduce_scatter | solution.py:359
  800.9 483.0 %reduce-scatter.15.cloned.1.call-start = ((), (), s32[]{:S(2)}) async-start(), calls=%async_computation.20 | async-start | bytes 14155776 | tf_op jit(solution)/shard_map/reduce_scatter | solution.py:356
  (141 other events, 1088.3 us)
Sparse Core Ops, SparseCore 0:
  10.3 66.8 all-gather.6
  79.4 39.1 all-gather.8
  120.8 176.0 all-gather.10
  298.9 97.1 all-gather.12
  645.7 59.8 reduce-scatter.12
  709.1 79.2 reduce-scatter.10
  792.2 59.0 reduce-scatter.20
  855.1 60.1 reduce-scatter.18
  917.7 33.1 all-reduce.9
  954.4 118.5 reduce-scatter.16
  1076.6 207.2 reduce-scatter.14
where the time goes:
time: 1300 us; the launch traced here: 1290 us
  waiting for transfers between devices  680 us (52%)
  matrix products  316 us (24%)
  blocking collectives  80.4 us (6%)
  other arithmetic  79 us (6%)
  local copies, waits for them, and re-layouts  66 us (5%)
  starting transfers between devices  54.4 us (4%)
  between operations  18 us (1%)
    reduce_scatter x1, waiting for transfers between devices, on_device(): lax.psum_scatter(expert_sums[0].astype(jnp.bfloat16), 'fsdp', scatter_dim...  208 us
    reduce_scatter x1, waiting for transfers between devices, on_device(): lax.psum_scatter(expert_sums[1].astype(jnp.bfloat16), 'fsdp', scatter_dim...  118 us
    reduce_scatter x1, waiting for transfers between devices, on_device(): lax.psum_scatter(mixer_sums[0].astype(jnp.bfloat16), 'fsdp', scatter_dime...  82.8 us
    all_gather x1, waiting for transfers between devices, on_device(): lax.all_gather(w_gate_up, 'fsdp', axis=1, tiled=True)  79.2 us
    all_gather x1, waiting for transfers between devices, on_device(): lax.all_gather(w_down, 'fsdp', axis=1, tiled=True)  78.6 us
    unnamed x13, waiting for transfers between devices  43.3 us
    dot_general x2, matrix products, micro_step(): jnp.einsum('slcd,slcf->ldf', received, gate_up_grad, preferred_element_ty...  38.9 us
    unnamed x2, blocking collectives  30.1 us
  transfers between devices with their start and end apart: 19, of which 12 were waited for; matrix products, arithmetic and copies ran while one was open for 28% of the time, Pallas kernels for 0%

commit v1 on v0

v1 whole, which is shorter than its diff:
```python
import functools
import math

import jax
import jax.numpy as jnp
from jax import lax
from jax.experimental import pallas as pl
from jax.experimental.pallas import tpu as pltpu
from jax.sharding import Mesh
from jax.sharding import PartitionSpec as P

D = 768
HEADS = 12
HEAD_DIM = 64
FF = 2048
EXPERTS = 8
SEQ = 512
CAP = 128
CHOICES = EXPERTS + 4
SLOTS = EXPERTS * CAP

EPSILON = 1e-05
ROPE_BASE = 10000.0
FLOOR_SCORE = -1e30
HIGHEST = lax.Precision.HIGHEST
BF = jnp.bfloat16
F32 = jnp.float32
VMEM_MOST = 56 * 2**20


def dot(a, b):
    return jnp.dot(a, b, preferred_element_type=F32)


def dot_nt(a, b):
    return lax.dot_general(a, b, (((1,), (1,)), ((), ())), preferred_element_type=F32)


def dot_tn(a, b):
    return lax.dot_general(a, b, (((0,), (0,)), ((), ())), preferred_element_type=F32)


def pair_tables(route, capacity):
    choice_ids = jnp.arange(CHOICES, dtype=jnp.int32)
    route_hot = (route[:, :, None] == choice_ids).astype(F32)
    counts = jnp.sum(route_hot, axis=1)
    seq_index = jnp.arange(SEQ)
    before = (seq_index[:, None] > seq_index[None, :]).astype(BF)
    earlier = dot(before, counts.astype(BF))
    slot_rank = jnp.sum(earlier[:, None, :] * route_hot, axis=-1)
    cap_limit = jnp.sum(route_hot[:, :, :EXPERTS] * capacity.astype(F32), axis=-1)
    kept_pairs = (route < EXPERTS) & (slot_rank < cap_limit)
    slot_index = jnp.where(kept_pairs, route * CAP + slot_rank.astype(jnp.int32), -1)
    return slot_index, route_hot


def rope_tables(position, head_dim):
    half_dim = head_dim // 2
    frequency = jnp.exp(
        jnp.arange(half_dim, dtype=F32) * (-2.0 * math.log(ROPE_BASE) / head_dim)
    )
    angles = position.astype(F32)[:, None] * frequency[None, :]
    return (jnp.cos(angles)[:, None, :], jnp.sin(angles)[:, None, :])


def rotate(values, cosine, sine_part):
    half_dim = values.shape[-1] // 2
    first_half, second_half = (values[..., :half_dim], values[..., half_dim:])
    return jnp.concatenate(
        [
            first_half * cosine - second_half * sine_part,
            first_half * sine_part + second_half * cosine,
        ],
        axis=-1,
    )


def norm_forward(inputs, gain):
    inverse = lax.rsqrt(jnp.mean(inputs * inputs, axis=-1, keepdims=True) + EPSILON)
    return (inputs * inverse * gain, inverse)


def norm_backward(inputs, inverse, gain, grad_in):
    scaled = grad_in * gain
    gain_grad = jnp.sum(grad_in * inputs * inverse, axis=0)
    inner_mean = jnp.mean(scaled * inputs, axis=-1, keepdims=True)
    return (inverse * scaled - inputs * inverse * inverse * inverse * inner_mean, gain_grad)


def masked_scores(query_rot, key_rot, allowed):
    scores = jnp.einsum("qhd,khd->hqk", query_rot, key_rot, preferred_element_type=F32)
    return jnp.where(allowed[None], scores * (1.0 / math.sqrt(HEAD_DIM)), FLOOR_SCORE)


def forward_part(inputs_low, cot_low, prev_low, route, capacity, segment, position, mixer):
    w_qkv, w_out, gate_matrix, const_values, gain_one, gain_two = mixer
    inputs = inputs_low.astype(F32)
    normed_one, inverse_one = norm_forward(inputs, gain_one)
    act_one = normed_one.astype(BF)
    qkv = dot(act_one, w_qkv)
    cosine, sine_part = rope_tables(position, HEAD_DIM)
    query_rot = rotate(qkv[:, :D].reshape(SEQ, HEADS, HEAD_DIM), cosine, sine_part).astype(BF)
    key_rot = rotate(qkv[:, D : 2 * D].reshape(SEQ, HEADS, HEAD_DIM), cosine, sine_part).astype(BF)
    value_low = qkv[:, 2 * D :].reshape(SEQ, HEADS, HEAD_DIM).astype(BF)
    seq_index = jnp.arange(SEQ, dtype=jnp.int32)
    allowed = (seq_index[:, None] >= seq_index[None, :]) & (segment[:, None] == segment[None, :])
    scores = masked_scores(query_rot, key_rot, allowed)
    row_max = jnp.max(scores, axis=-1, keepdims=True)
    log_total = row_max + jnp.log(jnp.sum(jnp.exp(scores - row_max), axis=-1, keepdims=True))
    prob_low = jnp.exp(scores - log_total).astype(BF)
    attended = jnp.einsum("hqk,khd->qhd", prob_low, value_low, preferred_element_type=F32)
    attended_low = attended.reshape(SEQ, D).astype(BF)
    residual = inputs + dot(attended_low, w_out)
    normed_two, inverse_two = norm_forward(residual, gain_two)
    act_two = normed_two.astype(BF)
    logits_all = dot(act_two, gate_matrix)
    router = logits_all[:, :CHOICES] + prev_low.astype(F32)
    slot_index, route_hot = pair_tables(route, capacity)
    gates = jax.nn.softmax(jnp.sum(router[:, None, :] * route_hot, axis=-1), axis=1)
    const_gates = jax.nn.softmax(logits_all[:, CHOICES:].reshape(SEQ, 2, 2), axis=-1)
    slot_ids = jnp.arange(SLOTS, dtype=jnp.int32)
    pick_table = (slot_index[None, :, :] == slot_ids[:, None, None]).astype(BF)
    send_rows = dot(jnp.sum(pick_table, axis=2), act_two).astype(BF)
    grad_out = cot_low.astype(F32)
    term_grad_low = (gates[..., None] * grad_out[:, None, :]).astype(BF)
    slot_grad = jnp.einsum("esk,skd->ed", pick_table, term_grad_low, preferred_element_type=F32)
    sent = jnp.stack([send_rows, slot_grad.astype(BF)]).reshape(2, EXPERTS, CAP, D)
    kept = dict(
        inputs=inputs, inverse_one=inverse_one, act_one=act_one, cosine=cosine, sine_part=sine_part,
        query_rot=query_rot, key_rot=key_rot, value_low=value_low, allowed=allowed,
        log_total=log_total, attended_low=attended_low, residual=residual,
        normed_two=normed_two, inverse_two=inverse_two, act_two=act_two, gates=gates,
        const_gates=const_gates, pick_table=pick_table, route_hot=route_hot, grad_out=grad_out,
    )
    return sent.transpose(1, 0, 2, 3), kept


FC = 512


def expert_rows_body(x_ref, g_ref, wg_ref, wu_ref, wd_ref, hid_ref, dg_ref, du_ref, out_ref, acc, racc):
    step = pl.program_id(0)
    x = x_ref[:, 0].reshape(-1, D)
    g = g_ref[:, 0].reshape(-1, D)
    wg, wu, wd = wg_ref[...], wu_ref[...], wd_ref[...]
    gate = dot(x, wg)
    up = dot(x, wu)
    hgrad = dot_nt(g, wd).astype(BF).astype(F32)
    sig = 1.0 / (1.0 + jnp.exp(-gate))
    act = gate * sig
    hidden = (act * up).astype(BF)
    dgate = (hgrad * up * sig * (1.0 + gate * (1.0 - sig))).astype(BF)
    dup = (hgrad * act).astype(BF)
    hid_ref[...] = hidden
    dg_ref[...] = dgate
    du_ref[...] = dup
    prod = dot(hidden, wd)
    rgrad = dot_nt(dgate, wg) + dot_nt(dup, wu)

    @pl.when(step == 0)
    def _():
        acc[...] = prod
        racc[...] = rgrad

    @pl.when(step > 0)
    def _():
        acc[...] += prod
        racc[...] += rgrad

    @pl.when(step == pl.num_programs(0) - 1)
    def _():
        out_ref[:, 0] = acc[...].astype(BF).reshape(-1, CAP, D)
        out_ref[:, 1] = racc[...].astype(BF).reshape(-1, CAP, D)


def expert_rows(received, w_gate_up, w_down):
    n = received.shape[0]
    rows = n * CAP
    steps = FF // FC
    wide = jax.ShapeDtypeStruct((rows, FF), BF)
    block = pl.BlockSpec((rows, FC), lambda j: (0, j))
    return pl.pallas_call(
        expert_rows_body,
        grid=(steps,),
        in_specs=[
            pl.BlockSpec((n, 1, CAP, D), lambda j: (0, 0, 0, 0)),
            pl.BlockSpec((n, 1, CAP, D), lambda j: (0, 1, 0, 0)),
            pl.BlockSpec((D, FC), lambda j: (0, j)),
            pl.BlockSpec((D, FC), lambda j: (0, steps + j)),
            pl.BlockSpec((FC, D), lambda j: (j, 0)),
        ],
        out_specs=[block, block, block, pl.BlockSpec((n, 2, CAP, D), lambda j: (0, 0, 0, 0))],
        out_shape=[wide, wide, wide, jax.ShapeDtypeStruct((n, 2, CAP, D), BF)],
        scratch_shapes=[pltpu.VMEM((rows, D), F32), pltpu.VMEM((rows, D), F32)],
        compiler_params=pltpu.CompilerParams(
            dimension_semantics=("arbitrary",), vmem_limit_bytes=VMEM_MOST
        ),
        cost_estimate=pl.CostEstimate(
            flops=12 * rows * D * FF, bytes_accessed=18 * D * FF // 3 + 6 * rows * FF, transcendentals=rows * FF
        ),
    )(received, received, w_gate_up, w_gate_up, w_down)


FW = 512


def expert_wgrad_body(parts, *refs):
    received = refs[:parts]
    hid, dg, du = refs[parts : 2 * parts], refs[2 * parts : 3 * parts], refs[3 * parts : 4 * parts]
    dgate_ref, dup_ref, down_ref, xt, gb = refs[4 * parts :]
    rows = received[0].shape[0] * CAP

    @pl.when(pl.program_id(0) == 0)
    def _():
        for i in range(parts):
            xt[:, i * rows : (i + 1) * rows] = received[i][:, 0].reshape(rows, D).T
            gb[i * rows : (i + 1) * rows, :] = received[i][:, 1].reshape(rows, D)

    def joined(vs):
        return jnp.concatenate([v[...] for v in vs], axis=0)

    dgate_ref[...] = dot(xt[...], joined(dg)).astype(BF)
    dup_ref[...] = dot(xt[...], joined(du)).astype(BF)
    down_ref[...] = dot_tn(joined(hid), gb[...]).astype(BF)


def expert_wgrad(received, hid, dg, du):
    parts = len(received)
    n = received[0].shape[0]
    rows = n * CAP
    whole = pl.BlockSpec((n, 2, CAP, D), lambda j: (0, 0, 0, 0))
    block = pl.BlockSpec((rows, FW), lambda j: (0, j))
    half = jax.ShapeDtypeStruct((D, FF), BF)
    return pl.pallas_call(
        functools.partial(expert_wgrad_body, parts),
        grid=(FF // FW,),
        in_specs=[whole] * parts + [block] * (3 * parts),
        out_specs=[
            pl.BlockSpec((D, FW), lambda j: (0, j)),
            pl.BlockSpec((D, FW), lambda j: (0, j)),
            pl.BlockSpec((FW, D), lambda j: (j, 0)),
        ],
        out_shape=[half, half, jax.ShapeDtypeStruct((FF, D), BF)],
        scratch_shapes=[pltpu.VMEM((D, parts * rows), BF), pltpu.VMEM((parts * rows, D), BF)],
        compiler_params=pltpu.CompilerParams(
            dimension_semantics=("arbitrary",), vmem_limit_bytes=VMEM_MOST
        ),
        cost_estimate=pl.CostEstimate(
            flops=6 * parts * rows * D * FF, bytes_accessed=6 * parts * rows * FF + 6 * D * FF, transcendentals=0
        ),
    )(*received, *hid, *dg, *du)


def expert_part(received, w_gate_up, w_down):
    made = [expert_rows(r, w_gate_up, w_down) for r in received]
    grads = expert_wgrad(received, *[[m[i] for m in made] for i in range(3)])
    return [m[3] for m in made], grads


def backward_part(returned, kept, mixer):
    w_qkv, w_out, gate_matrix, const_values, gain_one, gain_two = mixer
    k = kept
    gates, grad_out, const_gates, normed_two = k["gates"], k["grad_out"], k["const_gates"], k["normed_two"]
    route_hot, pick_table = k["route_hot"], k["pick_table"]
    copy_mask = route_hot[:, :, EXPERTS + 1]
    const_mask = route_hot[:, :, EXPERTS + 2 :]
    const_vec = const_values.astype(F32)
    produced = returned[:, 0].reshape(SLOTS, D)
    back_rows = returned[:, 1].reshape(SLOTS, D)
    combined = jnp.einsum("esk,ed->skd", pick_table, produced, preferred_element_type=F32)
    const_out = (
        const_gates[..., 0:1] * normed_two[:, None, :]
        + const_gates[..., 1:2] * const_vec.T[None, :, :]
    )
    term = combined + copy_mask[..., None] * normed_two[:, None, :]
    term = (
        term
        + const_mask[:, :, 0, None] * const_out[:, None, 0, :]
        + const_mask[:, :, 1, None] * const_out[:, None, 1, :]
    )
    output = k["residual"] + jnp.sum(gates[..., None] * term, axis=1)
    gate_grad = jnp.sum(grad_out[:, None, :] * term, axis=-1)
    term_grad = gates[..., None] * grad_out[:, None, :]
    dispatch_grad = jnp.einsum(
        "es,ed->sd", jnp.sum(pick_table, axis=2), back_rows, preferred_element_type=F32
    )
    direct_weight = (
        copy_mask
        + const_mask[:, :, 0] * const_gates[:, None, 0, 0]
        + const_mask[:, :, 1] * const_gates[:, None, 1, 0]
    )
    direct_grad = jnp.sum(direct_weight[..., None] * term_grad, axis=1)
    along_normed = jnp.sum(term_grad * normed_two[:, None, :], axis=-1)
    along_vector = jnp.einsum("skd,dc->skc", term_grad, const_vec, precision=HIGHEST)
    in_normed = jnp.sum(const_mask * along_normed[..., None], axis=1)
    in_vector = jnp.sum(const_mask * along_vector, axis=1)
    const_in_grad = jnp.stack([in_normed, in_vector], axis=-1)
    const_logit_grad = const_gates * (
        const_in_grad - jnp.sum(const_gates * const_in_grad, axis=-1, keepdims=True)
    )
    vector_wgrad = jnp.einsum(
        "skc,skd->dc", const_mask * const_gates[:, None, :, 1], term_grad, precision=HIGHEST
    )
    picked_grad = gates * (gate_grad - jnp.sum(gates * gate_grad, axis=1, keepdims=True))
    router_grad = jnp.sum(picked_grad[..., None] * route_hot, axis=1)
    logit_grad = jnp.concatenate([router_grad, const_logit_grad.reshape(SEQ, 4)], axis=1).astype(BF)
    gate_wgrad = dot(k["act_two"].T, logit_grad)
    router_back = dot(logit_grad, gate_matrix.T)
    normed_grad = router_back + dispatch_grad + direct_grad
    residual_norm_grad, gain_two_grad = norm_backward(
        k["residual"], k["inverse_two"], gain_two, normed_grad
    )
    residual_grad = grad_out + residual_norm_grad
    out_grad_low = residual_grad.astype(BF)
    out_wgrad = dot(k["attended_low"].T, out_grad_low)
    attended_grad = dot(out_grad_low, w_out.T).astype(BF).reshape(SEQ, HEADS, HEAD_DIM)
    prob_full = jnp.exp(masked_scores(k["query_rot"], k["key_rot"], k["allowed"]) - k["log_total"])
    prob_grad = jnp.einsum("qhd,khd->hqk", attended_grad, k["value_low"], preferred_element_type=F32)
    row_inner = jnp.sum(prob_full * prob_grad, axis=-1, keepdims=True)
    score_grad = (prob_full * (prob_grad - row_inner)).astype(BF)
    scale = 1.0 / math.sqrt(HEAD_DIM)
    query_grad = jnp.einsum("hqk,khd->qhd", score_grad, k["key_rot"], preferred_element_type=F32) * scale
    key_grad = jnp.einsum("hqk,qhd->khd", score_grad, k["query_rot"], preferred_element_type=F32) * scale
    value_grad = jnp.einsum("hqk,qhd->khd", prob_full.astype(BF), attended_grad, preferred_element_type=F32)
    qkv_grad = jnp.concatenate(
        [
            rotate(query_grad, k["cosine"], -k["sine_part"]).reshape(SEQ, D),
            rotate(key_grad, k["cosine"], -k["sine_part"]).reshape(SEQ, D),
            value_grad.reshape(SEQ, D),
        ],
        axis=1,
    ).astype(BF)
    qkv_wgrad = dot(k["act_one"].T, qkv_grad)
    act_one_grad = dot(qkv_grad, w_qkv.T)
    input_norm_grad, gain_one_grad = norm_backward(k["inputs"], k["inverse_one"], gain_one, act_one_grad)
    input_grad = residual_grad + input_norm_grad
    grads = (qkv_wgrad, out_wgrad, gate_wgrad, vector_wgrad, gain_one_grad, gain_two_grad)
    return output.astype(BF), input_grad, router_grad, grads


class Paired:
    axes = ("half", "low", "inner", "side", "core")
    fsdp = ("half", "low", "inner")
    expert = ("side", "core")
    rows = ("side", "low", "inner")
    route_axes = ("half", "low", "inner", "core")

    def __init__(self, mesh):
        self.mesh = Mesh(mesh.devices.reshape(2, 2, 2, 2, 2), self.axes)
        self.routes = []
        for turn in range(4):
            pairs = []
            for z in range(4):
                for y in range(2):
                    for c in range(2):
                        half, inner = (z ^ turn) >> 1, (z ^ turn) & 1
                        pairs.append(((z * 2 + y) * 2 + c, ((half * 2 + c) * 2 + inner) * 2 + y))
            self.routes.append(pairs)

    @staticmethod
    def swap(value):
        return lax.ppermute(value, "core", [(0, 1), (1, 0)])

    @staticmethod
    def place():
        z = lax.axis_index("half") * 2 + lax.axis_index("low")
        here = lax.axis_index("half") * 2 + lax.axis_index("inner")
        return z, here, lax.axis_index("core")

    def gather(self, weight):
        z, here, core = self.place()
        own = []
        for turn in range(4):
            mine = lax.dynamic_index_in_dim(weight, (z ^ turn) & 1, 0, False)
            own.append(lax.ppermute(mine, self.route_axes, self.routes[turn]))
        other = [self.swap(v) for v in own]
        stack = jnp.stack(own + other)
        blocks = []
        for zz in range(4):
            for y in range(2):
                blocks.append(lax.dynamic_index_in_dim(stack, (y ^ core) * 4 + (zz ^ here), 0, False))
        return jnp.concatenate(blocks)

    def scatter(self, grad):
        z, here, core = self.place()
        grad = grad.reshape((4, 2, grad.shape[0] // 8) + grad.shape[1:])
        got = []
        for turn in range(4):
            part = lax.dynamic_index_in_dim(grad, here ^ turn, 0, False)
            keep = lax.dynamic_index_in_dim(part, core, 0, False)
            give = lax.dynamic_index_in_dim(part, 1 - core, 0, False)
            total = (keep.astype(F32) + self.swap(give).astype(F32)).astype(BF)
            back = [(b, a) for a, b in self.routes[turn]]
            got.append(lax.ppermute(total, self.route_axes, back).astype(F32))
        even = (z & 1) == 0
        first = jnp.where(even, got[0] + got[2], got[1] + got[3])
        second = jnp.where(even, got[1] + got[3], got[0] + got[2])
        return jnp.stack([first, second])


class Plain:
    axes = ("outer", "inner", "expert")
    fsdp = ("outer", "inner")
    expert = ("expert",)
    rows = ("expert", "inner")

    def __init__(self, mesh):
        fsdp, expert = mesh.shape["fsdp"], mesh.shape["expert"]
        inner = EXPERTS // expert
        self.mesh = Mesh(mesh.devices.reshape(fsdp // inner, inner, expert), self.axes)

    def gather(self, weight):
        own = lax.all_to_all(weight, "inner", 0, 0, tiled=True)
        full = lax.all_gather(own, "outer", axis=0, tiled=True)
        return full.reshape((-1,) + weight.shape[2:])

    def scatter(self, grad):
        inner = lax.axis_size("inner")
        part = lax.psum_scatter(grad, "outer", scatter_dimension=0, tiled=True)
        part = part.reshape((inner, part.shape[0] // inner) + part.shape[1:])
        return lax.all_to_all(part, "inner", 0, 0, tiled=True).astype(F32)


def solution(mesh):
    plan = Paired(mesh) if (mesh.shape["fsdp"], mesh.shape["expert"]) == (8, 4) else Plain(mesh)

    def on_device(
        tokens, cotangent, prev_logits, routes, capacity, segments, positions,
        w_qkv, w_out, gate_matrix, const_values, attn_gain, moe_gain, w_gate_up, w_down,
    ):
        rows = w_qkv.shape[0]
        pad = jnp.zeros((rows, 128 - 20), BF)
        small = jnp.concatenate(
            [gate_matrix, const_values, attn_gain[:, None], moe_gain[:, None], pad], axis=1
        )
        packed = lax.all_gather(
            jnp.concatenate([w_qkv, w_out, small], axis=1), plan.fsdp, axis=0, tiled=True
        )
        mixer = (
            packed[:, : 3 * D],
            packed[:, 3 * D : 4 * D],
            packed[:, 4 * D : 4 * D + 16],
            packed[:, 4 * D + 16 : 4 * D + 18],
            packed[:, 4 * D + 18].astype(F32),
            packed[:, 4 * D + 19].astype(F32),
        )
        gate_up_full = plan.gather(w_gate_up)
        down_full = plan.gather(w_down)
        parts = tokens.shape[0] // SEQ
        received, keeps = [], []
        for part in range(parts):
            span = slice(part * SEQ, (part + 1) * SEQ)
            sent, kept = forward_part(
                tokens[span], cotangent[span], prev_logits[span], routes[span], capacity,
                segments[span], positions[span], mixer,
            )
            received.append(lax.all_to_all(sent, plan.rows, 0, 0, tiled=True))
            keeps.append(kept)
        back, (gate_wgrad, up_wgrad, down_wgrad) = expert_part(received, gate_up_full, down_full)
        gate_up_total = jnp.concatenate([plan.scatter(gate_wgrad), plan.scatter(up_wgrad)], axis=2)
        down_total = plan.scatter(down_wgrad)
        outs, sums = [], None
        for part in range(parts):
            returned = lax.all_to_all(back[part], plan.rows, 0, 0, tiled=True)
            result = backward_part(returned, keeps[part], mixer)
            outs.append(result[:3])
            sums = result[3] if sums is None else jax.tree.map(jnp.add, sums, result[3])
        small_sum = jnp.concatenate(
            [sums[2], sums[3], sums[4][:, None], sums[5][:, None], jnp.zeros((D, 128 - 20), F32)], axis=1
        )
        total = jnp.concatenate([sums[0], sums[1], small_sum], axis=1).astype(BF)
        total = lax.psum_scatter(total, plan.axes, scatter_dimension=0, tiled=True)
        total = lax.all_gather(total, plan.expert, axis=0, tiled=True).astype(F32)
        return (
            jnp.concatenate([o[0] for o in outs]),
            jnp.concatenate([o[1] for o in outs]),
            jnp.concatenate([o[2] for o in outs]),
            total[:, : 3 * D],
            total[:, 3 * D : 4 * D],
            total[:, 4 * D : 4 * D + 16],
            total[:, 4 * D + 16 : 4 * D + 18],
            total[:, 4 * D + 18],
            total[:, 4 * D + 19],
            gate_up_total,
            down_total,
        )

    every = plan.fsdp + plan.expert
    split = P(every, None)
    shard = P(plan.fsdp, None)
    line = P(plan.fsdp)
    whole = P(plan.expert, plan.fsdp, None)
    return jax.shard_map(
        on_device,
        mesh=plan.mesh,
        in_specs=(
            split, split, split, split, P(), P(every), P(every),
            shard, shard, shard, shard, line, line, whole, whole,
        ),
        out_specs=(split, split, split, shard, shard, shard, shard, line, line, whole, whole),
        check_vma=False,
    )
```

time: 1300 us -> 833 us (0.64)
  waiting for transfers between devices: 680 us -> 164 us
  matrix products: 316 us -> 162 us
  starting transfers between devices: 54.4 us -> 169 us
  Pallas kernels: 0 us -> 84.8 us
  local copies, waits for them, and re-layouts: 66 us -> 142 us
  blocking collectives: 80.4 us -> 23.6 us
  other arithmetic: 79 us -> 63.9 us
    reduce_scatter x4 -> x0, waiting for transfers between devices: 424 us -> none  [the longest x1 208 us: on_device(): lax.psum_scatter(expert_sums[0].astype(jnp.bfloat16), 'fsdp', scatter_dim...]
    all_gather x4 -> x1, waiting for transfers between devices: 158 us -> 0.45 us  [on_device(): lax.all_gather(jnp.concatenate([w_qkv, w_out, small], axis=1), plan.fsdp,...]
    dot_general x54 -> x44, matrix products: 316 us -> 162 us  [the longest x22 54.8 us: dot(): return jnp.dot(a, b, preferred_element_type=F32)]
    ppermute x0 -> x40, starting transfers between devices: none -> 126 us  [the longest x12 71.3 us: scatter(): got.append(lax.ppermute(total, self.route_axes, back).astype(F32))]
    ppermute x0 -> x40, waiting for transfers between devices: none -> 126 us  [the longest x8 83.4 us: gather(): own.append(lax.ppermute(mine, self.route_axes, self.routes[turn]))]
    pallas_call x0 -> x3, Pallas kernels: none -> 84.8 us  [the longest x2 57.1 us: expert_rows(): pl.pallas_call(expert_rows_body, grid=(steps,), in_specs=[pl.BlockSpec((n...]
    unnamed x322 -> x403, local copies, waits for them, and re-layouts: 21.9 us -> 66.4 us
    unnamed x13 -> x3, waiting for transfers between devices: 43.3 us -> 0.03 us
  transfers between devices with their start and end apart: 19 -> 46, of which waited for: 12 -> 11; matrix products, arithmetic and copies ran while one was open for 28% -> 26% of each run, Pallas kernels for 0% -> 10%
where the time goes in v1:
time: 833 us; the launch traced here: 826 us
  starting transfers between devices  169 us (20%)
  waiting for transfers between devices  164 us (20%)
  matrix products  162 us (19%)
  local copies, waits for them, and re-layouts  142 us (17%)
  Pallas kernels  84.8 us (10%)
  other arithmetic  63.9 us (8%)
  blocking collectives  23.6 us (3%)
  between operations  17.1 us (2%)
    ppermute x8, waiting for transfers between devices, gather(): own.append(lax.ppermute(mine, self.route_axes, self.routes[turn]))  83.4 us
    ppermute x12, starting transfers between devices, scatter(): got.append(lax.ppermute(total, self.route_axes, back).astype(F32))  71.3 us
    unnamed x403, local copies, waits for them, and re-layouts  66.4 us
    pallas_call x2, Pallas kernels, expert_rows(): pl.pallas_call(expert_rows_body, grid=(steps,), in_specs=[pl.BlockSpec((n...  57.1 us
    dot_general x22, matrix products, dot(): return jnp.dot(a, b, preferred_element_type=F32)  54.8 us
    ppermute x12, waiting for transfers between devices, scatter(): got.append(lax.ppermute(total, self.route_axes, back).astype(F32))  41.6 us
    ppermute x8, starting transfers between devices, gather(): own.append(lax.ppermute(mine, self.route_axes, self.routes[turn]))  37.1 us
    all_to_all x2, starting transfers between devices, on_device(): received.append(lax.all_to_all(sent, plan.rows, 0, 0, tiled=True))  32.5 us
  transfers between devices with their start and end apart: 46, of which 11 were waited for; matrix products, arithmetic and copies ran while one was open for 26% of the time, Pallas kernels for 10%

profile of v1, /device:TPU:1, one launch (start us, length us, event | category | flops | bytes accessed | tf_op | source)
XLA Modules:
  0.0 825.8 jit_solution(9113202955532550080)
XLA Ops:
  46.1 11.3 %collective-permute-done.10 = bf16[256,768]{1,0:T(8,128)(2,1)} collective-permute-done((bf16[256,768]{1,0:T(8,128)(2,1)}, bf16[256,768]{1,0:T(8,128)(2,1)}, u32[]{:S(2)}, u32[]{:S(2)}) %collective-permute-start.10) | collective-permute-done | bytes 393248 | tf_op jit(solution)/shard_map/ppermute | solution.py:375
  57.4 10.9 %collective-permute-start.1 = (bf16[96,4096]{1,0:T(8,128)(2,1)S(1)}, bf16[96,4096]{1,0:T(8,128)(2,1)}, u32[]{:S(2)}, u32[]{:S(2)}) collective-permute-start(bf16[96,4096]{1,0:T(8,128)(2,1)S(1)} %copy-done.76), channel_id=1, source_target_pairs={{0,4},{1,12},{4,5},{5,13},{8,0},{9,8},{12,1},{13,9},{16,20},{17,28... | collective-permute-start | bytes 2359304 | tf_op jit(solution)/shard_map/ppermute | solution.py:375
  68.2 11.5 %collective-permute-start.2 = (bf16[96,4096]{1,0:T(8,128)(2,1)S(1)}, bf16[96,4096]{1,0:T(8,128)(2,1)}, u32[]{:S(2)}, u32[]{:S(2)}) collective-permute-start(bf16[96,4096]{1,0:T(8,128)(2,1)S(1)} %copy-done.75), channel_id=1, source_target_pairs={{0,16},{1,24},{4,17},{5,25},{8,20},{9,28},{12,21},{13,29},{16,0},{... | collective-permute-start | bytes 2359304 | tf_op jit(solution)/shard_map/ppermute | solution.py:375
  85.0 12.6 %collective-permute-done.1 = bf16[96,4096]{1,0:T(8,128)(2,1)} collective-permute-done((bf16[96,4096]{1,0:T(8,128)(2,1)S(1)}, bf16[96,4096]{1,0:T(8,128)(2,1)}, u32[]{:S(2)}, u32[]{:S(2)}) %collective-permute-start.1) | collective-permute-done | bytes 786464 | tf_op jit(solution)/shard_map/ppermute | solution.py:375
  101.5 59.5 %collective-permute-done.2 = bf16[96,4096]{1,0:T(8,128)(2,1)} collective-permute-done((bf16[96,4096]{1,0:T(8,128)(2,1)S(1)}, bf16[96,4096]{1,0:T(8,128)(2,1)}, u32[]{:S(2)}, u32[]{:S(2)}) %collective-permute-start.2) | collective-permute-done | bytes 786464 | tf_op jit(solution)/shard_map/ppermute | solution.py:375
  203.6 8.5 %convolution_convert_fusion.6 = bf16[12,64,512]{2,1,0:T(8,128)(2,1)S(1)} fusion(bf16[512,12,64]{0,2,1:T(8,128)(2,1)} %bitcast.327, f32[12,512,512]{1,2,0:T(8,128)} %copy-done, f32[12,512]{1,0:T(8,128)S(1)} %log_add_fusion, pred[512,512]{0,1:T(8,128)(4,1)S(1)} %get-tuple-element.257), kind=kOutput, calls=%fused_computation.149 | convolution fusion | flops 415629312 | bytes 14442496 | tf_op jit(solution)/shard_map/hqk,khd->qhd/dot_general | solution.py:111
  228.0 8.2 convolution_convert_fusion.7
  252.4 27.8 %all-to-all-start = ((bf16[8,2,128,768]{3,2,1,0:T(8,128)(2,1)}), bf16[8,2,128,768]{3,2,1,0:T(8,128)(2,1)}, u32[]{:S(2)}, u32[]{:S(2)}) async-start(bf16[8,2,128,768]{3,2,1,0:T(8,128)(2,1)} %maximum_bitcast_fusion), calls=%async_computation | async-start | bytes 6291456 | tf_op jit(solution)/shard_map/all_to_all | solution.py:457
  300.1 24.4 %all-to-all-done.x_ref.g_ref.refs_0_ = bf16[8,2,128,768]{3,2,1,0:T(8,128)(2,1)} async-done(((bf16[8,2,128,768]{3,2,1,0:T(8,128)(2,1)}), bf16[8,2,128,768]{3,2,1,0:T(8,128)(2,1)}, u32[]{:S(2)}, u32[]{:S(2)}) %all-to-all-start) | async-done | bytes 3145760 | tf_op jit(solution)/shard_map/all_to_all | solution.py:457
  345.7 28.6 %shard_map.230 = (bf16[1024,2048]{1,0:T(8,128)(2,1)}, bf16[1024,2048]{1,0:T(8,128)(2,1)}, bf16[1024,2048]{1,0:T(8,128)(2,1)}, bf16[8,2,128,768]{3,2,1,0:T(8,128)(2,1)}) custom-call(bf16[8,2,128,768]{3,2,1,0:T(8,128)(2,1)} %all-to-all-done.x_ref.g_ref.refs_0_, bf16[8,2,128,768]{3,2,1,0:T(8,128)(2,1)} %all-to-all-done.x_ref.g_ref.refs_0_, ...), custom_call_target="tpu_custom_call" | custom-call | flops 19327352832 | bytes 22020096 | tf_op jit(solution)/shard_map/pallas_call | solution.py:182
  380.1 28.6 %shard_map.231 = (bf16[1024,2048]{1,0:T(8,128)(2,1)}, bf16[1024,2048]{1,0:T(8,128)(2,1)}, bf16[1024,2048]{1,0:T(8,128)(2,1)}, bf16[8,2,128,768]{3,2,1,0:T(8,128)(2,1)}) custom-call(bf16[8,2,128,768]{3,2,1,0:T(8,128)(2,1)} %all-to-all-done.2.x_ref.g_ref.refs_1_, bf16[8,2,128,768]{3,2,1,0:T(8,128)(2,1)} %all-to-all-done.2.x_ref.g_ref.refs_1_, ...), custom_call_target="tpu_custom_call" | custom-call | flops 19327352832 | bytes 22020096 | tf_op jit(solution)/shard_map/pallas_call | solution.py:182
  408.7 13.0 %all-to-all-done.1 = bf16[8,2,128,768]{3,2,1,0:T(8,128)(2,1)} async-done(((bf16[8,2,128,768]{3,2,1,0:T(8,128)(2,1)}), bf16[8,2,128,768]{3,2,1,0:T(8,128)(2,1)}, u32[]{:S(2)}, u32[]{:S(2)}) %all-to-all-start.1) | async-done | bytes 3145760 | tf_op jit(solution)/shard_map/all_to_all | solution.py:464
  520.5 13.6 %multiply_reduce_fusion.1 = (f32[12,512]{1,0:T(8,128)S(1)}, f32[12,512,512]{1,2,0:T(8,128)}) fusion(f32[12,512,512]{1,2,0:T(8,128)} %copy-done.1, f32[12,512]{1,0:T(8,128)S(1)} %copy-done.93, pred[512,512]{0,1:T(8,128)(4,1)S(1)} %copy-done.28, bf16[512,12,64]{0,2,1:T(8,128)(2,1)} %bitcast.331, bf16[512,12,64]{0,2,1:T(8,128)(2,1)} %bitcast.330), kind=kOutput, calls=%fused_computation.4 | convolution fusion | flops 418375680 | bytes 27049984 | tf_op jit(solution)/shard_map/qhd,khd->hqk/dot_general | solution.py:318
  534.1 7.1 multiply_convert_fusion.1
  556.1 13.7 %multiply_reduce_fusion = (f32[12,512]{1,0:T(8,128)S(1)}, f32[12,512,512]{1,2,0:T(8,128)}) fusion(f32[12,512,512]{1,2,0:T(8,128)} %copy-done, f32[12,512]{1,0:T(8,128)S(1)} %copy-done.91, pred[512,512]{0,1:T(8,128)(4,1)S(1)} %copy-done.27, bf16[512,12,64]{0,2,1:T(8,128)(2,1)} %bitcast.333, bf16[512,12,64]{0,2,1:T(8,128)(2,1)} %bitcast.328), kind=kOutput, calls=%fused_computation.2 | convolution fusion | flops 418375680 | bytes 27049984 | tf_op jit(solution)/shard_map/qhd,khd->hqk/dot_general | solution.py:318
  609.5 8.5 %add_convert_fusion = bf16[768,2304]{1,0:T(8,128)(2,1)} fusion(f32[768,2304]{1,0:T(8,128)} %fusion.101, bf16[512,768]{0,1:T(8,128)(2,1)S(1)} %bitcast.390, bf16[512,768]{0,1:T(8,128)(2,1)S(1)} %bitcast.356, bf16[512,768]{0,1:T(8,128)(2,1)S(1)} %bitcast.352, f32[512]{0:T(512)S(1)} %copy-done.150, f32[768]{0:T(1024)S(1)} %copy-done.144, ...), kind=kOutput, calls=%fused_computation.27 | convolution fusion | flops 1824129024 | bytes 13768704 | tf_op jit(solution)/shard_map/dot_general | solution.py:32
  618.7 8.5 %concatenate.93 = bf16[768,3200]{1,0:T(8,128)(2,1)} concatenate(bf16[768,2304]{1,0:T(8,128)(2,1)} %add_convert_fusion, bf16[768,768]{1,0:T(8,128)(2,1)} %add_convert_fusion.1, bf16[768,16]{1,0:T(8,128)(2,1)} %copy.201, bf16[768,2]{1,0:T(8,128)(2,1)S(1)} %copy-done.77, bf16[768,1]{1,0:T(8,128)(2,1)} %add.602, bf16[768,1]{1,0:T(8,128)(2,1)S(1)} %add.603, ...), dimensions={1} | concatenate | bytes 9830400 | tf_op jit(solution)/shard_map/concatenate | solution.py:471
  627.3 27.7 %shard_map.232 = (bf16[768,2048]{1,0:T(8,128)(2,1)}, bf16[768,2048]{1,0:T(8,128)(2,1)}, bf16[2048,768]{1,0:T(8,128)(2,1)}) custom-call(bf16[8,2,128,768]{3,2,1,0:T(8,128)(2,1)} %all-to-all-done.x_ref.g_ref.refs_0_, bf16[8,2,128,768]{3,2,1,0:T(8,128)(2,1)} %all-to-all-done.2.x_ref.g_ref.refs_1_, bf16[1024,2048]{1,0:T(8,128)(2,1)} %get-tuple-element.24.refs_2_, ...), custom_call_target="tpu_custom_call" | custom-call | flops 19327352832 | bytes 34603008 | tf_op jit(solution)/shard_map/pallas_call | solution.py:234
  679.9 22.4 %collective-permute-done.33 = bf16[256,768]{1,0:T(8,128)(2,1)S(1)} collective-permute-done((bf16[256,768]{1,0:T(8,128)(2,1)S(1)}, bf16[256,768]{1,0:T(8,128)(2,1)S(1)}, u32[]{:S(2)}, u32[]{:S(2)}) %collective-permute-start.33) | collective-permute-done | bytes 393248 | tf_op jit(solution)/shard_map/ppermute | solution.py:394
  704.7 8.1 collective-permute-start.21
  713.6 21.5 %collective-permute-start.25 = (bf16[96,2048]{1,0:T(8,128)(2,1)S(1)}, bf16[96,2048]{1,0:T(8,128)(2,1)S(1)}, u32[]{:S(2)}, u32[]{:S(2)}) collective-permute-start(bf16[96,2048]{1,0:T(8,128)(2,1)S(1)} %get-tuple-element.141), channel_id=1, source_target_pairs={{0,0},{8,1},{1,4},{9,5},{4,8},{12,9},{5,12},{13,13},{16,16},{24,17... | collective-permute-start | bytes 1179656 | tf_op jit(solution)/shard_map/ppermute | solution.py:394
  736.6 25.8 %collective-permute-start.29 = (bf16[96,2048]{1,0:T(8,128)(2,1)S(1)}, bf16[96,2048]{1,0:T(8,128)(2,1)S(1)}, u32[]{:S(2)}, u32[]{:S(2)}) collective-permute-start(bf16[96,2048]{1,0:T(8,128)(2,1)S(1)} %get-tuple-element.138), channel_id=1, source_target_pairs={{4,0},{12,1},{5,4},{13,5},{0,8},{8,9},{1,12},{9,13},{20,16},{28,17... | collective-permute-start | bytes 1179656 | tf_op jit(solution)/shard_map/ppermute | solution.py:394
  768.6 14.6 %collective-permute-done.29 = bf16[96,2048]{1,0:T(8,128)(2,1)S(1)} collective-permute-done((bf16[96,2048]{1,0:T(8,128)(2,1)S(1)}, bf16[96,2048]{1,0:T(8,128)(2,1)S(1)}, u32[]{:S(2)}, u32[]{:S(2)}) %collective-permute-start.29) | collective-permute-done | bytes 393248 | tf_op jit(solution)/shard_map/ppermute | solution.py:394
  791.2 23.6 %all_gather.7 = bf16[96,3200]{1,0:T(8,128)(2,1)S(1)} all-gather(bf16[24,3200]{1,0:T(8,128)(2,1)} %reduce-scatter.4.cloned.1.call-done), channel_id=1, replica_groups=mesh['half'=2,'low'=2,'inner'=2,'side'=2,'core'=2] {'side','core'}, dimensions={0}, use_global_device_ids=true | all-gather | bytes 768000 | tf_op jit(solution)/shard_map/all_gather | solution.py:473
  (676 shorter events, 369.1 us)
Async XLA Ops:
  7.2 166.9 %all-gather.2.cloned.1.call-start = ((), (), s32[]{:S(2)}) async-start(), calls=%async_computation.5 | async-start | bytes 5529600 | tf_op jit(solution)/shard_map/all_gather | solution.py:436
  23.4 44.9 %collective-permute-start.11 = (bf16[256,768]{1,0:T(8,128)(2,1)}, bf16[256,768]{1,0:T(8,128)(2,1)}, u32[]{:S(2)}, u32[]{:S(2)}) collective-permute-start(bf16[256,768]{1,0:T(8,128)(2,1)} %get-tuple-element.188), channel_id=1, source_target_pairs={{0,20},{1,28},{4,21},{5,29},{8,16},{9,24},{12,17},{13,25},{16,4},{... | collective-permute-start | bytes 1179656 | tf_op jit(solution)/shard_map/ppermute | solution.py:375
  26.6 57.9 %collective-permute-start = (bf16[96,4096]{1,0:T(8,128)(2,1)}, bf16[96,4096]{1,0:T(8,128)(2,1)}, u32[]{:S(2)}, u32[]{:S(2)}) collective-permute-start(bf16[96,4096]{1,0:T(8,128)(2,1)} %get-tuple-element.186), channel_id=1, source_target_pairs={{0,0},{1,8},{4,1},{5,9},{8,4},{9,12},{12,5},{13,13},{16,16},{17,24... | collective-permute-start | bytes 2359304 | tf_op jit(solution)/shard_map/ppermute | solution.py:375
  37.6 42.1 %collective-permute-start.12 = (bf16[256,768]{1,0:T(8,128)(2,1)}, bf16[256,768]{1,0:T(8,128)(2,1)S(1)}, u32[]{:S(2)}, u32[]{:S(2)}) collective-permute-start(bf16[256,768]{1,0:T(8,128)(2,1)} %collective-permute-done.8), channel_id=1, source_target_pairs={{0,1},{1,0},{2,3},{3,2},{4,5},{5,4},{6,7},{7,6},{8,9},{9,8},{10,11... | collective-permute-start | bytes 1179656 | tf_op jit(solution)/shard_map/ppermute | solution.py:362
  41.6 40.8 %collective-permute-start.13 = (bf16[256,768]{1,0:T(8,128)(2,1)}, bf16[256,768]{1,0:T(8,128)(2,1)S(1)}, u32[]{:S(2)}, u32[]{:S(2)}) collective-permute-start(bf16[256,768]{1,0:T(8,128)(2,1)} %collective-permute-done.9), channel_id=1, source_target_pairs={{0,1},{1,0},{2,3},{3,2},{4,5},{5,4},{6,7},{7,6},{8,9},{9,8},{10,11... | collective-permute-start | bytes 1179656 | tf_op jit(solution)/shard_map/ppermute | solution.py:362
  57.4 40.2 %collective-permute-start.1 = (bf16[96,4096]{1,0:T(8,128)(2,1)S(1)}, bf16[96,4096]{1,0:T(8,128)(2,1)}, u32[]{:S(2)}, u32[]{:S(2)}) collective-permute-start(bf16[96,4096]{1,0:T(8,128)(2,1)S(1)} %copy-done.76), channel_id=1, source_target_pairs={{0,4},{1,12},{4,5},{5,13},{8,0},{9,8},{12,1},{13,9},{16,20},{17,28... | collective-permute-start | bytes 2359304 | tf_op jit(solution)/shard_map/ppermute | solution.py:375
  68.2 92.8 %collective-permute-start.2 = (bf16[96,4096]{1,0:T(8,128)(2,1)S(1)}, bf16[96,4096]{1,0:T(8,128)(2,1)}, u32[]{:S(2)}, u32[]{:S(2)}) collective-permute-start(bf16[96,4096]{1,0:T(8,128)(2,1)S(1)} %copy-done.75), channel_id=1, source_target_pairs={{0,16},{1,24},{4,17},{5,25},{8,20},{9,28},{12,21},{13,29},{16,0},{... | collective-permute-start | bytes 2359304 | tf_op jit(solution)/shard_map/ppermute | solution.py:375
  79.7 82.2 %collective-permute-start.3 = (bf16[96,4096]{1,0:T(8,128)(2,1)S(1)}, bf16[96,4096]{1,0:T(8,128)(2,1)}, u32[]{:S(2)}, u32[]{:S(2)}) collective-permute-start(bf16[96,4096]{1,0:T(8,128)(2,1)S(1)} %copy-done.74), channel_id=1, source_target_pairs={{0,20},{1,28},{4,21},{5,29},{8,16},{9,24},{12,17},{13,25},{16,4},{... | collective-permute-start | bytes 2359304 | tf_op jit(solution)/shard_map/ppermute | solution.py:375
  84.4 77.6 %collective-permute-start.15 = (bf16[256,768]{1,0:T(8,128)(2,1)}, bf16[256,768]{1,0:T(8,128)(2,1)S(1)}, u32[]{:S(2)}, u32[]{:S(2)}) collective-permute-start(bf16[256,768]{1,0:T(8,128)(2,1)} %collective-permute-done.11), channel_id=1, source_target_pairs={{0,1},{1,0},{2,3},{3,2},{4,5},{5,4},{6,7},{7,6},{8,9},{9,8},{10,11... | collective-permute-start | bytes 1179656 | tf_op jit(solution)/shard_map/ppermute | solution.py:362
  84.5 201.0 %collective-permute-start.4 = (bf16[96,4096]{1,0:T(8,128)(2,1)}, bf16[96,4096]{1,0:T(8,128)(2,1)}, u32[]{:S(2)}, u32[]{:S(2)}) collective-permute-start(bf16[96,4096]{1,0:T(8,128)(2,1)} %collective-permute-done), channel_id=1, source_target_pairs={{0,1},{1,0},{2,3},{3,2},{4,5},{5,4},{6,7},{7,6},{8,9},{9,8},{10,11... | collective-permute-start | bytes 2359304 | tf_op jit(solution)/shard_map/ppermute | solution.py:362
  97.6 190.0 %collective-permute-start.5 = (bf16[96,4096]{1,0:T(8,128)(2,1)}, bf16[96,4096]{1,0:T(8,128)(2,1)}, u32[]{:S(2)}, u32[]{:S(2)}) collective-permute-start(bf16[96,4096]{1,0:T(8,128)(2,1)} %collective-permute-done.1), channel_id=1, source_target_pairs={{0,1},{1,0},{2,3},{3,2},{4,5},{5,4},{6,7},{7,6},{8,9},{9,8},{10,11... | collective-permute-start | bytes 2359304 | tf_op jit(solution)/shard_map/ppermute | solution.py:362
  161.1 128.6 %collective-permute-start.6 = (bf16[96,4096]{1,0:T(8,128)(2,1)}, bf16[96,4096]{1,0:T(8,128)(2,1)}, u32[]{:S(2)}, u32[]{:S(2)}) collective-permute-start(bf16[96,4096]{1,0:T(8,128)(2,1)} %collective-permute-done.2), channel_id=1, source_target_pairs={{0,1},{1,0},{2,3},{3,2},{4,5},{5,4},{6,7},{7,6},{8,9},{9,8},{10,11... | collective-permute-start | bytes 2359304 | tf_op jit(solution)/shard_map/ppermute | solution.py:362
  161.9 129.9 %collective-permute-start.7 = (bf16[96,4096]{1,0:T(8,128)(2,1)}, bf16[96,4096]{1,0:T(8,128)(2,1)}, u32[]{:S(2)}, u32[]{:S(2)}) collective-permute-start(bf16[96,4096]{1,0:T(8,128)(2,1)} %collective-permute-done.3), channel_id=1, source_target_pairs={{0,1},{1,0},{2,3},{3,2},{4,5},{5,4},{6,7},{7,6},{8,9},{9,8},{10,11... | collective-permute-start | bytes 2359304 | tf_op jit(solution)/shard_map/ppermute | solution.py:362
  252.4 72.0 %all-to-all-start = ((bf16[8,2,128,768]{3,2,1,0:T(8,128)(2,1)}), bf16[8,2,128,768]{3,2,1,0:T(8,128)(2,1)}, u32[]{:S(2)}, u32[]{:S(2)}) async-start(bf16[8,2,128,768]{3,2,1,0:T(8,128)(2,1)} %maximum_bitcast_fusion), calls=%async_computation | async-start | bytes 6291456 | tf_op jit(solution)/shard_map/all_to_all | solution.py:457
  324.4 49.8 %all-to-all-start.2 = ((bf16[8,2,128,768]{3,2,1,0:T(8,128)(2,1)}), bf16[8,2,128,768]{3,2,1,0:T(8,128)(2,1)}, u32[]{:S(2)}, u32[]{:S(2)}) async-start(bf16[8,2,128,768]{3,2,1,0:T(8,128)(2,1)} %maximum_bitcast_fusion.1), calls=%async_computation.2 | async-start | bytes 6291456 | tf_op jit(solution)/shard_map/all_to_all | solution.py:457
  374.3 47.4 %all-to-all-start.1 = ((bf16[8,2,128,768]{3,2,1,0:T(8,128)(2,1)}), bf16[8,2,128,768]{3,2,1,0:T(8,128)(2,1)}, u32[]{:S(2)}, u32[]{:S(2)}) async-start(bf16[8,2,128,768]{3,2,1,0:T(8,128)(2,1)} %get-tuple-element.22), calls=%async_computation.1 | async-start | bytes 6291456 | tf_op jit(solution)/shard_map/all_to_all | solution.py:464
  421.7 70.1 %all-to-all-start.3 = ((bf16[8,2,128,768]{3,2,1,0:T(8,128)(2,1)}), bf16[8,2,128,768]{3,2,1,0:T(8,128)(2,1)}, u32[]{:S(2)}, u32[]{:S(2)}) async-start(bf16[8,2,128,768]{3,2,1,0:T(8,128)(2,1)} %get-tuple-element.23), calls=%async_computation.3 | async-start | bytes 6291456 | tf_op jit(solution)/shard_map/all_to_all | solution.py:464
  426.3 365.0 %reduce-scatter.4.cloned.1.call-start = ((), (), s32[]{:S(2)}) async-start(), calls=%async_computation.6 | async-start | bytes 5068800
  674.1 38.7 %collective-permute-start.37 = (bf16[256,768]{1,0:T(8,128)(2,1)S(1)}, bf16[256,768]{1,0:T(8,128)(2,1)S(1)}, u32[]{:S(2)}, u32[]{:S(2)}) collective-permute-start(bf16[256,768]{1,0:T(8,128)(2,1)S(1)} %get-tuple-element.122), channel_id=1, source_target_pairs={{4,0},{12,1},{5,4},{13,5},{0,8},{8,9},{1,12},{9,13},{20,16},{28,17... | collective-permute-start | bytes 1179656 | tf_op jit(solution)/shard_map/ppermute | solution.py:394
  677.3 59.2 %collective-permute-start.17 = (bf16[96,2048]{1,0:T(8,128)(2,1)S(1)}, bf16[96,2048]{1,0:T(8,128)(2,1)S(1)}, u32[]{:S(2)}, u32[]{:S(2)}) collective-permute-start(bf16[96,2048]{1,0:T(8,128)(2,1)S(1)} %get-tuple-element.133), channel_id=1, source_target_pairs={{0,0},{8,1},{1,4},{9,5},{4,8},{12,9},{5,12},{13,13},{16,16},{24,17... | collective-permute-start | bytes 1179656 | tf_op jit(solution)/shard_map/ppermute | solution.py:394
  704.7 57.7 %collective-permute-start.21 = (bf16[96,2048]{1,0:T(8,128)(2,1)S(1)}, bf16[96,2048]{1,0:T(8,128)(2,1)S(1)}, u32[]{:S(2)}, u32[]{:S(2)}) collective-permute-start(bf16[96,2048]{1,0:T(8,128)(2,1)S(1)} %get-tuple-element.130), channel_id=1, source_target_pairs={{4,0},{12,1},{5,4},{13,5},{0,8},{8,9},{1,12},{9,13},{20,16},{28,17... | collective-permute-start | bytes 1179656 | tf_op jit(solution)/shard_map/ppermute | solution.py:394
  712.8 50.9 %collective-permute-start.23 = (bf16[96,2048]{1,0:T(8,128)(2,1)S(1)}, bf16[96,2048]{1,0:T(8,128)(2,1)S(1)}, u32[]{:S(2)}, u32[]{:S(2)}) collective-permute-start(bf16[96,2048]{1,0:T(8,128)(2,1)S(1)} %get-tuple-element.131), channel_id=1, source_target_pairs={{20,0},{28,1},{21,4},{29,5},{16,8},{24,9},{17,12},{25,13},{4,16},{... | collective-permute-start | bytes 1179656 | tf_op jit(solution)/shard_map/ppermute | solution.py:394
  713.6 50.4 %collective-permute-start.25 = (bf16[96,2048]{1,0:T(8,128)(2,1)S(1)}, bf16[96,2048]{1,0:T(8,128)(2,1)S(1)}, u32[]{:S(2)}, u32[]{:S(2)}) collective-permute-start(bf16[96,2048]{1,0:T(8,128)(2,1)S(1)} %get-tuple-element.141), channel_id=1, source_target_pairs={{0,0},{8,1},{1,4},{9,5},{4,8},{12,9},{5,12},{13,13},{16,16},{24,17... | collective-permute-start | bytes 1179656 | tf_op jit(solution)/shard_map/ppermute | solution.py:394
  736.6 46.6 %collective-permute-start.29 = (bf16[96,2048]{1,0:T(8,128)(2,1)S(1)}, bf16[96,2048]{1,0:T(8,128)(2,1)S(1)}, u32[]{:S(2)}, u32[]{:S(2)}) collective-permute-start(bf16[96,2048]{1,0:T(8,128)(2,1)S(1)} %get-tuple-element.138), channel_id=1, source_target_pairs={{4,0},{12,1},{5,4},{13,5},{0,8},{8,9},{1,12},{9,13},{20,16},{28,17... | collective-permute-start | bytes 1179656 | tf_op jit(solution)/shard_map/ppermute | solution.py:394
  (202 other events, 2654.8 us)
Sparse Core Ops, SparseCore 0:
  12.6 161.4 all-gather.1
  627.4 163.4 reduce-scatter.3

commit v2 on v1

v2 whole, which is shorter than its diff:
```python
import functools
import math

import jax
import jax.numpy as jnp
from jax import lax
from jax.experimental import pallas as pl
from jax.experimental.pallas import tpu as pltpu
from jax.sharding import Mesh
from jax.sharding import PartitionSpec as P

D = 768
HEADS = 12
HEAD_DIM = 64
FF = 2048
EXPERTS = 8
SEQ = 512
CAP = 128
CHOICES = EXPERTS + 4
SLOTS = EXPERTS * CAP

EPSILON = 1e-05
ROPE_BASE = 10000.0
FLOOR_SCORE = -1e30
HIGHEST = lax.Precision.HIGHEST
BF = jnp.bfloat16
F32 = jnp.float32
VMEM_MOST = 56 * 2**20


def dot(a, b):
    return jnp.dot(a, b, preferred_element_type=F32)


def dot_nt(a, b):
    return lax.dot_general(a, b, (((1,), (1,)), ((), ())), preferred_element_type=F32)


def dot_tn(a, b):
    return lax.dot_general(a, b, (((0,), (0,)), ((), ())), preferred_element_type=F32)


def pair_slots(route, capacity):
    route_hot = (route[:, :, None] == jnp.arange(CHOICES, dtype=jnp.int32)).astype(F32)
    seq_index = jnp.arange(SEQ)
    before = (seq_index[:, None] > seq_index[None, :]).astype(BF)
    earlier = dot(before, jnp.sum(route_hot, axis=1).astype(BF))
    slot_rank = jnp.sum(earlier[:, None, :] * route_hot, axis=-1)
    cap_limit = jnp.sum(route_hot[:, :, :EXPERTS] * capacity.astype(F32), axis=-1)
    kept_pairs = (route < EXPERTS) & (slot_rank < cap_limit)
    return jnp.where(kept_pairs, route * CAP + slot_rank.astype(jnp.int32), -1)


HALF = SEQ // 2
FORWARD_LASTS = 100
PAIRS = HEADS // 2


def lanes(rows):
    return lax.broadcasted_iota(jnp.int32, (rows, 128), 1)


def swap_halves(v):
    low = lanes(v.shape[0]) % HEAD_DIM < HEAD_DIM // 2
    return jnp.where(low, pltpu.roll(v, 128 - HEAD_DIM // 2, 1), pltpu.roll(v, HEAD_DIM // 2, 1))


def row_mean(v):
    return jnp.sum(v, axis=1, keepdims=True) * (1.0 / D)


def head_masks():
    low = lax.broadcasted_iota(jnp.int32, (1, 128), 1) < HEAD_DIM
    return (jnp.where(low, 1.0, 0.0).astype(BF), jnp.where(low, 0.0, 1.0).astype(BF))


def forward_body(
    tok, cot, prev, route, slot_row, seg_col, seg_row, cos, sin, w_qkv, w_out, w_small, vecs,
    sent, qkv, att, resid, lse_out, aux, act, bias, tg0, tg1, lse,
):
    gain_one, gain_two = vecs[0:1, :], vecs[1:2, :]
    for r in range(2):
        rows = slice(r * HALF, (r + 1) * HALF)
        x = tok[rows, :].astype(F32)
        act[rows, :] = (x * lax.rsqrt(row_mean(x * x) + EPSILON) * gain_one).astype(BF)
        qi = lax.broadcasted_iota(jnp.int32, (HALF, SEQ), 0) + r * HALF
        ki = lax.broadcasted_iota(jnp.int32, (HALF, SEQ), 1)
        ok = (qi >= ki) & (seg_col[rows, :] == seg_row[...])
        bias[rows, :] = jnp.where(ok, 0.0, FLOOR_SCORE)
    for block in range(9):
        part = dot(act[...], w_qkv[:, block * 256 : block * 256 + 256])
        for i in range(2):
            v = part[:, i * 128 : i * 128 + 128]
            if block < 6:
                v = v * cos[...] + swap_halves(v) * sin[...]
            if block < 3:
                v = v * (1.0 / math.sqrt(HEAD_DIM))
            at = block * 256 + i * 128
            qkv[:, at : at + 128] = v.astype(BF)
    masks = head_masks()

    def pair(p, carry):
        q = qkv[:, pl.ds(pl.multiple_of(p * 128, 128), 128)]
        k = qkv[:, pl.ds(pl.multiple_of(D + p * 128, 128), 128)]
        v = qkv[:, pl.ds(pl.multiple_of(2 * D + p * 128, 128), 128)]
        for b in range(2):
            rows, reach = slice(b * HALF, (b + 1) * HALF), (b + 1) * HALF
            out = None
            for h in range(2):
                s = dot_nt(q[rows, :] * masks[h], k[:reach, :]) + bias[rows, :reach]
                top = jnp.max(s, axis=1, keepdims=True)
                e = jnp.exp(s - top)
                total = jnp.sum(e, axis=1, keepdims=True)
                o = dot((e * (1.0 / total)).astype(BF), v[:reach, :] * masks[h])
                out = o if out is None else out + o
                lse[rows, :] = jnp.where(lanes(HALF) == 2 * p + h, top + jnp.log(total), lse[rows, :])
            att[rows, pl.ds(pl.multiple_of(p * 128, 128), 128)] = out.astype(BF)
        return carry

    lax.fori_loop(0, PAIRS, pair, 0)
    lse_out[...] = lse[...].T[:16, :]
    lane = lanes(HALF)

    def column(v, at):
        return jnp.sum(jnp.where(lane == at, v, 0.0), axis=1, keepdims=True)

    for r in range(2):
        rows = slice(r * HALF, (r + 1) * HALF)
        res = tok[rows, :].astype(F32) + dot(att[rows, :], w_out[...])
        resid[rows, :] = res
        act2 = (res * lax.rsqrt(row_mean(res * res) + EPSILON) * gain_two).astype(BF)
        act[rows, :] = act2
        logits = dot(act2, w_small[...])
        router = logits + prev[rows, :].astype(F32)
        r0, r1 = column(router, route[rows, 0:1]), column(router, route[rows, 1:2])
        top = jnp.maximum(r0, r1)
        e0, e1 = jnp.exp(r0 - top), jnp.exp(r1 - top)
        g0, g1 = e0 / (e0 + e1), e1 / (e0 + e1)
        made = jnp.where(lane == 0, g0, jnp.where(lane == 1, g1, 0.0))
        for c in range(2):
            a, b = column(logits, CHOICES + 2 * c), column(logits, CHOICES + 2 * c + 1)
            top = jnp.maximum(a, b)
            ea, eb = jnp.exp(a - top), jnp.exp(b - top)
            made = jnp.where(lane == 2 + 2 * c, ea / (ea + eb), made)
            made = jnp.where(lane == 3 + 2 * c, eb / (ea + eb), made)
        aux[rows, :] = made
        g = cot[rows, :].astype(F32)
        tg0[rows, :] = (g0 * g).astype(BF)
        tg1[rows, :] = (g1 * g).astype(BF)

    def dispatch(b, carry):
        ids = lax.broadcasted_iota(jnp.int32, (256, SEQ), 0) + b * 256
        p0 = jnp.where(slot_row[0:1, :] == ids, 1.0, 0.0)
        p1 = jnp.where(slot_row[1:2, :] == ids, 1.0, 0.0)
        sent[pl.ds(b * 2, 2), 0] = dot((p0 + p1).astype(BF), act[...]).astype(BF).reshape(2, CAP, D)
        sg = dot(p0.astype(BF), tg0[...]) + dot(p1.astype(BF), tg1[...])
        sent[pl.ds(b * 2, 2), 1] = sg.astype(BF).reshape(2, CAP, D)
        return carry

    lax.fori_loop(0, SLOTS // 256, dispatch, 0)


def seq_block(width, part, col=0):
    return pl.BlockSpec((SEQ, width), lambda i, part=part, col=col: (part, col))


def fixed(shape, *at):
    at = at or (0,) * len(shape)
    return pl.BlockSpec(shape, lambda i, at=at: at)


def lasting(microseconds):
    return pl.CostEstimate(flops=microseconds * 10**9, bytes_accessed=0, transcendentals=0)


def kernel_params():
    return pltpu.CompilerParams(dimension_semantics=("arbitrary",), vmem_limit_bytes=VMEM_MOST)


def forward_part(part, t, packed, vecs):
    return pl.pallas_call(
        forward_body,
        grid=(1,),
        in_specs=[
            seq_block(D, part), seq_block(D, part), seq_block(128, part), seq_block(2, part),
            fixed((None, 2, SEQ), part, 0, 0), seq_block(1, part), fixed((None, 1, SEQ), part, 0, 0),
            seq_block(128, part), seq_block(128, part),
            fixed((D, 3 * D), 0, 0), fixed((D, D), 0, 3), fixed((D, 128), 0, 24), fixed((8, D)),
        ],
        out_specs=[
            fixed((EXPERTS, 2, CAP, D)), fixed((SEQ, 3 * D)), fixed((SEQ, D)), fixed((SEQ, D)),
            fixed((16, SEQ)), fixed((SEQ, 128)),
        ],
        out_shape=[
            jax.ShapeDtypeStruct((EXPERTS, 2, CAP, D), BF),
            jax.ShapeDtypeStruct((SEQ, 3 * D), BF),
            jax.ShapeDtypeStruct((SEQ, D), BF),
            jax.ShapeDtypeStruct((SEQ, D), F32),
            jax.ShapeDtypeStruct((16, SEQ), F32),
            jax.ShapeDtypeStruct((SEQ, 128), F32),
        ],
        scratch_shapes=[
            pltpu.VMEM((SEQ, D), BF), pltpu.VMEM((SEQ, SEQ), F32), pltpu.VMEM((SEQ, D), BF),
            pltpu.VMEM((SEQ, D), BF), pltpu.VMEM((SEQ, 128), F32),
        ],
        compiler_params=kernel_params(),
        cost_estimate=lasting(FORWARD_LASTS),
    )(
        t["tokens"], t["cotangent"], t["prev"], t["routes"], t["slot_row"], t["seg_col"], t["seg_row"],
        t["cos"], t["sin"], packed, packed, packed, vecs,
    )


def combine_body(
    prior, back, resid, cot, aux, slot, route, att, w_out, w_small, vecs, p_out, p_small, p_rows,
    out, rgrad, router_out, agrad, out_w, small_w, rows_w,
):
    @pl.when(pl.program_id(0) == 0)
    def _():
        if prior:
            out_w[...], small_w[...], rows_w[...] = p_out[...], p_small[...], p_rows[...]
        else:
            out_w[...] = jnp.zeros_like(out_w)
            small_w[...] = jnp.zeros_like(small_w)
            rows_w[...] = jnp.zeros_like(rows_w)

    gain_two = vecs[1:2, :]
    consts = (vecs[2:3, :], vecs[3:4, :])
    res = resid[...]
    g = cot[...].astype(F32)
    inverse = lax.rsqrt(row_mean(res * res) + EPSILON)
    unit = res * inverse
    normed = unit * gain_two
    lane = lanes(HALF)
    gates = (aux[:, 0:1], aux[:, 1:2])
    cg = ((aux[:, 2:3], aux[:, 3:4]), (aux[:, 4:5], aux[:, 5:6]))
    ids = lax.broadcasted_iota(jnp.int32, (HALF, SLOTS), 1)
    picks = [jnp.where(slot[:, k : k + 1] == ids, 1.0, 0.0) for k in range(2)]
    rows = back[:, 0].reshape(SLOTS, D)
    g_normed = jnp.sum(g * normed, axis=1, keepdims=True)
    g_const = [jnp.sum(g * v, axis=1, keepdims=True) for v in consts]
    gate_grads, straight, total = [], 0.0, res
    const_mask = [
        [jnp.where(route[:, k : k + 1] == EXPERTS + 2 + c, 1.0, 0.0) for c in range(2)] for k in range(2)
    ]
    for k in range(2):
        combined = dot(picks[k].astype(BF), rows)
        direct = jnp.where(route[:, k : k + 1] == EXPERTS + 1, 1.0, 0.0)
        for c in range(2):
            direct += const_mask[k][c] * cg[c][0]
        grad = jnp.sum(g * combined, axis=1, keepdims=True) + direct * g_normed
        for c in range(2):
            grad += const_mask[k][c] * cg[c][1] * g_const[c]
        gate_grads.append(grad)
        straight += gates[k] * direct
        total = total + gates[k] * combined
    total = total + straight * normed
    logit_grad = 0.0
    made = [jnp.zeros((1, D), F32)] * 2
    for c in range(2):
        share = const_mask[0][c] * gates[0] + const_mask[1][c] * gates[1]
        weight = share * cg[c][1]
        total = total + weight * consts[c]
        made[c] = jnp.sum(weight * g, axis=0, keepdims=True)
        first, second = share * g_normed, share * g_const[c]
        inner = cg[c][0] * first + cg[c][1] * second
        for i, v in enumerate((first, second)):
            logit_grad += jnp.where(lane == CHOICES + 2 * c + i, cg[c][i] * (v - inner), 0.0)
    out[...] = total.astype(BF)
    mean_grad = gates[0] * gate_grads[0] + gates[1] * gate_grads[1]
    router = 0.0
    for k in range(2):
        router += jnp.where(lane == route[:, k : k + 1], gates[k] * (gate_grads[k] - mean_grad), 0.0)
    router_out[...] = router[:, :CHOICES]
    logit_low = (router + logit_grad).astype(BF)
    small_w[...] += dot_tn(normed.astype(BF), logit_low)
    normed_grad = dot_nt(logit_low, w_small[...])
    normed_grad += dot((picks[0] + picks[1]).astype(BF), back[:, 1].reshape(SLOTS, D))
    normed_grad += straight * g
    scaled = normed_grad * gain_two
    gain_grad = jnp.sum(normed_grad * unit, axis=0, keepdims=True)
    residual_grad = g + inverse * (scaled - unit * row_mean(scaled * unit))
    rgrad[...] = residual_grad
    low = residual_grad.astype(BF)
    agrad[...] = dot_nt(low, w_out[...]).astype(BF)
    out_w[...] += dot_tn(att[...], low)
    rows_w[0:1, :] += made[0]
    rows_w[1:2, :] += made[1]
    rows_w[2:3, :] += gain_grad


def combine_part(part, back, kept, t, packed, vecs, prior):
    _, _, att, resid, _, aux = kept

    def tile(width, mine=True):
        base = 0 if mine else 2 * part
        return pl.BlockSpec((HALF, width), lambda i, base=base: (base + i, 0))

    sums = [
        jax.ShapeDtypeStruct((D, D), F32), jax.ShapeDtypeStruct((D, 128), F32), jax.ShapeDtypeStruct((8, D), F32)
    ]
    sum_specs = [fixed((D, D)), fixed((D, 128)), fixed((8, D))]
    body = functools.partial(combine_body, prior is not None)
    if prior is None:
        given = []

        def body(*refs):
            combine_body(False, *refs[:10], None, None, None, *refs[10:])

    else:
        given = list(prior)
    return pl.pallas_call(
        body,
        grid=(2,),
        in_specs=[
            fixed((EXPERTS, 2, CAP, D)), tile(D), tile(D, False), tile(128), tile(2, False), tile(2, False),
            tile(D), fixed((D, D), 0, 3), fixed((D, 128), 0, 24), fixed((8, D)),
        ] + (sum_specs if given else []),
        out_specs=[tile(D), tile(D), tile(CHOICES), tile(D)] + sum_specs,
        out_shape=[
            jax.ShapeDtypeStruct((SEQ, D), BF), jax.ShapeDtypeStruct((SEQ, D), F32),
            jax.ShapeDtypeStruct((SEQ, CHOICES), F32), jax.ShapeDtypeStruct((SEQ, D), BF),
        ] + sums,
        compiler_params=kernel_params(),
        cost_estimate=lasting(1),
    )(back, resid, t["cotangent"], aux, t["slots"], t["routes"], att, packed, packed, vecs, *given)


def attention_back_body(
    qkv, agrad, lse, seg_col, seg_row, cos, sin, w_qkv, tok, vecs, rgrad, grad_in, qkv_grad, act, gain_w, bias
):
    for b in range(2):
        rows = slice(b * HALF, (b + 1) * HALF)
        ki = lax.broadcasted_iota(jnp.int32, (HALF, SEQ), 0) + b * HALF
        qi = lax.broadcasted_iota(jnp.int32, (HALF, SEQ), 1)
        ok = (qi >= ki) & (seg_col[rows, :] == seg_row[...])
        bias[rows, :] = jnp.where(ok, 0.0, FLOOR_SCORE)
    masks = head_masks()
    scale = 1.0 / math.sqrt(HEAD_DIM)

    def one_pair(p, carry):
        at = [pl.ds(pl.multiple_of(i * D + p * 128, 128), 128) for i in range(3)]
        q, k, v = [qkv[:, a] for a in at]
        da = agrad[:, at[0]]
        kg, vg, qg = [None, None], [None, None], [None, None]

        def add(store, i, value):
            store[i] = value if store[i] is None else store[i] + value

        for h in range(2):
            qh, dh = q * masks[h], da * masks[h]
            probs, grads, keyed = [], [], []
            for b in range(2):
                keys, first = slice(b * HALF, (b + 1) * HALF), b * HALF
                kh = k[keys, :] * masks[h]
                st = dot_nt(kh, q[first:, :]) + bias[keys, first:]
                probs.append(jnp.exp(st - lse[pl.ds(2 * p + h, 1), first:]))
                grads.append(dot_nt(v[keys, :] * masks[h], da[first:, :]))
                keyed.append(kh)
            inner = [jnp.sum(probs[b] * grads[b], axis=0, keepdims=True) for b in range(2)]
            late = inner[0][:, HALF:] + inner[1]
            whole = jnp.concatenate([inner[0][:, :HALF], late], axis=1)
            for b, mean in enumerate((whole, late)):
                first = b * HALF
                ds = (probs[b] * (grads[b] - mean)).astype(BF)
                add(kg, b, dot(ds, qh[first:, :]))
                add(vg, b, dot(probs[b].astype(BF), dh[first:, :]))
                full = dot_tn(ds, keyed[b])
                if b == 0:
                    add(qg, 0, full[:HALF, :])
                    add(qg, 1, full[HALF:, :])
                else:
                    add(qg, 1, full)
        for b in range(2):
            rows = slice(b * HALF, (b + 1) * HALF)
            c, s = cos[rows, :], sin[rows, :]
            qb = qg[b] * scale
            qkv_grad[rows, at[0]] = (qb * c - swap_halves(qb) * s).astype(BF)
            qkv_grad[rows, at[1]] = (kg[b] * c - swap_halves(kg[b]) * s).astype(BF)
            qkv_grad[rows, at[2]] = vg[b].astype(BF)
        return carry

    lax.fori_loop(0, PAIRS, one_pair, 0)
    gain_one = vecs[0:1, :]
    gain_grad = 0.0
    for b in range(2):
        rows = slice(b * HALF, (b + 1) * HALF)
        x = tok[rows, :].astype(F32)
        inverse = lax.rsqrt(row_mean(x * x) + EPSILON)
        unit = x * inverse
        act[rows, :] = (unit * gain_one).astype(BF)
        grad = dot_nt(qkv_grad[rows, :], w_qkv[...])
        scaled = grad * gain_one
        gain_grad += jnp.sum(grad * unit, axis=0, keepdims=True)
        grad_in[rows, :] = rgrad[rows, :] + inverse * (scaled - unit * row_mean(scaled * unit))
    gain_w[...] = jnp.broadcast_to(gain_grad, gain_w.shape)


def attention_back(part, kept, rgrad, agrad, t, packed, vecs):
    _, qkv, _, _, lse, _ = kept
    return pl.pallas_call(
        attention_back_body,
        grid=(1,),
        in_specs=[
            fixed((SEQ, 3 * D)), fixed((SEQ, D)), fixed((16, SEQ)),
            seq_block(1, part), fixed((None, 1, SEQ), part, 0, 0), seq_block(128, part), seq_block(128, part),
            fixed((D, 3 * D), 0, 0), seq_block(D, part), fixed((8, D)), fixed((SEQ, D)),
        ],
        out_specs=[fixed((SEQ, D)), fixed((SEQ, 3 * D)), fixed((SEQ, D)), fixed((8, D))],
        out_shape=[
            jax.ShapeDtypeStruct((SEQ, D), F32), jax.ShapeDtypeStruct((SEQ, 3 * D), BF),
            jax.ShapeDtypeStruct((SEQ, D), BF), jax.ShapeDtypeStruct((8, D), F32),
        ],
        scratch_shapes=[pltpu.VMEM((SEQ, SEQ), F32)],
        compiler_params=kernel_params(),
        cost_estimate=lasting(1),
    )(
        qkv, agrad, lse, t["seg_col"], t["seg_row"], t["cos"], t["sin"], packed, t["tokens"], vecs, rgrad
    )


def qkv_wgrad_body(parts, *refs):
    acts, grads, out, turned = refs[:parts], refs[parts : 2 * parts], refs[2 * parts], refs[2 * parts + 1]

    @pl.when(pl.program_id(0) == 0)
    def _():
        for i in range(parts):
            turned[:, i * SEQ : (i + 1) * SEQ] = acts[i][...].T

    out[...] = dot(turned[...], jnp.concatenate([v[...] for v in grads], axis=0)).astype(BF)


def qkv_wgrad(acts, grads):
    parts = len(acts)
    return pl.pallas_call(
        functools.partial(qkv_wgrad_body, parts),
        grid=(3,),
        in_specs=[fixed((SEQ, D))] * parts + [pl.BlockSpec((SEQ, D), lambda i: (0, i))] * parts,
        out_specs=pl.BlockSpec((D, D), lambda i: (0, i)),
        out_shape=jax.ShapeDtypeStruct((D, 3 * D), BF),
        scratch_shapes=[pltpu.VMEM((D, parts * SEQ), BF)],
        compiler_params=kernel_params(),
        cost_estimate=lasting(1),
    )(*acts, *grads)


def tables(tokens, cotangent, prev_logits, routes, capacity, segments, positions):
    parts = tokens.shape[0] // SEQ
    slots = jnp.concatenate(
        [pair_slots(routes[i * SEQ : (i + 1) * SEQ], capacity) for i in range(parts)]
    )
    lane = jnp.arange(128) % HEAD_DIM
    frequency = jnp.exp((lane % (HEAD_DIM // 2)).astype(F32) * (-2.0 * math.log(ROPE_BASE) / HEAD_DIM))
    angles = positions.astype(F32)[:, None] * frequency[None, :]
    sign = jnp.where(lane < HEAD_DIM // 2, -1.0, 1.0)
    return dict(
        tokens=tokens,
        cotangent=cotangent,
        prev=jnp.pad(prev_logits, ((0, 0), (0, 128 - CHOICES))),
        routes=routes,
        slots=slots,
        slot_row=slots.reshape(parts, SEQ, 2).transpose(0, 2, 1),
        seg_col=segments[:, None],
        seg_row=segments.reshape(parts, 1, SEQ),
        cos=jnp.cos(angles),
        sin=jnp.sin(angles) * sign,
    )


FC = 512


def expert_rows_body(x_ref, g_ref, wg_ref, wu_ref, wd_ref, hid_ref, dg_ref, du_ref, out_ref, acc, racc):
    step = pl.program_id(0)
    x = x_ref[:, 0].reshape(-1, D)
    g = g_ref[:, 0].reshape(-1, D)
    wg, wu, wd = wg_ref[...], wu_ref[...], wd_ref[...]
    gate = dot(x, wg)
    up = dot(x, wu)
    hgrad = dot_nt(g, wd).astype(BF).astype(F32)
    sig = 1.0 / (1.0 + jnp.exp(-gate))
    act = gate * sig
    hidden = (act * up).astype(BF)
    dgate = (hgrad * up * sig * (1.0 + gate * (1.0 - sig))).astype(BF)
    dup = (hgrad * act).astype(BF)
    hid_ref[...] = hidden
    dg_ref[...] = dgate
    du_ref[...] = dup
    prod = dot(hidden, wd)
    rgrad = dot_nt(dgate, wg) + dot_nt(dup, wu)

    @pl.when(step == 0)
    def _():
        acc[...] = prod
        racc[...] = rgrad

    @pl.when(step > 0)
    def _():
        acc[...] += prod
        racc[...] += rgrad

    @pl.when(step == pl.num_programs(0) - 1)
    def _():
        out_ref[:, 0] = acc[...].astype(BF).reshape(-1, CAP, D)
        out_ref[:, 1] = racc[...].astype(BF).reshape(-1, CAP, D)


def expert_rows(received, w_gate_up, w_down):
    n = received.shape[0]
    rows = n * CAP
    steps = FF // FC
    wide = jax.ShapeDtypeStruct((rows, FF), BF)
    block = pl.BlockSpec((rows, FC), lambda j: (0, j))
    return pl.pallas_call(
        expert_rows_body,
        grid=(steps,),
        in_specs=[
            pl.BlockSpec((n, 1, CAP, D), lambda j: (0, 0, 0, 0)),
            pl.BlockSpec((n, 1, CAP, D), lambda j: (0, 1, 0, 0)),
            pl.BlockSpec((D, FC), lambda j: (0, j)),
            pl.BlockSpec((D, FC), lambda j: (0, steps + j)),
            pl.BlockSpec((FC, D), lambda j: (j, 0)),
        ],
        out_specs=[block, block, block, pl.BlockSpec((n, 2, CAP, D), lambda j: (0, 0, 0, 0))],
        out_shape=[wide, wide, wide, jax.ShapeDtypeStruct((n, 2, CAP, D), BF)],
        scratch_shapes=[pltpu.VMEM((rows, D), F32), pltpu.VMEM((rows, D), F32)],
        compiler_params=pltpu.CompilerParams(
            dimension_semantics=("arbitrary",), vmem_limit_bytes=VMEM_MOST
        ),
        cost_estimate=lasting(28),
    )(received, received, w_gate_up, w_gate_up, w_down)


FW = 512


def down_wgrad_body(parts, *refs):
    hid, received, out = refs[:parts], refs[parts : 2 * parts], refs[2 * parts]
    rows = jnp.concatenate([v[:, 0].reshape(-1, D) for v in received], axis=0)
    out[...] = dot_tn(jnp.concatenate([v[...] for v in hid], axis=0), rows).astype(BF)


def down_wgrad(received, hid):
    parts, (n, _, _, _) = len(received), received[0].shape
    return pl.pallas_call(
        functools.partial(down_wgrad_body, parts),
        grid=(FF // FW,),
        in_specs=[pl.BlockSpec((n * CAP, FW), lambda j: (0, j))] * parts
        + [pl.BlockSpec((n, 1, CAP, D), lambda j: (0, 1, 0, 0))] * parts,
        out_specs=pl.BlockSpec((FW, D), lambda j: (j, 0)),
        out_shape=jax.ShapeDtypeStruct((FF, D), BF),
        compiler_params=kernel_params(),
        cost_estimate=lasting(10),
    )(*hid, *received)


def gate_up_wgrad_body(parts, *refs):
    received, dg, du = refs[:parts], refs[parts : 2 * parts], refs[2 * parts : 3 * parts]
    out, xt = refs[3 * parts :]
    rows = received[0].shape[0] * CAP

    @pl.when(pl.program_id(0) == 0)
    def _():
        for i in range(parts):
            xt[:, i * rows : (i + 1) * rows] = received[i][:, 0].reshape(rows, D).T

    for k, grads in enumerate((dg, du)):
        out[k] = dot(xt[...], jnp.concatenate([v[...] for v in grads], axis=0)).astype(BF)


def gate_up_wgrad(received, dg, du):
    parts, (n, _, _, _) = len(received), received[0].shape
    return pl.pallas_call(
        functools.partial(gate_up_wgrad_body, parts),
        grid=(FF // FW,),
        in_specs=[pl.BlockSpec((n, 1, CAP, D), lambda j: (0, 0, 0, 0))] * parts
        + [pl.BlockSpec((n * CAP, FW), lambda j: (0, j))] * (2 * parts),
        out_specs=pl.BlockSpec((2, D, FW), lambda j: (0, 0, j)),
        out_shape=jax.ShapeDtypeStruct((2, D, FF), BF),
        scratch_shapes=[pltpu.VMEM((D, parts * n * CAP), BF)],
        compiler_params=kernel_params(),
        cost_estimate=lasting(20),
    )(*received, *dg, *du)


def place_body(spots, count, *refs):
    offsets, blocks, outs, sems = refs[0], refs[1 : 1 + count], refs[1 + count : -1], refs[-1]
    copies = []
    for i, (block, first, rows, out, column) in enumerate(spots):
        width = blocks[block].shape[1]
        start = pl.multiple_of(offsets[2 * i], 16)
        across = pl.ds(pl.multiple_of(offsets[2 * i + 1], 128), width) if column else pl.ds(0, width)
        copies.append(
            pltpu.make_async_copy(
                blocks[block].at[pl.ds(first, rows), :], outs[out].at[pl.ds(start, rows), across], sems.at[i]
            )
        )
    for copy in copies:
        copy.start()
    for copy in copies:
        copy.wait()


def place(blocks, spots, offsets, shapes):
    size = sum(math.prod(v) for v in shapes) * 4
    anywhere = pl.BlockSpec(memory_space=pl.ANY)
    return pl.pallas_call(
        functools.partial(place_body, spots, len(blocks)),
        in_specs=[pl.BlockSpec(memory_space=pltpu.SMEM)] + [anywhere] * len(blocks),
        out_specs=[pl.BlockSpec(memory_space=pltpu.VMEM)] * len(shapes),
        out_shape=[jax.ShapeDtypeStruct(v, BF) for v in shapes],
        scratch_shapes=[pltpu.SemaphoreType.DMA((len(spots),))],
        compiler_params=pltpu.CompilerParams(vmem_limit_bytes=VMEM_MOST),
        cost_estimate=lasting(size // 2**20),
    )(jnp.stack(offsets).astype(jnp.int32), *blocks)


def pick(value, index, axis=0):
    return lax.dynamic_index_in_dim(value, index, axis, False)


def added(*values):
    return sum(v.astype(F32) for v in values).astype(BF)


class Paired:
    axes = ("half", "low", "inner", "side", "core")
    fsdp = ("half", "low", "inner")
    expert = ("side", "core")
    rows = ("side", "low", "inner")
    route_axes = ("half", "low", "inner", "core")
    near = 896

    def __init__(self, mesh):
        self.mesh = Mesh(mesh.devices.reshape(2, 2, 2, 2, 2), self.axes)
        self.routes = []
        for turn in range(4):
            pairs = []
            for z in range(4):
                for y in range(2):
                    for c in range(2):
                        half, inner = (z ^ turn) >> 1, (z ^ turn) & 1
                        pairs.append(((z * 2 + y) * 2 + c, ((half * 2 + c) * 2 + inner) * 2 + y))
            self.routes.append(pairs)

    @staticmethod
    def swap(value, axis="core"):
        return lax.ppermute(value, axis, [(0, 1), (1, 0)])

    @staticmethod
    def along(value, turn):
        return lax.ppermute(value, ("half", "low"), [(i, i ^ turn) for i in range(4)])

    @staticmethod
    def spot():
        z = lax.axis_index("half") * 2 + lax.axis_index("low")
        return z, lax.axis_index("inner"), lax.axis_index("side"), lax.axis_index("core")

    def send(self, weights, which, turn):
        mine = pick(weights[which], (self.spot()[0] ^ turn) & 1)
        return lax.ppermute(mine, self.route_axes, self.routes[turn])

    def gather_shared(self, shard, weights, early):
        z, y, x, c = self.spot()
        rows, width = shard.shape
        rows, width = rows // 2, width // 2
        mine = lax.dynamic_slice(shard, (c * rows, x * width), (rows, width))
        stack = jnp.concatenate([mine] + [self.along(mine, turn) for turn in (1, 2, 3)])
        stack, weights, early = lax.optimization_barrier((stack, weights, early))
        sent = {(0, 2): self.send(weights, 0, 2)}
        over_y, over_x = self.swap(stack, "inner"), self.swap(stack, "side")
        far = self.swap(over_y[:, : self.near], "side"), self.swap(over_x[:, self.near :], "inner")
        blocks = [stack, over_y, over_x, *far]
        flips = [(0, 0, 0), (1, 0, 0), (0, 1, 0), (1, 1, 0), (1, 1, self.near)]
        spots, offsets = [], []
        for i, (dy, dx, column) in enumerate(flips + flips):
            core = c if i < len(flips) else 1 - c
            for turn in range(4):
                spots.append((i, turn * rows, rows, 0, True))
                offsets += [((z ^ turn) * 2 + (y ^ dy)) * 2 * rows + core * rows, (x ^ dx) * width + column]
        blocks += [self.swap(v) for v in blocks]
        blocks, weights, sent = lax.optimization_barrier((blocks, weights, sent))
        [full] = place(blocks, spots, offsets, [(16 * rows, 2 * width)])
        return full, early, (weights, sent)

    def gather_more(self, held, value, names):
        weights, sent = held
        more = [self.send(weights, *v) for v in names]
        value, weights, more = lax.optimization_barrier((value, weights, more))
        return (weights, {**sent, **dict(zip(names, more))}), value

    def reduce_shared(self, total):
        z, y, x, c = self.spot()
        rows, width = total.shape[0] // 16, total.shape[1] // 2
        near = (width // 128 + 1) // 2 * 128
        total = total.reshape(4, 2, 2, rows, 2 * width)
        total = added(pick(total, c, 2), self.swap(pick(total, 1 - c, 2)))
        parts = total.reshape(4, 2, rows, 2, width)
        one, two = parts[..., :near], parts[..., near:]
        one = added(pick(one, x, 3), self.swap(pick(one, 1 - x, 3), "side"))
        two = added(pick(two, y, 1), self.swap(pick(two, 1 - y, 1), "inner"))
        one = added(pick(one, y, 1), self.swap(pick(one, 1 - y, 1), "inner"))
        two = added(pick(two, x, 2), self.swap(pick(two, 1 - x, 2), "side"))
        both = jnp.concatenate([one, two], axis=2)
        mine = added(pick(both, z), *[self.along(pick(both, z ^ turn), turn) for turn in (1, 2, 3)])
        other = self.swap(mine, "side")
        line = jnp.where(x == 0, jnp.concatenate([mine, other], 1), jnp.concatenate([other, mine], 1))
        other = self.swap(line)
        both = jnp.where(c == 0, jnp.concatenate([line, other]), jnp.concatenate([other, line]))
        return both.astype(F32)

    def gather_expert(self, held):
        weights, sent = held
        c = lax.axis_index("core")
        here = lax.axis_index("half") * 2 + lax.axis_index("inner")
        names = [(which, turn) for which in range(2) for turn in range(4)]
        own = [sent[v] if v in sent else self.send(weights, *v) for v in names]
        blocks = own + [self.swap(v) for v in own]
        spots, offsets = [], []
        for i, block in enumerate(blocks):
            which, turn = i % len(own) // 4, i % 4
            rows = block.shape[0]
            core = c if i < len(own) else 1 - c
            spots.append((i, 0, rows, which, False))
            offsets += [((here ^ turn) * 2 + core) * rows, jnp.int32(0)]
        return place(blocks, spots, offsets, [(8 * w.shape[1], w.shape[2]) for w in weights])

    def scatter_start(self, grad, axis):
        c = lax.axis_index("core")
        shape = grad.shape
        grad = grad.reshape(shape[:axis] + (4, 2, shape[axis] // 8) + shape[axis + 1 :])
        return added(pick(grad, c, axis + 1), self.swap(pick(grad, 1 - c, axis + 1)))

    def scatter_send(self, parts, axis):
        here = lax.axis_index("half") * 2 + lax.axis_index("inner")
        got = {}
        for turn in (2, 3, 0, 1):
            back = [(b, a) for a, b in self.routes[turn]]
            got[turn] = lax.ppermute(pick(parts, here ^ turn, axis), self.route_axes, back)
        return got

    def scatter_end(self, got, axis):
        even = (self.spot()[0] & 1) == 0
        first, second = [got[i].astype(F32) + got[i + 2].astype(F32) for i in range(2)]
        return jnp.stack([jnp.where(even, first, second), jnp.where(even, second, first)])


class Plain:
    axes = ("outer", "inner", "expert")
    fsdp = ("outer", "inner")
    expert = ("expert",)
    rows = ("expert", "inner")

    def __init__(self, mesh):
        fsdp, expert = mesh.shape["fsdp"], mesh.shape["expert"]
        inner = EXPERTS // expert
        self.mesh = Mesh(mesh.devices.reshape(fsdp // inner, inner, expert), self.axes)

    def gather_shared(self, shard, weights, early):
        return lax.all_gather(shard, self.fsdp, axis=0, tiled=True), early, weights

    def gather_more(self, held, value, names):
        return held, value

    def reduce_shared(self, total):
        total = lax.psum_scatter(total, self.axes, scatter_dimension=0, tiled=True)
        return lax.all_gather(total, self.expert, axis=0, tiled=True).astype(F32)

    def gather_expert(self, weights):
        full = []
        for weight in weights:
            own = lax.all_to_all(weight, "inner", 0, 0, tiled=True)
            own = lax.all_gather(own, "outer", axis=0, tiled=True)
            full.append(own.reshape((-1,) + weight.shape[2:]))
        return full

    def scatter_start(self, grad, axis):
        return grad

    def scatter_send(self, grad, axis):
        return grad

    def scatter_end(self, grad, axis):
        inner = lax.axis_size("inner")
        part = lax.psum_scatter(grad, "outer", scatter_dimension=axis, tiled=True)
        shape = part.shape
        part = part.reshape(shape[:axis] + (inner, shape[axis] // inner) + shape[axis + 1 :])
        part = jnp.moveaxis(part, axis, 0)
        return lax.all_to_all(part, "inner", 0, 0, tiled=True).astype(F32)


def solution(mesh):
    plan = Paired(mesh) if (mesh.shape["fsdp"], mesh.shape["expert"]) == (8, 4) else Plain(mesh)

    def on_device(
        tokens, cotangent, prev_logits, routes, capacity, segments, positions,
        w_qkv, w_out, gate_matrix, const_values, attn_gain, moe_gain, w_gate_up, w_down,
    ):
        rows = w_qkv.shape[0]
        pad = jnp.zeros((rows, 256 - 20), BF)
        small = jnp.concatenate(
            [gate_matrix, const_values, attn_gain[:, None], moe_gain[:, None], pad], axis=1
        )
        shard = jnp.concatenate([w_qkv, w_out, small], axis=1)
        t = tables(tokens, cotangent, prev_logits, routes, capacity, segments, positions)
        packed, t, held = plan.gather_shared(shard, (w_gate_up, w_down), t)
        columns = packed[:, 4 * D + 16 : 4 * D + 20].astype(F32).T
        vecs = jnp.concatenate([columns[2:], columns[:2], jnp.zeros((4, D), F32)])
        parts = tokens.shape[0] // SEQ
        kept, shared = [], packed
        for i in range(parts):
            if i == 1:
                held, shared = plan.gather_more(held, packed, ((1, 2), (1, 3)))
            kept.append(forward_part(i, t, shared, vecs))
        sends = [k[0] for k in kept]
        held, sends[-1] = plan.gather_more(held, sends[-1], ((0, 3), (0, 0)))
        gate_up_full, down_full = plan.gather_expert(held)
        received = [lax.all_to_all(v, plan.rows, 0, 0, tiled=True) for v in sends]
        made = [expert_rows(r, gate_up_full, down_full) for r in received]
        returned = [lax.all_to_all(m[3], plan.rows, 0, 0, tiled=True) for m in made]
        hid, dg, du = [[m[i] for m in made] for i in range(3)]
        started = plan.scatter_start(down_wgrad(received, hid), 0)
        dg, started = lax.optimization_barrier((dg, started))
        down_got = plan.scatter_send(started, 0)
        started = plan.scatter_start(gate_up_wgrad(received, dg, du), 1)
        firsts, lasts, sums = [], [], None
        for i in range(parts):
            *first, out_w, small_w, rows_w = combine_part(i, returned[i], kept[i], t, packed, vecs, sums)
            sums = (out_w, small_w, rows_w)
            if i == 0:
                first[1], started, down_got = lax.optimization_barrier((first[1], started, down_got))
                down_total = plan.scatter_end(down_got, 0)
                gate_up_got = plan.scatter_send(started, 1)
            firsts.append(first)
            lasts.append(attention_back(i, kept[i], first[1], first[3], t, packed, vecs))
        out_w = plan.reduce_shared(sums[0].astype(BF))
        qkv_w = qkv_wgrad([v[2] for v in lasts], [v[1] for v in lasts])
        gate_up_got, _ = lax.optimization_barrier((gate_up_got, qkv_w))
        gate_up_total = plan.scatter_end(gate_up_got, 1)
        gate_up_total = jnp.concatenate([gate_up_total[:, 0], gate_up_total[:, 1]], axis=2)
        gain_one_grad = sum(v[3][0] for v in lasts)
        row_sums = jnp.concatenate([sums[2][:2], gain_one_grad[None], sums[2][2:3]])
        small_sum = jnp.concatenate(
            [sums[1][:, :16], row_sums.T, jnp.zeros((D, 256 - 20), F32)], axis=1
        )
        total = plan.reduce_shared(jnp.concatenate([qkv_w, small_sum.astype(BF)], axis=1))
        return (
            jnp.concatenate([v[0] for v in firsts]),
            jnp.concatenate([v[0] for v in lasts]),
            jnp.concatenate([v[2] for v in firsts]),
            total[:, : 3 * D],
            out_w,
            total[:, 3 * D : 3 * D + 16],
            total[:, 3 * D + 16 : 3 * D + 18],
            total[:, 3 * D + 18],
            total[:, 3 * D + 19],
            gate_up_total,
            down_total,
        )

    every = plan.fsdp + plan.expert
    split = P(every, None)
    shard = P(plan.fsdp, None)
    line = P(plan.fsdp)
    whole = P(plan.expert, plan.fsdp, None)
    return jax.shard_map(
        on_device,
        mesh=plan.mesh,
        in_specs=(
            split, split, split, split, P(), P(every), P(every),
            shard, shard, shard, shard, line, line, whole, whole,
        ),
        out_specs=(split, split, split, shard, shard, shard, shard, line, line, whole, whole),
        check_vma=False,
    )
```

time: 833 us -> 581 us (0.70)
  matrix products: 162 us -> 0.47 us
  Pallas kernels: 84.8 us -> 216 us
  local copies, waits for them, and re-layouts: 142 us -> 56.6 us
  waiting for transfers between devices: 164 us -> 116 us
  starting transfers between devices: 169 us -> 142 us
  other arithmetic: 63.9 us -> 38.8 us
  blocking collectives: 23.6 us -> 0 us
  between operations: 17.1 us -> 2.02 us
    pallas_call x1 -> x11, Pallas kernels: 27.7 us -> 159 us  [the longest x2 40.5 us: forward_part(): pl.pallas_call(forward_body, grid=(1,), in_specs=[seq_block(D, part), seq...]
    dot_general x22 -> x0, matrix products: 107 us -> none  [the longest x2 27.2 us: backward_part(): jnp.einsum('qhd,khd->hqk', attended_grad, k['value_low'], preferred_eleme...]
    unnamed x403 -> x76, local copies, waits for them, and re-layouts: 66.4 us -> 9.23 us
    dot_general x22 -> x2, matrix products: 54.8 us -> 0.47 us  [dot(): return jnp.dot(a, b, preferred_element_type=F32)]
    all_to_all x4, waiting for transfers between devices: 37.4 us -> 0.01 us  [the longest x2 0.01 us: on_device(): received = [lax.all_to_all(v, plan.rows, 0, 0, tiled=True) for v in sends]]
    all_gather x1 -> x0, blocking collectives: 23.6 us -> none  [on_device(): total = lax.all_gather(total, plan.expert, axis=0, tiled=True).astype(F32)]
    all_to_all x4, starting transfers between devices: 42 us -> 19.6 us  [the longest x2 9.9 us: on_device(): received = [lax.all_to_all(v, plan.rows, 0, 0, tiled=True) for v in sends]]
    slice x23 -> x13, local copies, waits for them, and re-layouts: 26.2 us -> 6.82 us  [the longest x3 3.29 us: reduce_shared(): one, two = (parts[..., :near], parts[..., near:])]
  transfers between devices with their start and end apart: 46 -> 62, of which waited for: 11 -> 17; matrix products, arithmetic and copies ran while one was open for 26% -> 14% of each run, Pallas kernels for 10% -> 37%
where the time goes in v2:
time: 581 us; the launch traced here: 572 us
  Pallas kernels  216 us (37%)
  starting transfers between devices  142 us (24%)
  waiting for transfers between devices  116 us (20%)
  local copies, waits for them, and re-layouts  56.6 us (10%)
  other arithmetic  38.8 us (7%)
    ppermute x33, starting transfers between devices, swap(): return lax.ppermute(value, axis, [(0, 1), (1, 0)])  72.6 us
    ppermute x8, waiting for transfers between devices, send(): return lax.ppermute(mine, self.route_axes, self.routes[turn])  58.2 us
    pallas_call x2, Pallas kernels, expert_rows(): pl.pallas_call(expert_rows_body, grid=(steps,), in_specs=[pl.BlockSpec((n...  57.2 us
    pallas_call x2, Pallas kernels, forward_part(): pl.pallas_call(forward_body, grid=(1,), in_specs=[seq_block(D, part), seq...  40.5 us
    pallas_call x2, Pallas kernels, attention_back(): pl.pallas_call(attention_back_body, grid=(1,), in_specs=[fixed((SEQ, 3 *...  36.2 us
    ppermute x33, waiting for transfers between devices, swap(): return lax.ppermute(value, axis, [(0, 1), (1, 0)])  34 us
    pallas_call x2, Pallas kernels, combine_part(): pl.pallas_call(body, grid=(2,), in_specs=[fixed((EXPERTS, 2, CAP, D)), ti...  29.8 us
    ppermute x8, starting transfers between devices, send(): return lax.ppermute(mine, self.route_axes, self.routes[turn])  20.5 us
  transfers between devices with their start and end apart: 62, of which 17 were waited for; matrix products, arithmetic and copies ran while one was open for 14% of the time, Pallas kernels for 37%

profile of v2, /device:TPU:1, one launch (start us, length us, event | category | flops | bytes accessed | tf_op | source)
XLA Modules:
  0.0 571.8 jit_solution(12776283749485782858)
XLA Ops:
  37.8 8.4 %collective-permute-start.8 = (bf16[192,1664]{1,0:T(8,128)(2,1)}, bf16[192,1664]{1,0:T(8,128)(2,1)}, u32[]{:S(2)}, u32[]{:S(2)}) collective-permute-start(bf16[192,1664]{1,0:T(8,128)(2,1)} %collective-permute-done.3.refs_2_), channel_id=1, source_target_pairs={{0,1},{1,0},{2,3},{3,2},{4,5},{5,4},{6,7},{7,6},{8,9},{9,8},{10,11... | collective-permute-start | bytes 1916936 | tf_op jit(solution)/shard_map/ppermute | solution.py:648
  51.4 11.5 %collective-permute-done.6.refs_5_ = bf16[192,768]{1,0:T(8,128)(2,1)} collective-permute-done((bf16[192,768]{1,0:T(8,128)(2,1)S(1)}, bf16[192,768]{1,0:T(8,128)(2,1)}, u32[]{:S(2)}, u32[]{:S(2)}) %collective-permute-start.6) | collective-permute-done | bytes 294944 | tf_op jit(solution)/shard_map/ppermute | solution.py:648
  66.9 6.0 %shard_map.230.w_qkv.w_out.w_small.refs_7_.refs_8_ = bf16[768,3328]{1,0:T(8,128)(2,1)} custom-call(s32[80]{0:T(128)} %stack.209.refs_0_, bf16[192,1664]{1,0:T(8,128)(2,1)} %pad_maximum_fusion.5.refs_1_, bf16[192,1664]{1,0:T(8,128)(2,1)} %collective-permute-done.3.refs_2_, bf16[192,1664]{1,0:T(8,128)(2,1)} %collective-permute-done.4.refs_3_, ...), custom_call_target="tpu_custom_call" | custom-call | flops 8999999488 | tf_op jit(solution)/shard_map/pallas_call | solution.py:607
  78.1 20.3 %shard_map.231 = (bf16[8,2,128,768]{3,2,1,0:T(8,128)(2,1)}, bf16[512,2304]{1,0:T(8,128)(2,1)}, bf16[512,768]{1,0:T(8,128)(2,1)}, f32[512,768]{1,0:T(8,128)}, f32[16,512]{1,0:T(8,128)}, /*index=5*/f32[512,128]{1,0:T(8,128)}) custom-call(bf16[1024,768]{1,0:T(8,128)(2,1)} %tok.3, bf16[1024,768]{1,0:T(8,128)(2,1)} %cot.2, bf16[1024,128]{1,0:T(8,128)(2,1)} %pad.4.prev, ...), custom_call_target="tpu_custom_call" | custom-call | flops 99999997952 | tf_op jit(solution)/shard_map/pallas_call | solution.py:181
  109.1 6.6 %collective-permute-start.16 = (bf16[96,4096]{1,0:T(8,128)(2,1)S(1)}, bf16[96,4096]{1,0:T(8,128)(2,1)S(1)}, u32[]{:S(2)}, u32[]{:S(2)}) collective-permute-start(bf16[96,4096]{1,0:T(8,128)(2,1)S(1)} %get-tuple-element.272), channel_id=1, source_target_pairs={{0,0},{1,8},{4,1},{5,9},{8,4},{9,12},{12,5},{13,13},{16,16},{17,24... | collective-permute-start | bytes 2359304 | tf_op jit(solution)/shard_map/ppermute | solution.py:661
  115.8 20.3 %shard_map.232 = (bf16[8,2,128,768]{3,2,1,0:T(8,128)(2,1)}, bf16[512,2304]{1,0:T(8,128)(2,1)}, bf16[512,768]{1,0:T(8,128)(2,1)}, f32[512,768]{1,0:T(8,128)}, f32[16,512]{1,0:T(8,128)}, /*index=5*/f32[512,128]{1,0:T(8,128)}) custom-call(bf16[1024,768]{1,0:T(8,128)(2,1)} %tok.3, bf16[1024,768]{1,0:T(8,128)(2,1)} %cot.2, bf16[1024,128]{1,0:T(8,128)(2,1)} %pad.4.prev, ...), custom_call_target="tpu_custom_call" | custom-call | flops 99999997952 | tf_op jit(solution)/shard_map/pallas_call | solution.py:181
  136.0 28.9 %collective-permute-done.15.refs_4_ = bf16[96,4096]{1,0:T(8,128)(2,1)S(1)} collective-permute-done((bf16[96,4096]{1,0:T(8,128)(2,1)S(1)}, bf16[96,4096]{1,0:T(8,128)(2,1)S(1)}, u32[]{:S(2)}, u32[]{:S(2)}) %collective-permute-start.15) | collective-permute-done | bytes 786464 | tf_op jit(solution)/shard_map/ppermute | solution.py:661
  165.0 9.8 %collective-permute-done.16.refs_1_ = bf16[96,4096]{1,0:T(8,128)(2,1)S(1)} collective-permute-done((bf16[96,4096]{1,0:T(8,128)(2,1)S(1)}, bf16[96,4096]{1,0:T(8,128)(2,1)S(1)}, u32[]{:S(2)}, u32[]{:S(2)}) %collective-permute-start.16) | collective-permute-done | bytes 786464 | tf_op jit(solution)/shard_map/ppermute | solution.py:661
  193.0 25.4 %collective-permute-start.21 = (bf16[96,4096]{1,0:T(8,128)(2,1)}, bf16[96,4096]{1,0:T(8,128)(2,1)}, u32[]{:S(2)}, u32[]{:S(2)}) collective-permute-start(bf16[96,4096]{1,0:T(8,128)(2,1)} %collective-permute-done.17.refs_2_), channel_id=1, source_target_pairs={{0,1},{1,0},{2,3},{3,2},{4,5},{5,4},{6,7},{7,6},{8,9},{9,8},{10,11... | collective-permute-start | bytes 2359304 | tf_op jit(solution)/shard_map/ppermute | solution.py:648
  218.4 11.9 %collective-permute-done.18.refs_5_ = bf16[256,768]{1,0:T(8,128)(2,1)} collective-permute-done((bf16[256,768]{1,0:T(8,128)(2,1)S(1)}, bf16[256,768]{1,0:T(8,128)(2,1)}, u32[]{:S(2)}, u32[]{:S(2)}) %collective-permute-start.18) | collective-permute-done | bytes 393248 | tf_op jit(solution)/shard_map/ppermute | solution.py:661
  236.3 8.2 %shard_map.233 = (bf16[768,4096]{1,0:T(8,128)(2,1)}, bf16[2048,768]{1,0:T(8,128)(2,1)}) custom-call(s32[32]{0:T(128)} %stack.226.refs_0_, bf16[96,4096]{1,0:T(8,128)(2,1)} %copy-done.24, bf16[96,4096]{1,0:T(8,128)(2,1)} %collective-permute-done.17.refs_2_, bf16[96,4096]{1,0:T(8,128)(2,1)} %collective-permute-done.12.refs_3_, bf16[96,4096]{1,0:T(8,128)(2,1)} %copy-done.23, ...), custom_call_target="tpu_custom_call" | custom-call | flops 17999998976 | tf_op jit(solution)/shard_map/pallas_call | solution.py:607
  244.6 28.6 %shard_map.234 = (bf16[1024,2048]{1,0:T(8,128)(2,1)}, bf16[1024,2048]{1,0:T(8,128)(2,1)}, bf16[1024,2048]{1,0:T(8,128)(2,1)}, bf16[8,2,128,768]{3,2,1,0:T(8,128)(2,1)}) custom-call(bf16[8,2,128,768]{3,2,1,0:T(8,128)(2,1)} %all-to-all-done.x_ref.g_ref.refs_2_.refs_0_, bf16[8,2,128,768]{3,2,1,0:T(8,128)(2,1)} %all-to-all-done.x_ref.g_ref.refs_2_.refs_0_, ...), custom_call_target="tpu_custom_call" | custom-call | flops 28000000000 | tf_op jit(solution)/shard_map/pallas_call | solution.py:514
  279.7 28.6 %shard_map.236 = (bf16[1024,2048]{1,0:T(8,128)(2,1)}, bf16[1024,2048]{1,0:T(8,128)(2,1)}, bf16[1024,2048]{1,0:T(8,128)(2,1)}, bf16[8,2,128,768]{3,2,1,0:T(8,128)(2,1)}) custom-call(bf16[8,2,128,768]{3,2,1,0:T(8,128)(2,1)} %copy-done.5, bf16[8,2,128,768]{3,2,1,0:T(8,128)(2,1)} %copy-done.5, bf16[768,4096]{1,0:T(8,128)(2,1)} %get-tuple-element.140.wg_ref.wu_ref, ...), custom_call_target="tpu_custom_call" | custom-call | flops 28000000000 | tf_op jit(solution)/shard_map/pallas_call | solution.py:514
  308.3 10.9 %shard_map.238 = bf16[2048,768]{1,0:T(8,128)(2,1)} custom-call(bf16[1024,2048]{1,0:T(8,128)(2,1)} %get-tuple-element.163.refs_0_, bf16[1024,2048]{1,0:T(8,128)(2,1)} %get-tuple-element.164.refs_1_, bf16[8,2,128,768]{3,2,1,0:T(8,128)(2,1)} %all-to-all-done.x_ref.g_ref.refs_2_.refs_0_, bf16[8,2,128,768]{3,2,1,0:T(8,128)(2,1)} %copy-done.5), custom_call_target="tpu_custom_call" | custom-call | flops 10000000000 | tf_op jit(solution)/shard_map/pallas_call | solution.py:545
  335.8 19.1 %shard_map.239 = bf16[2,768,2048]{2,1,0:T(8,128)(2,1)} custom-call(bf16[8,2,128,768]{3,2,1,0:T(8,128)(2,1)} %all-to-all-done.x_ref.g_ref.refs_2_.refs_0_, bf16[8,2,128,768]{3,2,1,0:T(8,128)(2,1)} %copy-done.5, bf16[1024,2048]{1,0:T(8,128)(2,1)} %get-tuple-element.165.refs_2_, bf16[1024,2048]{1,0:T(8,128)(2,1)} %get-tuple-element.166.refs_3_, ...), custom_call_target="tpu_custom_call" | custom-call | flops 20000000000 | tf_op jit(solution)/shard_map/pallas_call | solution.py:573
  371.5 14.5 %shard_map.235 = (bf16[512,768]{1,0:T(8,128)(2,1)}, f32[512,768]{1,0:T(8,128)}, f32[512,12]{1,0:T(8,128)}, bf16[512,768]{1,0:T(8,128)(2,1)}, f32[768,768]{1,0:T(...) custom-call(bf16[8,2,128,768]{3,2,1,0:T(8,128)(2,1)} %copy-done.2, f32[512,768]{1,0:T(8,128)} %get-tuple-element.143.refs_1_, ...), custom_call_target="tpu_custom_call" | custom-call | flops 1000000000 | tf_op jit(solution)/shard_map/pallas_call | solution.py:312
  391.9 13.2 %collective-permute-done.30 = bf16[256,768]{1,0:T(8,128)(2,1)S(1)} collective-permute-done((bf16[256,768]{1,0:T(8,128)(2,1)}, bf16[256,768]{1,0:T(8,128)(2,1)S(1)}, u32[]{:S(2)}, u32[]{:S(2)}) %collective-permute-start.30) | collective-permute-done | bytes 393248 | tf_op jit(solution)/shard_map/ppermute | solution.py:739
  416.0 18.0 %shard_map.240 = (f32[512,768]{1,0:T(8,128)}, bf16[512,2304]{1,0:T(8,128)(2,1)}, bf16[512,768]{1,0:T(8,128)(2,1)}, f32[8,768]{1,0:T(8,128)}) custom-call(bf16[512,2304]{1,0:T(8,128)(2,1)} %get-tuple-element.157.qkv, bf16[512,768]{1,0:T(8,128)(2,1)} %get-tuple-element.158.agrad, f32[16,512]{1,0:T(8,128)} %get-tuple-element.159.lse, s32[1024,1]{1,0:T(8,128)} %copy.175.seg_col, ...), custom_call_target="tpu_custom_call" | custom-call | flops 1000000000 | tf_op jit(solution)/shard_map/pallas_call | solution.py:401
  438.4 15.3 %shard_map.237 = (bf16[512,768]{1,0:T(8,128)(2,1)}, f32[512,768]{1,0:T(8,128)}, f32[512,12]{1,0:T(8,128)}, bf16[512,768]{1,0:T(8,128)(2,1)}, f32[768,768]{1,0:T(...) custom-call(bf16[8,2,128,768]{3,2,1,0:T(8,128)(2,1)} %copy-done.1, f32[512,768]{1,0:T(8,128)} %get-tuple-element.150.resid, ...), custom_call_target="tpu_custom_call" | custom-call | flops 1000000000 | tf_op jit(solution)/shard_map/pallas_call | solution.py:312
  456.3 18.3 %shard_map.241 = (f32[512,768]{1,0:T(8,128)}, bf16[512,2304]{1,0:T(8,128)(2,1)}, bf16[512,768]{1,0:T(8,128)(2,1)}, f32[8,768]{1,0:T(8,128)}) custom-call(bf16[512,2304]{1,0:T(8,128)(2,1)} %get-tuple-element.172.qkv, bf16[512,768]{1,0:T(8,128)(2,1)} %get-tuple-element.173.agrad, f32[16,512]{1,0:T(8,128)} %get-tuple-element.174.lse, s32[1024,1]{1,0:T(8,128)} %copy.175.seg_col, ...), custom_call_target="tpu_custom_call" | custom-call | flops 1000000000 | tf_op jit(solution)/shard_map/pallas_call | solution.py:401
  476.4 8.0 %shard_map.242 = bf16[768,2304]{1,0:T(8,128)(2,1)} custom-call(bf16[512,768]{1,0:T(8,128)(2,1)} %get-tuple-element.179.refs_0_, bf16[512,768]{1,0:T(8,128)(2,1)} %get-tuple-element.180.refs_1_, bf16[512,2304]{1,0:T(8,128)(2,1)} %get-tuple-element.181.refs_2_, bf16[512,2304]{1,0:T(8,128)(2,1)} %get-tuple-element.182.refs_3_), custom_call_target="tpu_custom_call" | custom-call | flops 1000000000 | tf_op jit(solution)/shard_map/pallas_call | solution.py:435
  484.4 6.7 %concatenate.72 = bf16[768,2560]{1,0:T(8,128)(2,1)} concatenate(bf16[768,2304]{1,0:T(8,128)(2,1)} %shard_map.242, bf16[768,16]{1,0:T(8,128)(2,1)S(1)} %slice.146, bf16[768,4]{1,0:T(8,128)(2,1)S(1)} %bitcast.200, bf16[768,236]{1,0:T(8,128)(2,1)S(1)} %broadcast_in_dim.55), dimensions={1} | concatenate | bytes 7864320 | tf_op jit(solution)/shard_map/concatenate | solution.py:846
  548.5 5.9 %collective-permute-done.40 = bf16[48,1280]{1,0:T(8,128)(2,1)S(1)} collective-permute-done((bf16[48,1280]{1,0:T(8,128)(2,1)S(1)}, bf16[48,1280]{1,0:T(8,128)(2,1)S(1)}, u32[]{:S(2)}, u32[]{:S(2)}) %collective-permute-start.40) | collective-permute-done | bytes 122912 | tf_op jit(solution)/shard_map/ppermute | solution.py:652
  555.1 6.3 %collective-permute-start.53 = (bf16[48,768]{1,0:T(8,128)(2,1)S(1)}, bf16[48,768]{1,0:T(8,128)(2,1)S(1)}, u32[]{:S(2)}, u32[]{:S(2)}) collective-permute-start(bf16[48,768]{1,0:T(8,128)(2,1)S(1)} %maximum_select_fusion.3), channel_id=1, source_target_pairs={{0,1},{1,0},{2,3},{3,2},{4,5},{5,4},{6,7},{7,6},{8,9},{9,8},{10,11... | collective-permute-start | bytes 221192 | tf_op jit(solution)/shard_map/ppermute | solution.py:648
  (290 shorter events, 219.4 us)
Async XLA Ops:
  27.0 39.9 %collective-permute-start.12 = (bf16[96,4096]{1,0:T(8,128)(2,1)S(1)}, bf16[96,4096]{1,0:T(8,128)(2,1)}, u32[]{:S(2)}, u32[]{:S(2)}) collective-permute-start(bf16[96,4096]{1,0:T(8,128)(2,1)S(1)} %dynamic-slice_bitcast_fusion.10), channel_id=1, source_target_pairs={{0,16},{1,24},{4,17},{5,25},{8,20},{9,28},{12,21},{13,29},{16,0},{... | collective-permute-start | bytes 2359304 | tf_op jit(solution)/shard_map/ppermute | solution.py:661
  74.2 31.0 %collective-permute-start.13 = (bf16[256,768]{1,0:T(8,128)(2,1)S(1)}, bf16[256,768]{1,0:T(8,128)(2,1)S(1)}, u32[]{:S(2)}, u32[]{:S(2)}) collective-permute-start(bf16[256,768]{1,0:T(8,128)(2,1)S(1)} %get-tuple-element.279), channel_id=1, source_target_pairs={{0,16},{1,24},{4,17},{5,25},{8,20},{9,28},{12,21},{13,29},{16,0},{... | collective-permute-start | bytes 1179656 | tf_op jit(solution)/shard_map/ppermute | solution.py:661
  75.3 29.9 %collective-permute-start.14 = (bf16[256,768]{1,0:T(8,128)(2,1)S(1)}, bf16[256,768]{1,0:T(8,128)(2,1)S(1)}, u32[]{:S(2)}, u32[]{:S(2)}) collective-permute-start(bf16[256,768]{1,0:T(8,128)(2,1)S(1)} %get-tuple-element.278), channel_id=1, source_target_pairs={{0,20},{1,28},{4,21},{5,29},{8,16},{9,24},{12,17},{13,25},{16,4},{... | collective-permute-start | bytes 1179656 | tf_op jit(solution)/shard_map/ppermute | solution.py:661
  98.3 77.6 %all-to-all-start = ((bf16[8,2,128,768]{3,2,1,0:T(8,128)(2,1)}), bf16[8,2,128,768]{3,2,1,0:T(8,128)(2,1)}, u32[]{:S(2)}, u32[]{:S(2)}) async-start(bf16[8,2,128,768]{3,2,1,0:T(8,128)(2,1)} %get-tuple-element.126), calls=%async_computation | async-start | bytes 6291456 | tf_op jit(solution)/shard_map/all_to_all | solution.py:818
  102.8 86.3 %collective-permute-start.22 = (bf16[96,4096]{1,0:T(8,128)(2,1)}, bf16[96,4096]{1,0:T(8,128)(2,1)}, u32[]{:S(2)}, u32[]{:S(2)}) collective-permute-start(bf16[96,4096]{1,0:T(8,128)(2,1)} %collective-permute-done.12.refs_3_), channel_id=1, source_target_pairs={{0,1},{1,0},{2,3},{3,2},{4,5},{5,4},{6,7},{7,6},{8,9},{9,8},{10,11... | collective-permute-start | bytes 2359304 | tf_op jit(solution)/shard_map/ppermute | solution.py:648
  105.4 59.6 %collective-permute-start.15 = (bf16[96,4096]{1,0:T(8,128)(2,1)S(1)}, bf16[96,4096]{1,0:T(8,128)(2,1)S(1)}, u32[]{:S(2)}, u32[]{:S(2)}) collective-permute-start(bf16[96,4096]{1,0:T(8,128)(2,1)S(1)} %get-tuple-element.273), channel_id=1, source_target_pairs={{0,20},{1,28},{4,21},{5,29},{8,16},{9,24},{12,17},{13,25},{16,4},{... | collective-permute-start | bytes 2359304 | tf_op jit(solution)/shard_map/ppermute | solution.py:661
  109.1 65.6 %collective-permute-start.16 = (bf16[96,4096]{1,0:T(8,128)(2,1)S(1)}, bf16[96,4096]{1,0:T(8,128)(2,1)S(1)}, u32[]{:S(2)}, u32[]{:S(2)}) collective-permute-start(bf16[96,4096]{1,0:T(8,128)(2,1)S(1)} %get-tuple-element.272), channel_id=1, source_target_pairs={{0,0},{1,8},{4,1},{5,9},{8,4},{9,12},{12,5},{13,13},{16,16},{17,24... | collective-permute-start | bytes 2359304 | tf_op jit(solution)/shard_map/ppermute | solution.py:661
  175.9 97.2 %all-to-all-start.2 = ((bf16[8,2,128,768]{3,2,1,0:T(8,128)(2,1)}), bf16[8,2,128,768]{3,2,1,0:T(8,128)(2,1)S(1)}, u32[]{:S(2)}, u32[]{:S(2)}) async-start(bf16[8,2,128,768]{3,2,1,0:T(8,128)(2,1)} %get-tuple-element.148), calls=%async_computation.2 | async-start | bytes 6291456 | tf_op jit(solution)/shard_map/all_to_all | solution.py:818
  184.0 46.2 %collective-permute-start.18 = (bf16[256,768]{1,0:T(8,128)(2,1)S(1)}, bf16[256,768]{1,0:T(8,128)(2,1)}, u32[]{:S(2)}, u32[]{:S(2)}) collective-permute-start(bf16[256,768]{1,0:T(8,128)(2,1)S(1)} %get-tuple-element.277), channel_id=1, source_target_pairs={{0,0},{1,8},{4,1},{5,9},{8,4},{9,12},{12,5},{13,13},{16,16},{17,24... | collective-permute-start | bytes 1179656 | tf_op jit(solution)/shard_map/ppermute | solution.py:661
  187.9 46.6 %collective-permute-start.19 = (bf16[256,768]{1,0:T(8,128)(2,1)S(1)}, bf16[256,768]{1,0:T(8,128)(2,1)S(1)}, u32[]{:S(2)}, u32[]{:S(2)}) collective-permute-start(bf16[256,768]{1,0:T(8,128)(2,1)S(1)} %get-tuple-element.276), channel_id=1, source_target_pairs={{0,4},{1,12},{4,5},{5,13},{8,0},{9,8},{12,1},{13,9},{16,20},{17,28... | collective-permute-start | bytes 1179656 | tf_op jit(solution)/shard_map/ppermute | solution.py:661
  189.1 47.2 %collective-permute-start.20 = (bf16[96,4096]{1,0:T(8,128)(2,1)}, bf16[96,4096]{1,0:T(8,128)(2,1)}, u32[]{:S(2)}, u32[]{:S(2)}) collective-permute-start(bf16[96,4096]{1,0:T(8,128)(2,1)} %copy-done.24), channel_id=1, source_target_pairs={{0,1},{1,0},{2,3},{3,2},{4,5},{5,4},{6,7},{7,6},{8,9},{9,8},{10,11... | collective-permute-start | bytes 2359304 | tf_op jit(solution)/shard_map/ppermute | solution.py:648
  189.1 47.2 %collective-permute-start.23 = (bf16[96,4096]{1,0:T(8,128)(2,1)}, bf16[96,4096]{1,0:T(8,128)(2,1)}, u32[]{:S(2)}, u32[]{:S(2)}) collective-permute-start(bf16[96,4096]{1,0:T(8,128)(2,1)} %copy-done.23), channel_id=1, source_target_pairs={{0,1},{1,0},{2,3},{3,2},{4,5},{5,4},{6,7},{7,6},{8,9},{9,8},{10,11... | collective-permute-start | bytes 2359304 | tf_op jit(solution)/shard_map/ppermute | solution.py:648
  193.0 43.3 %collective-permute-start.21 = (bf16[96,4096]{1,0:T(8,128)(2,1)}, bf16[96,4096]{1,0:T(8,128)(2,1)}, u32[]{:S(2)}, u32[]{:S(2)}) collective-permute-start(bf16[96,4096]{1,0:T(8,128)(2,1)} %collective-permute-done.17.refs_2_), channel_id=1, source_target_pairs={{0,1},{1,0},{2,3},{3,2},{4,5},{5,4},{6,7},{7,6},{8,9},{9,8},{10,11... | collective-permute-start | bytes 2359304 | tf_op jit(solution)/shard_map/ppermute | solution.py:648
  274.8 54.5 %all-to-all-start.1 = ((bf16[8,2,128,768]{3,2,1,0:T(8,128)(2,1)}), bf16[8,2,128,768]{3,2,1,0:T(8,128)(2,1)S(1)}, u32[]{:S(2)}, u32[]{:S(2)}) async-start(bf16[8,2,128,768]{3,2,1,0:T(8,128)(2,1)} %get-tuple-element.142), calls=%async_computation.1 | async-start | bytes 6291456 | tf_op jit(solution)/shard_map/all_to_all | solution.py:820
  331.0 105.7 %all-to-all-start.3 = ((bf16[8,2,128,768]{3,2,1,0:T(8,128)(2,1)}), bf16[8,2,128,768]{3,2,1,0:T(8,128)(2,1)S(1)}, u32[]{:S(2)}, u32[]{:S(2)}) async-start(bf16[8,2,128,768]{3,2,1,0:T(8,128)(2,1)} %get-tuple-element.149), calls=%async_computation.3 | async-start | bytes 6291456 | tf_op jit(solution)/shard_map/all_to_all | solution.py:820
  363.1 41.9 %collective-permute-start.30 = (bf16[256,768]{1,0:T(8,128)(2,1)}, bf16[256,768]{1,0:T(8,128)(2,1)S(1)}, u32[]{:S(2)}, u32[]{:S(2)}) collective-permute-start(bf16[256,768]{1,0:T(8,128)(2,1)} %get-tuple-element.271), channel_id=1, source_target_pairs={{0,0},{8,1},{1,4},{9,5},{4,8},{12,9},{5,12},{13,13},{16,16},{24,17... | collective-permute-start | bytes 1179656 | tf_op jit(solution)/shard_map/ppermute | solution.py:739
  366.7 38.4 %collective-permute-start.31 = (bf16[256,768]{1,0:T(8,128)(2,1)}, bf16[256,768]{1,0:T(8,128)(2,1)}, u32[]{:S(2)}, u32[]{:S(2)}) collective-permute-start(bf16[256,768]{1,0:T(8,128)(2,1)} %get-tuple-element.270), channel_id=1, source_target_pairs={{4,0},{12,1},{5,4},{13,5},{0,8},{8,9},{1,12},{9,13},{20,16},{28,17... | collective-permute-start | bytes 1179656 | tf_op jit(solution)/shard_map/ppermute | solution.py:739
  368.3 36.8 %collective-permute-start.32 = (bf16[256,768]{1,0:T(8,128)(2,1)}, bf16[256,768]{1,0:T(8,128)(2,1)}, u32[]{:S(2)}, u32[]{:S(2)}) collective-permute-start(bf16[256,768]{1,0:T(8,128)(2,1)} %get-tuple-element.269), channel_id=1, source_target_pairs={{16,0},{24,1},{17,4},{25,5},{20,8},{28,9},{21,12},{29,13},{0,16},{... | collective-permute-start | bytes 1179656 | tf_op jit(solution)/shard_map/ppermute | solution.py:739
  368.3 36.8 %collective-permute-start.33 = (bf16[256,768]{1,0:T(8,128)(2,1)}, bf16[256,768]{1,0:T(8,128)(2,1)}, u32[]{:S(2)}, u32[]{:S(2)}) collective-permute-start(bf16[256,768]{1,0:T(8,128)(2,1)} %get-tuple-element.268), channel_id=1, source_target_pairs={{20,0},{28,1},{21,4},{29,5},{16,8},{24,9},{17,12},{25,13},{4,16},{... | collective-permute-start | bytes 1179656 | tf_op jit(solution)/shard_map/ppermute | solution.py:739
  406.8 88.8 %collective-permute-start.54 = (bf16[2,96,2048]{2,1,0:T(8,128)(2,1)}, bf16[2,96,2048]{2,1,0:T(8,128)(2,1)}, u32[]{:S(2)}, u32[]{:S(2)}) collective-permute-start(bf16[2,96,2048]{2,1,0:T(8,128)(2,1)} %get-tuple-element.263), channel_id=1, source_target_pairs={{0,0},{8,1},{1,4},{9,5},{4,8},{12,9},{5,12},{13,13},{16,16},{24,17... | collective-permute-start | bytes 2359304 | tf_op jit(solution)/shard_map/ppermute | solution.py:739
  409.5 89.0 %collective-permute-start.55 = (bf16[2,96,2048]{2,1,0:T(8,128)(2,1)}, bf16[2,96,2048]{2,1,0:T(8,128)(2,1)}, u32[]{:S(2)}, u32[]{:S(2)}) collective-permute-start(bf16[2,96,2048]{2,1,0:T(8,128)(2,1)} %get-tuple-element.262), channel_id=1, source_target_pairs={{4,0},{12,1},{5,4},{13,5},{0,8},{8,9},{1,12},{9,13},{20,16},{28,17... | collective-permute-start | bytes 2359304 | tf_op jit(solution)/shard_map/ppermute | solution.py:739
  410.5 88.0 %collective-permute-start.56 = (bf16[2,96,2048]{2,1,0:T(8,128)(2,1)}, bf16[2,96,2048]{2,1,0:T(8,128)(2,1)}, u32[]{:S(2)}, u32[]{:S(2)}) collective-permute-start(bf16[2,96,2048]{2,1,0:T(8,128)(2,1)} %get-tuple-element.261), channel_id=1, source_target_pairs={{16,0},{24,1},{17,4},{25,5},{20,8},{28,9},{21,12},{29,13},{0,16},{... | collective-permute-start | bytes 2359304 | tf_op jit(solution)/shard_map/ppermute | solution.py:739
  415.2 83.3 %collective-permute-start.57 = (bf16[2,96,2048]{2,1,0:T(8,128)(2,1)}, bf16[2,96,2048]{2,1,0:T(8,128)(2,1)}, u32[]{:S(2)}, u32[]{:S(2)}) collective-permute-start(bf16[2,96,2048]{2,1,0:T(8,128)(2,1)} %get-tuple-element.260), channel_id=1, source_target_pairs={{20,0},{28,1},{21,4},{29,5},{16,8},{24,9},{17,12},{25,13},{4,16},{... | collective-permute-start | bytes 2359304 | tf_op jit(solution)/shard_map/ppermute | solution.py:739
  456.3 42.3 %collective-permute-start.44 = (bf16[4,2,48,768]{3,2,1,0:T(8,128)(2,1)}, bf16[4,2,48,768]{3,2,1,0:T(8,128)(2,1)}, u32[]{:S(2)}, u32[]{:S(2)}) collective-permute-start(bf16[4,2,48,768]{3,2,1,0:T(8,128)(2,1)} %dynamic-slice_bitcast_fusion.11), channel_id=1, source_target_pairs={{0,1},{1,0},{2,3},{3,2},{4,5},{5,4},{6,7},{7,6},{8,9},{9,8},{10,11... | collective-permute-start | bytes 1769480 | tf_op jit(solution)/shard_map/ppermute | solution.py:648
  (71 other events, 909.1 us)

commit v3 on v2

--- a/solution.py
+++ b/solution.py
@@ -52,7 +52,6 @@
 
 
 HALF = SEQ // 2
-FORWARD_LASTS = 100
 PAIRS = HEADS // 2
 
 
@@ -170,7 +169,7 @@
 
 
 def lasting(microseconds):
-    return pl.CostEstimate(flops=microseconds * 10**9, bytes_accessed=0, transcendentals=0)
+    return pl.CostEstimate(flops=microseconds * 10**9 + 1, bytes_accessed=0, transcendentals=0)
 
 
 def kernel_params():
@@ -204,7 +203,7 @@
             pltpu.VMEM((SEQ, D), BF), pltpu.VMEM((SEQ, 128), F32),
         ],
         compiler_params=kernel_params(),
-        cost_estimate=lasting(FORWARD_LASTS),
+        cost_estimate=lasting(100),
     )(
         t["tokens"], t["cotangent"], t["prev"], t["routes"], t["slot_row"], t["seg_col"], t["seg_row"],
         t["cos"], t["sin"], packed, packed, packed, vecs,
@@ -322,7 +321,7 @@
             jax.ShapeDtypeStruct((SEQ, CHOICES), F32), jax.ShapeDtypeStruct((SEQ, D), BF),
         ] + sums,
         compiler_params=kernel_params(),
-        cost_estimate=lasting(1),
+        cost_estimate=lasting(0),
     )(back, resid, t["cotangent"], aux, t["slots"], t["routes"], att, packed, packed, vecs, *given)
 
 
@@ -413,35 +412,69 @@
         ],
         scratch_shapes=[pltpu.VMEM((SEQ, SEQ), F32)],
         compiler_params=kernel_params(),
-        cost_estimate=lasting(1),
+        cost_estimate=lasting(0),
     )(
         qkv, agrad, lse, t["seg_col"], t["seg_row"], t["cos"], t["sin"], packed, t["tokens"], vecs, rgrad
     )
 
 
-def qkv_wgrad_body(parts, *refs):
-    acts, grads, out, turned = refs[:parts], refs[parts : 2 * parts], refs[2 * parts], refs[2 * parts + 1]
-
-    @pl.when(pl.program_id(0) == 0)
+def mixer_wgrad_body(parts, groups, *refs):
+    core, acts, grads, gains = refs[0], refs[1 : 1 + parts], refs[1 + parts : 1 + 2 * parts], refs[1 + 2 * parts : 1 + 3 * parts]
+    small, rows, give, keep, turned, last = refs[1 + 3 * parts :]
+    step, half = pl.program_id(0), D // 2
+    chunk = half // groups
+
+    def scattered(store, across, value):
+        for group in range(groups):
+            for c in range(2):
+                kept = (core[0] == c).astype(jnp.int32)
+                at = pl.ds(pl.multiple_of(kept * half + group * chunk, 16), chunk)
+                first = (2 * group + c) * chunk
+                store[at, across] = value[first : first + chunk, :]
+
+    @pl.when(step == 0)
     def _():
         for i in range(parts):
-            turned[:, i * SEQ : (i + 1) * SEQ] = acts[i][...].T
-
-    out[...] = dot(turned[...], jnp.concatenate([v[...] for v in grads], axis=0)).astype(BF)
-
-
-def qkv_wgrad(acts, grads):
+            scattered(turned, slice(i * SEQ, (i + 1) * SEQ), acts[i][...].T)
+
+    @pl.when(step < 9)
+    def _():
+        made = dot(turned[...], jnp.concatenate([v[...] for v in grads], axis=0)).astype(BF)
+        give[...] = made[:half, :]
+        keep[...] = made[half:, :]
+
+    @pl.when(step == 9)
+    def _():
+        gain_one = sum(v[0:1, :] for v in gains)
+        line = lax.broadcasted_iota(jnp.int32, (128, D), 0)
+        stacked = 0.0
+        for i, row in enumerate((rows[0:1, :], rows[1:2, :], gain_one, rows[2:3, :])):
+            stacked += jnp.where(line == 16 + i, row, 0.0)
+        scattered(last, slice(0, 128), (small[...] + stacked.T).astype(BF))
+        give[:, :128] = last[:half, :]
+        keep[:, :128] = last[half:, :]
+        give[:, 128:] = jnp.zeros((half, 128), BF)
+        keep[:, 128:] = jnp.zeros((half, 128), BF)
+
+
+def mixer_wgrad(acts, grads, gains, small, rows, groups, core):
     parts = len(acts)
+    half = pl.BlockSpec((D // 2, 256), lambda i: (0, i))
+    out = jax.ShapeDtypeStruct((D // 2, 3 * D + 256), BF)
     return pl.pallas_call(
-        functools.partial(qkv_wgrad_body, parts),
-        grid=(3,),
-        in_specs=[fixed((SEQ, D))] * parts + [pl.BlockSpec((SEQ, D), lambda i: (0, i))] * parts,
-        out_specs=pl.BlockSpec((D, D), lambda i: (0, i)),
-        out_shape=jax.ShapeDtypeStruct((D, 3 * D), BF),
-        scratch_shapes=[pltpu.VMEM((D, parts * SEQ), BF)],
+        functools.partial(mixer_wgrad_body, parts, groups),
+        grid=(10,),
+        in_specs=[pl.BlockSpec(memory_space=pltpu.SMEM)]
+        + [fixed((SEQ, D))] * parts
+        + [pl.BlockSpec((SEQ, 256), lambda i: (0, jnp.minimum(i, 8)))] * parts
+        + [fixed((8, D))] * parts
+        + [fixed((D, 128)), fixed((8, D))],
+        out_specs=[half, half],
+        out_shape=[out, out],
+        scratch_shapes=[pltpu.VMEM((D, parts * SEQ), BF), pltpu.VMEM((D, 128), BF)],
         compiler_params=kernel_params(),
-        cost_estimate=lasting(1),
-    )(*acts, *grads)
+        cost_estimate=lasting(0),
+    )(jnp.stack([core]).astype(jnp.int32), *acts, *grads, *gains, small, rows)
 
 
 def tables(tokens, cotangent, prev_logits, routes, capacity, segments, positions):
@@ -579,20 +612,21 @@
         out_shape=jax.ShapeDtypeStruct((2, D, FF), BF),
         scratch_shapes=[pltpu.VMEM((D, parts * n * CAP), BF)],
         compiler_params=kernel_params(),
-        cost_estimate=lasting(20),
+        cost_estimate=lasting(0),
     )(*received, *dg, *du)
 
 
 def place_body(spots, count, *refs):
     offsets, blocks, outs, sems = refs[0], refs[1 : 1 + count], refs[1 + count : -1], refs[-1]
     copies = []
-    for i, (block, first, rows, out, column) in enumerate(spots):
-        width = blocks[block].shape[1]
-        start = pl.multiple_of(offsets[2 * i], 16)
-        across = pl.ds(pl.multiple_of(offsets[2 * i + 1], 128), width) if column else pl.ds(0, width)
+    for i, (block, row, rows, column, columns, out) in enumerate(spots):
+        down = pl.ds(pl.multiple_of(offsets[2 * i], 16), rows)
+        across = pl.ds(pl.multiple_of(offsets[2 * i + 1], 128), columns)
         copies.append(
             pltpu.make_async_copy(
-                blocks[block].at[pl.ds(first, rows), :], outs[out].at[pl.ds(start, rows), across], sems.at[i]
+                blocks[block].at[pl.ds(row, rows), pl.ds(column, columns)],
+                outs[out].at[down, across],
+                sems.at[i],
             )
         )
     for copy in copies:
@@ -602,7 +636,6 @@
 
 
 def place(blocks, spots, offsets, shapes):
-    size = sum(math.prod(v) for v in shapes) * 4
     anywhere = pl.BlockSpec(memory_space=pl.ANY)
     return pl.pallas_call(
         functools.partial(place_body, spots, len(blocks)),
@@ -611,7 +644,7 @@
         out_shape=[jax.ShapeDtypeStruct(v, BF) for v in shapes],
         scratch_shapes=[pltpu.SemaphoreType.DMA((len(spots),))],
         compiler_params=pltpu.CompilerParams(vmem_limit_bytes=VMEM_MOST),
-        cost_estimate=lasting(size // 2**20),
+        cost_estimate=lasting(0),
     )(jnp.stack(offsets).astype(jnp.int32), *blocks)
 
 
@@ -630,6 +663,7 @@
     rows = ("side", "low", "inner")
     route_axes = ("half", "low", "inner", "core")
     near = 896
+    cut = 3072
 
     def __init__(self, mesh):
         self.mesh = Mesh(mesh.devices.reshape(2, 2, 2, 2, 2), self.axes)
@@ -656,8 +690,28 @@
         z = lax.axis_index("half") * 2 + lax.axis_index("low")
         return z, lax.axis_index("inner"), lax.axis_index("side"), lax.axis_index("core")
 
-    def send(self, weights, which, turn):
-        mine = pick(weights[which], (self.spot()[0] ^ turn) & 1)
+    @staticmethod
+    def joined(gate_up, down):
+        high, edge = gate_up.shape[1], D - 256
+        tail = down[:, 2 * high :]
+        half = tail.shape[1] // 2
+        under = jnp.concatenate([tail[:, :half, edge:], tail[:, half:, edge:]], axis=2)
+        last = jnp.concatenate([tail[:, :, :edge], under], axis=1)
+        cut = Paired.cut
+        rest = jnp.concatenate([gate_up[:, :, cut:], down[:, :high], down[:, high : 2 * high], last], axis=2)
+        return gate_up[:, :, :cut], rest
+
+    @staticmethod
+    def rects(high, deep):
+        half, edge, at = deep // 2 - high, D - 256, 2 * FF - Paired.cut
+        yield 0, high, at, D, 0, 0
+        yield 0, high, at + D, D, high, 0
+        yield 0, 2 * half, at + 2 * D, edge, 2 * high, 0
+        yield 2 * half, half, at + 2 * D, 256, 2 * high, edge
+        yield 2 * half, half, at + 2 * D + 256, 256, 2 * high + half, edge
+
+    def send(self, joined, turn, part):
+        mine = pick(joined[part], (self.spot()[0] ^ turn) & 1)
         return lax.ppermute(mine, self.route_axes, self.routes[turn])
 
     def gather_shared(self, shard, weights, early):
@@ -666,8 +720,8 @@
         rows, width = rows // 2, width // 2
         mine = lax.dynamic_slice(shard, (c * rows, x * width), (rows, width))
         stack = jnp.concatenate([mine] + [self.along(mine, turn) for turn in (1, 2, 3)])
-        stack, weights, early = lax.optimization_barrier((stack, weights, early))
-        sent = {(0, 2): self.send(weights, 0, 2)}
+        stack, joined, early = lax.optimization_barrier((stack, self.joined(*weights), early))
+        sent = {(2, 0): self.send(joined, 2, 0)}
         over_y, over_x = self.swap(stack, "inner"), self.swap(stack, "side")
         far = self.swap(over_y[:, : self.near], "side"), self.swap(over_x[:, self.near :], "inner")
         blocks = [stack, over_y, over_x, *far]
@@ -676,31 +730,47 @@
         for i, (dy, dx, column) in enumerate(flips + flips):
             core = c if i < len(flips) else 1 - c
             for turn in range(4):
-                spots.append((i, turn * rows, rows, 0, True))
+                spots.append((i, turn * rows, rows, 0, blocks[i % len(flips)].shape[1], 0))
                 offsets += [((z ^ turn) * 2 + (y ^ dy)) * 2 * rows + core * rows, (x ^ dx) * width + column]
         blocks += [self.swap(v) for v in blocks]
-        blocks, weights, sent = lax.optimization_barrier((blocks, weights, sent))
+        blocks, joined, sent = lax.optimization_barrier((blocks, joined, sent))
         [full] = place(blocks, spots, offsets, [(16 * rows, 2 * width)])
-        return full, early, (weights, sent)
+        return full, early, (joined, sent)
 
     def gather_more(self, held, value, names):
-        weights, sent = held
-        more = [self.send(weights, *v) for v in names]
-        value, weights, more = lax.optimization_barrier((value, weights, more))
-        return (weights, {**sent, **dict(zip(names, more))}), value
-
-    def reduce_shared(self, total):
+        joined, sent = held
+        more = {v: self.send(joined, *v) for v in names}
+        value, joined, sent = lax.optimization_barrier((value, joined, {**sent, **more}))
+        return (joined, sent), value
+
+    def split(self):
+        return 8, lax.axis_index("core")
+
+    def halves(self, total):
+        c = lax.axis_index("core")
+        total = total.reshape(8, 2, total.shape[0] // 16, total.shape[1])
+        return pick(total, 1 - c, 1), pick(total, c, 1)
+
+    def reduce_first(self, give, keep):
         z, y, x, c = self.spot()
-        rows, width = total.shape[0] // 16, total.shape[1] // 2
+        width = give.shape[-1] // 2
         near = (width // 128 + 1) // 2 * 128
-        total = total.reshape(4, 2, 2, rows, 2 * width)
-        total = added(pick(total, c, 2), self.swap(pick(total, 1 - c, 2)))
-        parts = total.reshape(4, 2, rows, 2, width)
-        one, two = parts[..., :near], parts[..., near:]
-        one = added(pick(one, x, 3), self.swap(pick(one, 1 - x, 3), "side"))
+        parts = added(keep, self.swap(give)).reshape(4, 2, -1, 2 * width)
+
+        def columns(value, first, count):
+            return lax.dynamic_slice_in_dim(value, first, count, value.ndim - 1)
+
+        one = added(columns(parts, x * width, near), self.swap(columns(parts, (1 - x) * width, near), "side"))
+        two = jnp.concatenate([parts[..., near:width], parts[..., width + near :]], axis=3)
         two = added(pick(two, y, 1), self.swap(pick(two, 1 - y, 1), "inner"))
+        return one, two
+
+    def reduce_last(self, one, two):
+        z, y, x, c = self.spot()
+        rest = two.shape[2] // 2
         one = added(pick(one, y, 1), self.swap(pick(one, 1 - y, 1), "inner"))
-        two = added(pick(two, x, 2), self.swap(pick(two, 1 - x, 2), "side"))
+        near = lax.dynamic_slice_in_dim(two, x * rest, rest, 2)
+        two = added(near, self.swap(lax.dynamic_slice_in_dim(two, (1 - x) * rest, rest, 2), "side"))
         both = jnp.concatenate([one, two], axis=2)
         mine = added(pick(both, z), *[self.along(pick(both, z ^ turn), turn) for turn in (1, 2, 3)])
         other = self.swap(mine, "side")
@@ -709,21 +779,22 @@
         both = jnp.where(c == 0, jnp.concatenate([line, other]), jnp.concatenate([other, line]))
         return both.astype(F32)
 
-    def gather_expert(self, held):
-        weights, sent = held
+    def gather_expert(self, held, shapes):
+        sent = held[1]
         c = lax.axis_index("core")
         here = lax.axis_index("half") * 2 + lax.axis_index("inner")
-        names = [(which, turn) for which in range(2) for turn in range(4)]
-        own = [sent[v] if v in sent else self.send(weights, *v) for v in names]
+        own = [sent[turn, part] for turn in range(4) for part in range(2)]
         blocks = own + [self.swap(v) for v in own]
-        spots, offsets = [], []
-        for i, block in enumerate(blocks):
-            which, turn = i % len(own) // 4, i % 4
-            rows = block.shape[0]
-            core = c if i < len(own) else 1 - c
-            spots.append((i, 0, rows, which, False))
-            offsets += [((here ^ turn) * 2 + core) * rows, jnp.int32(0)]
-        return place(blocks, spots, offsets, [(8 * w.shape[1], w.shape[2]) for w in weights])
+        high, deep = shapes[0][1], shapes[1][1]
+        spots, offsets, zero = [], [], jnp.int32(0)
+        for i in range(0, 16, 2):
+            shard = (here ^ (i // 2 % 4)) * 2 + (c if i < 8 else 1 - c)
+            spots += [(i, 0, high, 0, self.cut, 0), (i + 1, 0, high, 0, 2 * FF - self.cut, 0)]
+            offsets += [shard * high, zero, shard * high, zero + self.cut]
+            for row, rows, column, columns, to_row, to_column in self.rects(high, deep):
+                spots.append((i + 1, row, rows, column, columns, 1))
+                offsets += [shard * deep + to_row, zero + to_column]
+        return place(blocks, spots, offsets, [(8 * high, 2 * FF), (8 * deep, D)])
 
     def scatter_start(self, grad, axis):
         c = lax.axis_index("core")
@@ -762,11 +833,20 @@
     def gather_more(self, held, value, names):
         return held, value
 
-    def reduce_shared(self, total):
+    def split(self):
+        return 1, jnp.int32(1)
+
+    def halves(self, total):
+        return jnp.split(total, 2)
+
+    def reduce_first(self, give, keep):
+        return jnp.concatenate([give, keep]), None
+
+    def reduce_last(self, total, _):
         total = lax.psum_scatter(total, self.axes, scatter_dimension=0, tiled=True)
         return lax.all_gather(total, self.expert, axis=0, tiled=True).astype(F32)
 
-    def gather_expert(self, weights):
+    def gather_expert(self, weights, shapes):
         full = []
         for weight in weights:
             own = lax.all_to_all(weight, "inner", 0, 0, tiled=True)
@@ -807,49 +887,57 @@
         columns = packed[:, 4 * D + 16 : 4 * D + 20].astype(F32).T
         vecs = jnp.concatenate([columns[2:], columns[:2], jnp.zeros((4, D), F32)])
         parts = tokens.shape[0] // SEQ
-        kept, shared = [], packed
+        kept, sends, shared = [], [], packed
         for i in range(parts):
             if i == 1:
-                held, shared = plan.gather_more(held, packed, ((1, 2), (1, 3)))
-            kept.append(forward_part(i, t, shared, vecs))
-        sends = [k[0] for k in kept]
-        held, sends[-1] = plan.gather_more(held, sends[-1], ((0, 3), (0, 0)))
-        gate_up_full, down_full = plan.gather_expert(held)
+                held, (shared, kept[0][5]) = plan.gather_more(held, (packed, kept[0][5]), ((2, 1), (0, 0), (0, 1), (1, 0)))
+            kept.append(list(forward_part(i, t, shared, vecs)))
+            sends.append(kept[i][0])
+        held, sends[-1] = plan.gather_more(held, sends[-1], ((3, 0), (3, 1), (1, 1)))
+        gate_up_full, down_full = plan.gather_expert(held, (w_gate_up.shape, w_down.shape))
         received = [lax.all_to_all(v, plan.rows, 0, 0, tiled=True) for v in sends]
         made = [expert_rows(r, gate_up_full, down_full) for r in received]
-        returned = [lax.all_to_all(m[3], plan.rows, 0, 0, tiled=True) for m in made]
         hid, dg, du = [[m[i] for m in made] for i in range(3)]
-        started = plan.scatter_start(down_wgrad(received, hid), 0)
-        dg, started = lax.optimization_barrier((dg, started))
-        down_got = plan.scatter_send(started, 0)
-        started = plan.scatter_start(gate_up_wgrad(received, dg, du), 1)
-        firsts, lasts, sums = [], [], None
+        backs = [m[3] for m in made]
+        down_w = down_wgrad(received, hid)
+        backs[-1], down_w = lax.optimization_barrier((backs[-1], down_w))
+        returned = [lax.all_to_all(v, plan.rows, 0, 0, tiled=True) for v in backs]
+        dg, down_w = lax.optimization_barrier((dg, down_w))
+        gate_up_w = gate_up_wgrad(received, dg, du)
+        returned[0], gate_up_w = lax.optimization_barrier((returned[0], gate_up_w))
+        down_got = plan.scatter_send(plan.scatter_start(down_w, 0), 0)
+        gate_up_sums = plan.scatter_start(gate_up_w, 1)
+        firsts, sums = [], None
         for i in range(parts):
             *first, out_w, small_w, rows_w = combine_part(i, returned[i], kept[i], t, packed, vecs, sums)
             sums = (out_w, small_w, rows_w)
-            if i == 0:
-                first[1], started, down_got = lax.optimization_barrier((first[1], started, down_got))
-                down_total = plan.scatter_end(down_got, 0)
-                gate_up_got = plan.scatter_send(started, 1)
             firsts.append(first)
+        out_halves = plan.halves(sums[0].astype(BF))
+        held = (out_halves, firsts[0][1], gate_up_sums, down_got)
+        out_halves, firsts[0][1], gate_up_sums, down_got = lax.optimization_barrier(held)
+        gate_up_got = plan.scatter_send(gate_up_sums, 1)
+        down_total = plan.scatter_end(down_got, 0)
+        out_summed = plan.reduce_first(*out_halves)
+        lasts = []
+        for i, first in enumerate(firsts):
+            if i == parts - 1:
+                out_summed, first[1] = lax.optimization_barrier((out_summed, first[1]))
+                out_total = plan.reduce_last(*out_summed)
             lasts.append(attention_back(i, kept[i], first[1], first[3], t, packed, vecs))
-        out_w = plan.reduce_shared(sums[0].astype(BF))
-        qkv_w = qkv_wgrad([v[2] for v in lasts], [v[1] for v in lasts])
-        gate_up_got, _ = lax.optimization_barrier((gate_up_got, qkv_w))
+        acts = [v[2] for v in lasts]
+        halves = mixer_wgrad(
+            acts, [v[1] for v in lasts], [v[3] for v in lasts], sums[1], sums[2], *plan.split()
+        )
+        halves, gate_up_got = lax.optimization_barrier((halves, gate_up_got))
+        total = plan.reduce_last(*plan.reduce_first(*halves))
         gate_up_total = plan.scatter_end(gate_up_got, 1)
         gate_up_total = jnp.concatenate([gate_up_total[:, 0], gate_up_total[:, 1]], axis=2)
-        gain_one_grad = sum(v[3][0] for v in lasts)
-        row_sums = jnp.concatenate([sums[2][:2], gain_one_grad[None], sums[2][2:3]])
-        small_sum = jnp.concatenate(
-            [sums[1][:, :16], row_sums.T, jnp.zeros((D, 256 - 20), F32)], axis=1
-        )
-        total = plan.reduce_shared(jnp.concatenate([qkv_w, small_sum.astype(BF)], axis=1))
         return (
             jnp.concatenate([v[0] for v in firsts]),
             jnp.concatenate([v[0] for v in lasts]),
             jnp.concatenate([v[2] for v in firsts]),
             total[:, : 3 * D],
-            out_w,
+            out_total,
             total[:, 3 * D : 3 * D + 16],
             total[:, 3 * D + 16 : 3 * D + 18],
             total[:, 3 * D + 18],

time: 581 us -> 543 us (0.935)
  local copies, waits for them, and re-layouts: 56.6 us -> 40.8 us
  starting transfers between devices: 142 us -> 127 us
  other arithmetic: 38.8 us -> 28.1 us
    ppermute x33, starting transfers between devices: 72.6 us -> 48.8 us  [swap(): return lax.ppermute(value, axis, [(0, 1), (1, 0)])]
    ppermute x8, waiting for transfers between devices: 13.2 us -> 0.02 us  [scatter_send(): lax.ppermute(pick(parts, here ^ turn, axis), self.route_axes, back)]
    ppermute x33, waiting for transfers between devices: 34 us -> 41.3 us  [swap(): return lax.ppermute(value, axis, [(0, 1), (1, 0)])]
    concatenate x2 -> x0, local copies, waits for them, and re-layouts: 6.92 us -> none  [the longest x1 6.74 us: on_device(): jnp.concatenate([qkv_w, small_sum.astype(BF)], axis=1)]
    squeeze x15 -> x12, local copies, waits for them, and re-layouts: 17.8 us -> 13.7 us  [pick(): return lax.dynamic_index_in_dim(value, index, axis, False)]
    unnamed x76 -> x86, local copies, waits for them, and re-layouts: 9.23 us -> 11.9 us
  transfers between devices with their start and end apart: 62 -> 62, of which waited for: 17 -> 23; matrix products, arithmetic and copies ran while one was open for 14% -> 9% of each run, Pallas kernels for 37% -> 40%
where the time goes in v3:
time: 543 us; the launch traced here: 533 us
  Pallas kernels  219 us (40%)
  starting transfers between devices  127 us (23%)
  waiting for transfers between devices  116 us (21%)
  local copies, waits for them, and re-layouts  40.8 us (8%)
  other arithmetic  28.1 us (5%)
    ppermute x8, waiting for transfers between devices, send(): return lax.ppermute(mine, self.route_axes, self.routes[turn])  62.2 us
    pallas_call x2, Pallas kernels, expert_rows(): pl.pallas_call(expert_rows_body, grid=(steps,), in_specs=[pl.BlockSpec((n...  57.2 us
    ppermute x33, starting transfers between devices, swap(): return lax.ppermute(value, axis, [(0, 1), (1, 0)])  48.8 us
    ppermute x33, waiting for transfers between devices, swap(): return lax.ppermute(value, axis, [(0, 1), (1, 0)])  41.3 us
    pallas_call x2, Pallas kernels, forward_part(): pl.pallas_call(forward_body, grid=(1,), in_specs=[seq_block(D, part), seq...  40.5 us
    pallas_call x2, Pallas kernels, attention_back(): pl.pallas_call(attention_back_body, grid=(1,), in_specs=[fixed((SEQ, 3 *...  36 us
    pallas_call x2, Pallas kernels, combine_part(): pl.pallas_call(body, grid=(2,), in_specs=[fixed((EXPERTS, 2, CAP, D)), ti...  30 us
    ppermute x8, starting transfers between devices, send(): return lax.ppermute(mine, self.route_axes, self.routes[turn])  25.9 us
  transfers between devices with their start and end apart: 62, of which 23 were waited for; matrix products, arithmetic and copies ran while one was open for 9% of the time, Pallas kernels for 40%

profile of v3, /device:TPU:1, one launch (start us, length us, event | category | flops | bytes accessed | tf_op | source)
XLA Modules:
  0.0 533.2 jit_solution(2142174105309336178)
XLA Ops:
  29.2 5.6 %collective-permute-done.3.refs_2_ = bf16[192,1664]{1,0:T(8,128)(2,1)} collective-permute-done((bf16[192,1664]{1,0:T(8,128)(2,1)S(1)}, bf16[192,1664]{1,0:T(8,128)(2,1)}, u32[]{:S(2)}, u32[]{:S(2)}) %collective-permute-start.3) | collective-permute-done | bytes 639008 | tf_op jit(solution)/shard_map/ppermute | solution.py:682
  38.0 7.8 %collective-permute-start.7 = (bf16[192,1664]{1,0:T(8,128)(2,1)S(1)}, bf16[192,1664]{1,0:T(8,128)(2,1)}, u32[]{:S(2)}, u32[]{:S(2)}) collective-permute-start(bf16[192,1664]{1,0:T(8,128)(2,1)S(1)} %pad_maximum_fusion.5.refs_1_), channel_id=1, source_target_pairs={{0,1},{1,0},{2,3},{3,2},{4,5},{5,4},{6,7},{7,6},{8,9},{9,8},{10,11... | collective-permute-start | bytes 1916936 | tf_op jit(solution)/shard_map/ppermute | solution.py:682
  47.4 8.3 %collective-permute-done.12.refs_5_ = bf16[96,3072]{1,0:T(8,128)(2,1)} collective-permute-done((bf16[96,3072]{1,0:T(8,128)(2,1)S(1)}, bf16[96,3072]{1,0:T(8,128)(2,1)}, u32[]{:S(2)}, u32[]{:S(2)}) %collective-permute-start.12) | collective-permute-done | bytes 589856 | tf_op jit(solution)/shard_map/ppermute | solution.py:715
  68.1 5.9 %shard_map.230.w_qkv.w_out.w_small.refs_7_.refs_8_ = bf16[768,3328]{1,0:T(8,128)(2,1)} custom-call(s32[80]{0:T(128)} %stack.300.refs_0_, bf16[192,1664]{1,0:T(8,128)(2,1)} %copy-done.6, bf16[192,1664]{1,0:T(8,128)(2,1)} %collective-permute-done.3.refs_2_, bf16[192,1664]{1,0:T(8,128)(2,1)} %collective-permute-done.4.refs_3_, bf16[192,896]{1,0:T(8,128)(2,1)} %copy-done.31, ...), custom_call_target="tpu_custom_call" | custom-call | flops 1 | tf_op jit(solution)/shard_map/pallas_call | solution.py:640
  84.2 7.3 %collective-permute-start.16 = (bf16[96,3072]{1,0:T(8,128)(2,1)}, bf16[96,3072]{1,0:T(8,128)(2,1)}, u32[]{:S(2)}, u32[]{:S(2)}) collective-permute-start(bf16[96,3072]{1,0:T(8,128)(2,1)} %get-tuple-element.319), channel_id=1, source_target_pairs={{0,16},{1,24},{4,17},{5,25},{8,20},{9,28},{12,21},{13,29},{16,0},{... | collective-permute-start | bytes 1769480 | tf_op jit(solution)/shard_map/ppermute | solution.py:715
  92.2 20.2 %shard_map.231 = (bf16[8,2,128,768]{3,2,1,0:T(8,128)(2,1)}, bf16[512,2304]{1,0:T(8,128)(2,1)}, bf16[512,768]{1,0:T(8,128)(2,1)}, f32[512,768]{1,0:T(8,128)}, f32[16,512]{1,0:T(8,128)}, /*index=5*/f32[512,128]{1,0:T(8,128)}) custom-call(bf16[1024,768]{1,0:T(8,128)(2,1)} %tok.3, bf16[1024,768]{1,0:T(8,128)(2,1)} %cot.2, bf16[1024,128]{1,0:T(8,128)(2,1)} %pad.4.prev, ...), custom_call_target="tpu_custom_call" | custom-call | flops 99999997952 | tf_op jit(solution)/shard_map/pallas_call | solution.py:180
  124.0 20.2 %shard_map.232 = (bf16[8,2,128,768]{3,2,1,0:T(8,128)(2,1)}, bf16[512,2304]{1,0:T(8,128)(2,1)}, bf16[512,768]{1,0:T(8,128)(2,1)}, f32[512,768]{1,0:T(8,128)}, f32[16,512]{1,0:T(8,128)}, /*index=5*/f32[512,128]{1,0:T(8,128)}) custom-call(bf16[1024,768]{1,0:T(8,128)(2,1)} %tok.3, bf16[1024,768]{1,0:T(8,128)(2,1)} %cot.2, bf16[1024,128]{1,0:T(8,128)(2,1)} %pad.4.prev, ...), custom_call_target="tpu_custom_call" | custom-call | flops 99999997952 | tf_op jit(solution)/shard_map/pallas_call | solution.py:180
  144.2 34.1 %collective-permute-done.17.refs_4_ = bf16[96,3072]{1,0:T(8,128)(2,1)S(1)} collective-permute-done((bf16[96,3072]{1,0:T(8,128)(2,1)S(1)}, bf16[96,3072]{1,0:T(8,128)(2,1)S(1)}, u32[]{:S(2)}, u32[]{:S(2)}) %collective-permute-start.17) | collective-permute-done | bytes 589856 | tf_op jit(solution)/shard_map/ppermute | solution.py:715
  178.3 11.8 %collective-permute-done.19.refs_8_ = bf16[96,3072]{1,0:T(8,128)(2,1)S(1)} collective-permute-done((bf16[96,3072]{1,0:T(8,128)(2,1)S(1)}, bf16[96,3072]{1,0:T(8,128)(2,1)S(1)}, u32[]{:S(2)}, u32[]{:S(2)}) %collective-permute-start.19) | collective-permute-done | bytes 589856 | tf_op jit(solution)/shard_map/ppermute | solution.py:715
  190.1 8.1 %collective-permute-done.18.refs_7_ = bf16[96,3072]{1,0:T(8,128)(2,1)S(1)} collective-permute-done((bf16[96,3072]{1,0:T(8,128)(2,1)S(1)}, bf16[96,3072]{1,0:T(8,128)(2,1)S(1)}, u32[]{:S(2)}, u32[]{:S(2)}) %collective-permute-start.18) | collective-permute-done | bytes 589856 | tf_op jit(solution)/shard_map/ppermute | solution.py:715
  200.7 6.6 %all-to-all-start.2 = ((bf16[8,2,128,768]{3,2,1,0:T(8,128)(2,1)}), bf16[8,2,128,768]{3,2,1,0:T(8,128)(2,1)}, u32[]{:S(2)}, u32[]{:S(2)}) async-start(bf16[8,2,128,768]{3,2,1,0:T(8,128)(2,1)} %get-tuple-element.172), calls=%async_computation.2 | async-start | bytes 6291456 | tf_op jit(solution)/shard_map/all_to_all | solution.py:898
  216.2 8.6 %shard_map.233 = (bf16[768,4096]{1,0:T(8,128)(2,1)}, bf16[2048,768]{1,0:T(8,128)(2,1)}) custom-call(s32[112]{0:T(128)} %stack.341.refs_0_, bf16[96,3072]{1,0:T(8,128)(2,1)} %collective-permute-done.13.refs_1_, bf16[96,3072]{1,0:T(8,128)(2,1)} %collective-permute-done.14.refs_2_, bf16[96,3072]{1,0:T(8,128)(2,1)} %collective-permute-done.15.refs_3_, ...), custom_call_target="tpu_custom_call" | custom-call | flops 1 | tf_op jit(solution)/shard_map/pallas_call | solution.py:640
  224.8 28.6 %shard_map.234 = (bf16[1024,2048]{1,0:T(8,128)(2,1)}, bf16[1024,2048]{1,0:T(8,128)(2,1)}, bf16[1024,2048]{1,0:T(8,128)(2,1)}, bf16[8,2,128,768]{3,2,1,0:T(8,128)(2,1)}) custom-call(bf16[8,2,128,768]{3,2,1,0:T(8,128)(2,1)} %copy-done, bf16[8,2,128,768]{3,2,1,0:T(8,128)(2,1)} %copy-done, bf16[768,4096]{1,0:T(8,128)(2,1)} %get-tuple-element.169.wg_ref.wu_ref, ...), custom_call_target="tpu_custom_call" | custom-call | flops 28000000000 | tf_op jit(solution)/shard_map/pallas_call | solution.py:547
  258.2 28.6 %shard_map.235 = (bf16[1024,2048]{1,0:T(8,128)(2,1)}, bf16[1024,2048]{1,0:T(8,128)(2,1)}, bf16[1024,2048]{1,0:T(8,128)(2,1)}, bf16[8,2,128,768]{3,2,1,0:T(8,128)(2,1)}) custom-call(bf16[8,2,128,768]{3,2,1,0:T(8,128)(2,1)} %all-to-all-done.2.x_ref.g_ref.refs_3_.refs_1_, bf16[8,2,128,768]{3,2,1,0:T(8,128)(2,1)} %all-to-all-done.2.x_ref.g_ref.refs_3_.refs_1_, ...), custom_call_target="tpu_custom_call" | custom-call | flops 28000000000 | tf_op jit(solution)/shard_map/pallas_call | solution.py:547
  286.8 10.9 %shard_map.236 = bf16[2048,768]{1,0:T(8,128)(2,1)} custom-call(bf16[1024,2048]{1,0:T(8,128)(2,1)} %get-tuple-element.176.refs_0_, bf16[1024,2048]{1,0:T(8,128)(2,1)} %get-tuple-element.177.refs_1_, bf16[8,2,128,768]{3,2,1,0:T(8,128)(2,1)} %copy-done, bf16[8,2,128,768]{3,2,1,0:T(8,128)(2,1)} %all-to-all-done.2.x_ref.g_ref.refs_3_.refs_1_), custom_call_target="tpu_custom_call" | custom-call | flops 10000000000 | tf_op jit(solution)/shard_map/pallas_call | solution.py:578
  309.1 19.1 %shard_map.237 = bf16[2,768,2048]{2,1,0:T(8,128)(2,1)} custom-call(bf16[8,2,128,768]{3,2,1,0:T(8,128)(2,1)} %copy-done, bf16[8,2,128,768]{3,2,1,0:T(8,128)(2,1)} %all-to-all-done.2.x_ref.g_ref.refs_3_.refs_1_, bf16[1024,2048]{1,0:T(8,128)(2,1)} %get-tuple-element.179.refs_2_, bf16[1024,2048]{1,0:T(8,128)(2,1)} %get-tuple-element.180.refs_3_, ...), custom_call_target="tpu_custom_call" | custom-call | flops 1 | tf_op jit(solution)/shard_map/pallas_call | solution.py:606
  348.9 7.3 %collective-permute-start.32 = (bf16[256,768]{1,0:T(8,128)(2,1)}, bf16[256,768]{1,0:T(8,128)(2,1)}, u32[]{:S(2)}, u32[]{:S(2)}) collective-permute-start(bf16[256,768]{1,0:T(8,128)(2,1)} %get-tuple-element.312), channel_id=1, source_target_pairs={{16,0},{24,1},{17,4},{25,5},{20,8},{28,9},{21,12},{29,13},{0,16},{... | collective-permute-start | bytes 1179656 | tf_op jit(solution)/shard_map/ppermute | solution.py:810
  357.5 14.6 %shard_map.238 = (bf16[512,768]{1,0:T(8,128)(2,1)}, f32[512,768]{1,0:T(8,128)}, f32[512,12]{1,0:T(8,128)}, bf16[512,768]{1,0:T(8,128)(2,1)}, f32[768,768]{1,0:T(...) custom-call(bf16[8,2,128,768]{3,2,1,0:T(8,128)(2,1)} %copy-done.1, f32[512,768]{1,0:T(8,128)} %get-tuple-element.184.refs_1_, ...), custom_call_target="tpu_custom_call" | custom-call | flops 1 | tf_op jit(solution)/shard_map/pallas_call | solution.py:311
  372.2 15.4 %shard_map.239 = (bf16[512,768]{1,0:T(8,128)(2,1)}, f32[512,768]{1,0:T(8,128)}, f32[512,12]{1,0:T(8,128)}, bf16[512,768]{1,0:T(8,128)(2,1)}, f32[768,768]{1,0:T(...) custom-call(bf16[8,2,128,768]{3,2,1,0:T(8,128)(2,1)} %all-to-all-done.3.back, f32[512,768]{1,0:T(8,128)} %get-tuple-element.190.resid, ...), custom_call_target="tpu_custom_call" | custom-call | flops 1 | tf_op jit(solution)/shard_map/pallas_call | solution.py:311
  405.2 18.0 %shard_map.240 = (f32[512,768]{1,0:T(8,128)}, bf16[512,2304]{1,0:T(8,128)(2,1)}, bf16[512,768]{1,0:T(8,128)(2,1)}, f32[8,768]{1,0:T(8,128)}) custom-call(bf16[512,2304]{1,0:T(8,128)(2,1)} %get-tuple-element.197.qkv, bf16[512,768]{1,0:T(8,128)(2,1)} %get-tuple-element.198.agrad, f32[16,512]{1,0:T(8,128)} %get-tuple-element.199.lse, s32[1024,1]{1,0:T(8,128)} %copy.157.seg_col, ...), custom_call_target="tpu_custom_call" | custom-call | flops 1 | tf_op jit(solution)/shard_map/pallas_call | solution.py:400
  432.7 18.0 %shard_map.241 = (f32[512,768]{1,0:T(8,128)}, bf16[512,2304]{1,0:T(8,128)(2,1)}, bf16[512,768]{1,0:T(8,128)(2,1)}, f32[8,768]{1,0:T(8,128)}) custom-call(bf16[512,2304]{1,0:T(8,128)(2,1)} %get-tuple-element.206.qkv, bf16[512,768]{1,0:T(8,128)(2,1)} %get-tuple-element.207.agrad, f32[16,512]{1,0:T(8,128)} %get-tuple-element.208.lse, s32[1024,1]{1,0:T(8,128)} %copy.157.seg_col, ...), custom_call_target="tpu_custom_call" | custom-call | flops 1 | tf_op jit(solution)/shard_map/pallas_call | solution.py:400
  450.7 11.2 %shard_map.242 = (bf16[384,2560]{1,0:T(8,128)(2,1)}, bf16[384,2560]{1,0:T(8,128)(2,1)}) custom-call(s32[1]{0:T(128)} %bitcast.90.refs_0_, bf16[512,768]{1,0:T(8,128)(2,1)} %get-tuple-element.216.refs_1_, bf16[512,768]{1,0:T(8,128)(2,1)} %get-tuple-element.217.refs_2_, bf16[512,2304]{1,0:T(8,128)(2,1)} %get-tuple-element.218.refs_3_, ...), custom_call_target="tpu_custom_call" | custom-call | flops 1 | tf_op jit(solution)/shard_map/pallas_call | solution.py:464
  463.3 10.7 %collective-permute-start.41 = (bf16[384,2560]{1,0:T(8,128)(2,1)}, bf16[384,2560]{1,0:T(8,128)(2,1)S(1)}, u32[]{:S(2)}, u32[]{:S(2)}) collective-permute-start(bf16[384,2560]{1,0:T(8,128)(2,1)} %get-tuple-element.228), channel_id=1, source_target_pairs={{0,1},{1,0},{2,3},{3,2},{4,5},{5,4},{6,7},{7,6},{8,9},{9,8},{10,11... | collective-permute-start | bytes 5898248 | tf_op jit(solution)/shard_map/ppermute | solution.py:682
  490.3 10.4 %collective-permute-done.42 = bf16[4,2,48,640]{3,2,1,0:T(8,128)(2,1)S(1)} collective-permute-done((bf16[4,2,48,640]{3,2,1,0:T(8,128)(2,1)S(1)}, bf16[4,2,48,640]{3,2,1,0:T(8,128)(2,1)S(1)}, u32[]{:S(2)}, u32[]{:S(2)}) %collective-permute-start.42) | collective-permute-done | bytes 491552 | tf_op jit(solution)/shard_map/ppermute | solution.py:682
  (294 shorter events, 194.0 us)
Async XLA Ops:
  22.4 23.5 %collective-permute-start.4 = (bf16[192,1664]{1,0:T(8,128)(2,1)S(1)}, bf16[192,1664]{1,0:T(8,128)(2,1)}, u32[]{:S(2)}, u32[]{:S(2)}) collective-permute-start(bf16[192,1664]{1,0:T(8,128)(2,1)S(1)} %pad_maximum_fusion.5.refs_1_), channel_id=1, source_target_pairs={{0,2},{2,0},{1,3},{3,1},{4,6},{6,4},{5,7},{7,5},{8,10},{10,8},{9,1... | collective-permute-start | bytes 1916936 | tf_op jit(solution)/shard_map/ppermute | solution.py:682
  23.6 32.0 %collective-permute-start.12 = (bf16[96,3072]{1,0:T(8,128)(2,1)S(1)}, bf16[96,3072]{1,0:T(8,128)(2,1)}, u32[]{:S(2)}, u32[]{:S(2)}) collective-permute-start(bf16[96,3072]{1,0:T(8,128)(2,1)S(1)} %dynamic-slice_bitcast_fusion.15), channel_id=1, source_target_pairs={{0,16},{1,24},{4,17},{5,25},{8,20},{9,28},{12,21},{13,29},{16,0},{... | collective-permute-start | bytes 1769480 | tf_op jit(solution)/shard_map/ppermute | solution.py:715
  38.0 30.0 %collective-permute-start.7 = (bf16[192,1664]{1,0:T(8,128)(2,1)S(1)}, bf16[192,1664]{1,0:T(8,128)(2,1)}, u32[]{:S(2)}, u32[]{:S(2)}) collective-permute-start(bf16[192,1664]{1,0:T(8,128)(2,1)S(1)} %pad_maximum_fusion.5.refs_1_), channel_id=1, source_target_pairs={{0,1},{1,0},{2,3},{3,2},{4,5},{5,4},{6,7},{7,6},{8,9},{9,8},{10,11... | collective-permute-start | bytes 1916936 | tf_op jit(solution)/shard_map/ppermute | solution.py:682
  76.3 39.8 %collective-permute-start.13 = (bf16[96,3072]{1,0:T(8,128)(2,1)}, bf16[96,3072]{1,0:T(8,128)(2,1)}, u32[]{:S(2)}, u32[]{:S(2)}) collective-permute-start(bf16[96,3072]{1,0:T(8,128)(2,1)} %get-tuple-element.322), channel_id=1, source_target_pairs={{0,0},{1,8},{4,1},{5,9},{8,4},{9,12},{12,5},{13,13},{16,16},{17,24... | collective-permute-start | bytes 1769480 | tf_op jit(solution)/shard_map/ppermute | solution.py:715
  79.5 36.7 %collective-permute-start.14 = (bf16[96,3072]{1,0:T(8,128)(2,1)}, bf16[96,3072]{1,0:T(8,128)(2,1)}, u32[]{:S(2)}, u32[]{:S(2)}) collective-permute-start(bf16[96,3072]{1,0:T(8,128)(2,1)} %get-tuple-element.320), channel_id=1, source_target_pairs={{0,0},{1,8},{4,1},{5,9},{8,4},{9,12},{12,5},{13,13},{16,16},{17,24... | collective-permute-start | bytes 1769480 | tf_op jit(solution)/shard_map/ppermute | solution.py:715
  82.6 33.5 %collective-permute-start.15 = (bf16[96,3072]{1,0:T(8,128)(2,1)}, bf16[96,3072]{1,0:T(8,128)(2,1)}, u32[]{:S(2)}, u32[]{:S(2)}) collective-permute-start(bf16[96,3072]{1,0:T(8,128)(2,1)} %get-tuple-element.321), channel_id=1, source_target_pairs={{0,4},{1,12},{4,5},{5,13},{8,0},{9,8},{12,1},{13,9},{16,20},{17,28... | collective-permute-start | bytes 1769480 | tf_op jit(solution)/shard_map/ppermute | solution.py:715
  84.2 32.0 %collective-permute-start.16 = (bf16[96,3072]{1,0:T(8,128)(2,1)}, bf16[96,3072]{1,0:T(8,128)(2,1)}, u32[]{:S(2)}, u32[]{:S(2)}) collective-permute-start(bf16[96,3072]{1,0:T(8,128)(2,1)} %get-tuple-element.319), channel_id=1, source_target_pairs={{0,16},{1,24},{4,17},{5,25},{8,20},{9,28},{12,21},{13,29},{16,0},{... | collective-permute-start | bytes 1769480 | tf_op jit(solution)/shard_map/ppermute | solution.py:715
  112.4 86.6 %all-to-all-start = ((bf16[8,2,128,768]{3,2,1,0:T(8,128)(2,1)}), bf16[8,2,128,768]{3,2,1,0:T(8,128)(2,1)S(1)}, u32[]{:S(2)}, u32[]{:S(2)}) async-start(bf16[8,2,128,768]{3,2,1,0:T(8,128)(2,1)} %get-tuple-element.147), calls=%async_computation | async-start | bytes 6291456 | tf_op jit(solution)/shard_map/all_to_all | solution.py:898
  117.6 60.8 %collective-permute-start.17 = (bf16[96,3072]{1,0:T(8,128)(2,1)S(1)}, bf16[96,3072]{1,0:T(8,128)(2,1)S(1)}, u32[]{:S(2)}, u32[]{:S(2)}) collective-permute-start(bf16[96,3072]{1,0:T(8,128)(2,1)S(1)} %get-tuple-element.318), channel_id=1, source_target_pairs={{0,4},{1,12},{4,5},{5,13},{8,0},{9,8},{12,1},{13,9},{16,20},{17,28... | collective-permute-start | bytes 1769480 | tf_op jit(solution)/shard_map/ppermute | solution.py:715
  119.0 71.1 %collective-permute-start.19 = (bf16[96,3072]{1,0:T(8,128)(2,1)S(1)}, bf16[96,3072]{1,0:T(8,128)(2,1)S(1)}, u32[]{:S(2)}, u32[]{:S(2)}) collective-permute-start(bf16[96,3072]{1,0:T(8,128)(2,1)S(1)} %get-tuple-element.317), channel_id=1, source_target_pairs={{0,20},{1,28},{4,21},{5,29},{8,16},{9,24},{12,17},{13,25},{16,4},{... | collective-permute-start | bytes 1769480 | tf_op jit(solution)/shard_map/ppermute | solution.py:715
  120.7 77.4 %collective-permute-start.18 = (bf16[96,3072]{1,0:T(8,128)(2,1)S(1)}, bf16[96,3072]{1,0:T(8,128)(2,1)S(1)}, u32[]{:S(2)}, u32[]{:S(2)}) collective-permute-start(bf16[96,3072]{1,0:T(8,128)(2,1)S(1)} %dynamic-slice_bitcast_fusion.9), channel_id=1, source_target_pairs={{0,20},{1,28},{4,21},{5,29},{8,16},{9,24},{12,17},{13,25},{16,4},{... | collective-permute-start | bytes 1769480 | tf_op jit(solution)/shard_map/ppermute | solution.py:715
  200.7 52.8 %all-to-all-start.2 = ((bf16[8,2,128,768]{3,2,1,0:T(8,128)(2,1)}), bf16[8,2,128,768]{3,2,1,0:T(8,128)(2,1)}, u32[]{:S(2)}, u32[]{:S(2)}) async-start(bf16[8,2,128,768]{3,2,1,0:T(8,128)(2,1)} %get-tuple-element.172), calls=%async_computation.2 | async-start | bytes 6291456 | tf_op jit(solution)/shard_map/all_to_all | solution.py:898
  253.4 49.5 %all-to-all-start.1 = ((bf16[8,2,128,768]{3,2,1,0:T(8,128)(2,1)}), bf16[8,2,128,768]{3,2,1,0:T(8,128)(2,1)S(1)}, u32[]{:S(2)}, u32[]{:S(2)}) async-start(bf16[8,2,128,768]{3,2,1,0:T(8,128)(2,1)} %get-tuple-element.171), calls=%async_computation.1 | async-start | bytes 6291456 | tf_op jit(solution)/shard_map/all_to_all | solution.py:904
  304.6 67.6 %all-to-all-start.3 = ((bf16[8,2,128,768]{3,2,1,0:T(8,128)(2,1)}), bf16[8,2,128,768]{3,2,1,0:T(8,128)(2,1)}, u32[]{:S(2)}, u32[]{:S(2)}) async-start(bf16[8,2,128,768]{3,2,1,0:T(8,128)(2,1)} %get-tuple-element.189), calls=%async_computation.3 | async-start | bytes 6291456 | tf_op jit(solution)/shard_map/all_to_all | solution.py:904
  332.3 58.0 %collective-permute-start.28 = (bf16[2,4,96,2048]{3,2,1,0:T(8,128)(2,1)}, bf16[2,4,96,2048]{3,2,1,0:T(8,128)(2,1)}, u32[]{:S(2)}, u32[]{:S(2)}) collective-permute-start(bf16[2,4,96,2048]{3,2,1,0:T(8,128)(2,1)} %dynamic-slice_bitcast_fusion), channel_id=1, source_target_pairs={{0,1},{1,0},{2,3},{3,2},{4,5},{5,4},{6,7},{7,6},{8,9},{9,8},{10,11... | collective-permute-start | bytes 9437192 | tf_op jit(solution)/shard_map/ppermute | solution.py:682
  343.9 51.3 %collective-permute-start.30 = (bf16[256,768]{1,0:T(8,128)(2,1)}, bf16[256,768]{1,0:T(8,128)(2,1)S(1)}, u32[]{:S(2)}, u32[]{:S(2)}) collective-permute-start(bf16[256,768]{1,0:T(8,128)(2,1)} %get-tuple-element.314), channel_id=1, source_target_pairs={{0,0},{8,1},{1,4},{9,5},{4,8},{12,9},{5,12},{13,13},{16,16},{24,17... | collective-permute-start | bytes 1179656 | tf_op jit(solution)/shard_map/ppermute | solution.py:810
  347.6 47.5 %collective-permute-start.31 = (bf16[256,768]{1,0:T(8,128)(2,1)}, bf16[256,768]{1,0:T(8,128)(2,1)S(1)}, u32[]{:S(2)}, u32[]{:S(2)}) collective-permute-start(bf16[256,768]{1,0:T(8,128)(2,1)} %get-tuple-element.313), channel_id=1, source_target_pairs={{4,0},{12,1},{5,4},{13,5},{0,8},{8,9},{1,12},{9,13},{20,16},{28,17... | collective-permute-start | bytes 1179656 | tf_op jit(solution)/shard_map/ppermute | solution.py:810
  348.9 46.3 %collective-permute-start.32 = (bf16[256,768]{1,0:T(8,128)(2,1)}, bf16[256,768]{1,0:T(8,128)(2,1)}, u32[]{:S(2)}, u32[]{:S(2)}) collective-permute-start(bf16[256,768]{1,0:T(8,128)(2,1)} %get-tuple-element.312), channel_id=1, source_target_pairs={{16,0},{24,1},{17,4},{25,5},{20,8},{28,9},{21,12},{29,13},{0,16},{... | collective-permute-start | bytes 1179656 | tf_op jit(solution)/shard_map/ppermute | solution.py:810
  356.2 39.0 %collective-permute-start.33 = (bf16[256,768]{1,0:T(8,128)(2,1)}, bf16[256,768]{1,0:T(8,128)(2,1)}, u32[]{:S(2)}, u32[]{:S(2)}) collective-permute-start(bf16[256,768]{1,0:T(8,128)(2,1)} %get-tuple-element.311), channel_id=1, source_target_pairs={{20,0},{28,1},{21,4},{29,5},{16,8},{24,9},{17,12},{25,13},{4,16},{... | collective-permute-start | bytes 1179656 | tf_op jit(solution)/shard_map/ppermute | solution.py:810
  395.2 28.0 %collective-permute-start.34 = (bf16[8,48,768]{2,1,0:T(8,128)(2,1)}, bf16[8,48,768]{2,1,0:T(8,128)(2,1)S(1)}, u32[]{:S(2)}, u32[]{:S(2)}) collective-permute-start(bf16[8,48,768]{2,1,0:T(8,128)(2,1)} %get-tuple-element.210), channel_id=1, source_target_pairs={{0,1},{1,0},{2,3},{3,2},{4,5},{5,4},{6,7},{7,6},{8,9},{9,8},{10,11... | collective-permute-start | bytes 1769480 | tf_op jit(solution)/shard_map/ppermute | solution.py:682
  397.7 64.2 %collective-permute-start.37 = (bf16[2,96,2048]{2,1,0:T(8,128)(2,1)S(1)}, bf16[2,96,2048]{2,1,0:T(8,128)(2,1)S(1)}, u32[]{:S(2)}, u32[]{:S(2)}) collective-permute-start(bf16[2,96,2048]{2,1,0:T(8,128)(2,1)S(1)} %get-tuple-element.305), channel_id=1, source_target_pairs={{0,0},{8,1},{1,4},{9,5},{4,8},{12,9},{5,12},{13,13},{16,16},{24,17... | collective-permute-start | bytes 2359304 | tf_op jit(solution)/shard_map/ppermute | solution.py:810
  400.2 61.8 %collective-permute-start.38 = (bf16[2,96,2048]{2,1,0:T(8,128)(2,1)S(1)}, bf16[2,96,2048]{2,1,0:T(8,128)(2,1)S(1)}, u32[]{:S(2)}, u32[]{:S(2)}) collective-permute-start(bf16[2,96,2048]{2,1,0:T(8,128)(2,1)S(1)} %get-tuple-element.304), channel_id=1, source_target_pairs={{4,0},{12,1},{5,4},{13,5},{0,8},{8,9},{1,12},{9,13},{20,16},{28,17... | collective-permute-start | bytes 2359304 | tf_op jit(solution)/shard_map/ppermute | solution.py:810
  401.2 60.8 %collective-permute-start.39 = (bf16[2,96,2048]{2,1,0:T(8,128)(2,1)S(1)}, bf16[2,96,2048]{2,1,0:T(8,128)(2,1)S(1)}, u32[]{:S(2)}, u32[]{:S(2)}) collective-permute-start(bf16[2,96,2048]{2,1,0:T(8,128)(2,1)S(1)} %get-tuple-element.303), channel_id=1, source_target_pairs={{16,0},{24,1},{17,4},{25,5},{20,8},{28,9},{21,12},{29,13},{0,16},{... | collective-permute-start | bytes 2359304 | tf_op jit(solution)/shard_map/ppermute | solution.py:810
  403.6 58.4 %collective-permute-start.40 = (bf16[2,96,2048]{2,1,0:T(8,128)(2,1)S(1)}, bf16[2,96,2048]{2,1,0:T(8,128)(2,1)S(1)}, u32[]{:S(2)}, u32[]{:S(2)}) collective-permute-start(bf16[2,96,2048]{2,1,0:T(8,128)(2,1)S(1)} %get-tuple-element.302), channel_id=1, source_target_pairs={{20,0},{28,1},{21,4},{29,5},{16,8},{24,9},{17,12},{25,13},{4,16},{... | collective-permute-start | bytes 2359304 | tf_op jit(solution)/shard_map/ppermute | solution.py:810
  (79 other events, 750.3 us)

commit v4 on v3

--- a/solution.py
+++ b/solution.py
@@ -721,7 +721,7 @@
         mine = lax.dynamic_slice(shard, (c * rows, x * width), (rows, width))
         stack = jnp.concatenate([mine] + [self.along(mine, turn) for turn in (1, 2, 3)])
         stack, joined, early = lax.optimization_barrier((stack, self.joined(*weights), early))
-        sent = {(2, 0): self.send(joined, 2, 0)}
+        sent = {(2, 0): (self.send(joined, 2, 0), None)}
         over_y, over_x = self.swap(stack, "inner"), self.swap(stack, "side")
         far = self.swap(over_y[:, : self.near], "side"), self.swap(over_x[:, self.near :], "inner")
         blocks = [stack, over_y, over_x, *far]
@@ -739,8 +739,10 @@
 
     def gather_more(self, held, value, names):
         joined, sent = held
-        more = {v: self.send(joined, *v) for v in names}
-        value, joined, sent = lax.optimization_barrier((value, joined, {**sent, **more}))
+        more = {v: (self.send(joined, *v), None) for v in names}
+        waiting = [v for v, (_, other) in sent.items() if other is None][:2]
+        done = {**sent, **{v: (sent[v][0], self.swap(sent[v][0])) for v in waiting}}
+        value, joined, sent = lax.optimization_barrier((value, joined, {**done, **more}))
         return (joined, sent), value
 
     def split(self):
@@ -783,8 +785,8 @@
         sent = held[1]
         c = lax.axis_index("core")
         here = lax.axis_index("half") * 2 + lax.axis_index("inner")
-        own = [sent[turn, part] for turn in range(4) for part in range(2)]
-        blocks = own + [self.swap(v) for v in own]
+        both = [sent[turn, part] for turn in range(4) for part in range(2)]
+        blocks = [v for v, _ in both] + [self.swap(v) if other is None else other for v, other in both]
         high, deep = shapes[0][1], shapes[1][1]
         spots, offsets, zero = [], [], jnp.int32(0)
         for i in range(0, 16, 2):
@@ -899,36 +901,33 @@
         made = [expert_rows(r, gate_up_full, down_full) for r in received]
         hid, dg, du = [[m[i] for m in made] for i in range(3)]
         backs = [m[3] for m in made]
+        gate_up_w = gate_up_wgrad(received, dg, du)
+        backs[-1], hid, gate_up_w = lax.optimization_barrier((backs[-1], hid, gate_up_w))
+        returned = [lax.all_to_all(v, plan.rows, 0, 0, tiled=True) for v in backs]
+        gate_up_sums = plan.scatter_start(gate_up_w, 1)
         down_w = down_wgrad(received, hid)
-        backs[-1], down_w = lax.optimization_barrier((backs[-1], down_w))
-        returned = [lax.all_to_all(v, plan.rows, 0, 0, tiled=True) for v in backs]
-        dg, down_w = lax.optimization_barrier((dg, down_w))
-        gate_up_w = gate_up_wgrad(received, dg, du)
-        returned[0], gate_up_w = lax.optimization_barrier((returned[0], gate_up_w))
-        down_got = plan.scatter_send(plan.scatter_start(down_w, 0), 0)
-        gate_up_sums = plan.scatter_start(gate_up_w, 1)
-        firsts, sums = [], None
+        returned[0], gate_up_sums, down_w = lax.optimization_barrier((returned[0], gate_up_sums, down_w))
+        gate_up_got = plan.scatter_send(gate_up_sums, 1)
+        down_sums = plan.scatter_start(down_w, 0)
+        firsts, lasts, sums = [], [], None
         for i in range(parts):
             *first, out_w, small_w, rows_w = combine_part(i, returned[i], kept[i], t, packed, vecs, sums)
             sums = (out_w, small_w, rows_w)
             firsts.append(first)
-        out_halves = plan.halves(sums[0].astype(BF))
-        held = (out_halves, firsts[0][1], gate_up_sums, down_got)
-        out_halves, firsts[0][1], gate_up_sums, down_got = lax.optimization_barrier(held)
-        gate_up_got = plan.scatter_send(gate_up_sums, 1)
-        down_total = plan.scatter_end(down_got, 0)
-        out_summed = plan.reduce_first(*out_halves)
-        lasts = []
-        for i, first in enumerate(firsts):
             if i == parts - 1:
-                out_summed, first[1] = lax.optimization_barrier((out_summed, first[1]))
-                out_total = plan.reduce_last(*out_summed)
+                held = (gate_up_got, down_sums, first[1], [v[3] for v in lasts])
+                gate_up_got, down_sums, first[1], _ = lax.optimization_barrier(held)
+                down_got = plan.scatter_send(down_sums, 0)
             lasts.append(attention_back(i, kept[i], first[1], first[3], t, packed, vecs))
+            if i == 0:
+                returned[-1], sums, _ = lax.optimization_barrier((returned[-1], sums, lasts[0][3]))
+        out_total = plan.reduce_last(*plan.reduce_first(*plan.halves(sums[0].astype(BF))))
         acts = [v[2] for v in lasts]
         halves = mixer_wgrad(
             acts, [v[1] for v in lasts], [v[3] for v in lasts], sums[1], sums[2], *plan.split()
         )
-        halves, gate_up_got = lax.optimization_barrier((halves, gate_up_got))
+        halves, down_got = lax.optimization_barrier((halves, down_got))
+        down_total = plan.scatter_end(down_got, 0)
         total = plan.reduce_last(*plan.reduce_first(*halves))
         gate_up_total = plan.scatter_end(gate_up_got, 1)
         gate_up_total = jnp.concatenate([gate_up_total[:, 0], gate_up_total[:, 1]], axis=2)

time: 543 us -> 533 us (0.982)
  waiting for transfers between devices: 116 us -> 100 us
    ppermute x33, waiting for transfers between devices: 41.3 us -> 29.8 us  [swap(): return lax.ppermute(value, axis, [(0, 1), (1, 0)])]
    ppermute x33, starting transfers between devices: 48.8 us -> 40.5 us  [swap(): return lax.ppermute(value, axis, [(0, 1), (1, 0)])]
    ppermute x8, starting transfers between devices: 21.1 us -> 27.7 us  [scatter_send(): lax.ppermute(pick(parts, here ^ turn, axis), self.route_axes, back)]
    unnamed x86 -> x74, local copies, waits for them, and re-layouts: 11.9 us -> 11 us
  transfers between devices with their start and end apart: 62 -> 62, of which waited for: 23 -> 19; matrix products, arithmetic and copies ran while one was open for 9% -> 10% of each run, Pallas kernels for 40% -> 41%
where the time goes in v4:
time: 533 us; the launch traced here: 522 us
  Pallas kernels  220 us (41%)
  starting transfers between devices  129 us (24%)
  waiting for transfers between devices  100 us (19%)
  local copies, waits for them, and re-layouts  39.4 us (7%)
  other arithmetic  31.7 us (6%)
    ppermute x8, waiting for transfers between devices, send(): return lax.ppermute(mine, self.route_axes, self.routes[turn])  62.1 us
    pallas_call x2, Pallas kernels, expert_rows(): pl.pallas_call(expert_rows_body, grid=(steps,), in_specs=[pl.BlockSpec((n...  57.2 us
    pallas_call x2, Pallas kernels, forward_part(): pl.pallas_call(forward_body, grid=(1,), in_specs=[seq_block(D, part), seq...  40.5 us
    ppermute x33, starting transfers between devices, swap(): return lax.ppermute(value, axis, [(0, 1), (1, 0)])  40.5 us
    pallas_call x2, Pallas kernels, attention_back(): pl.pallas_call(attention_back_body, grid=(1,), in_specs=[fixed((SEQ, 3 *...  36.2 us
    pallas_call x2, Pallas kernels, combine_part(): pl.pallas_call(body, grid=(2,), in_specs=[fixed((EXPERTS, 2, CAP, D)), ti...  30.1 us
    ppermute x33, waiting for transfers between devices, swap(): return lax.ppermute(value, axis, [(0, 1), (1, 0)])  29.8 us
    ppermute x8, starting transfers between devices, scatter_send(): lax.ppermute(pick(parts, here ^ turn, axis), self.route_axes, back)  27.7 us
  transfers between devices with their start and end apart: 62, of which 19 were waited for; matrix products, arithmetic and copies ran while one was open for 10% of the time, Pallas kernels for 41%

profile of v4, /device:TPU:1, one launch (start us, length us, event | category | flops | bytes accessed | tf_op | source)
XLA Modules:
  0.0 522.5 jit_solution(1966784757495226784)
XLA Ops:
  23.6 5.5 %collective-permute-start.12 = (bf16[96,3072]{1,0:T(8,128)(2,1)S(1)}, bf16[96,3072]{1,0:T(8,128)(2,1)}, u32[]{:S(2)}, u32[]{:S(2)}) collective-permute-start(bf16[96,3072]{1,0:T(8,128)(2,1)S(1)} %dynamic-slice_bitcast_fusion.14), channel_id=1, source_target_pairs={{0,16},{1,24},{4,17},{5,25},{8,20},{9,28},{12,21},{13,29},{16,0},{... | collective-permute-start | bytes 1769480 | tf_op jit(solution)/shard_map/ppermute | solution.py:715
  29.2 5.6 %collective-permute-done.3.refs_2_ = bf16[192,1664]{1,0:T(8,128)(2,1)} collective-permute-done((bf16[192,1664]{1,0:T(8,128)(2,1)S(1)}, bf16[192,1664]{1,0:T(8,128)(2,1)}, u32[]{:S(2)}, u32[]{:S(2)}) %collective-permute-start.3) | collective-permute-done | bytes 639008 | tf_op jit(solution)/shard_map/ppermute | solution.py:682
  38.0 7.8 %collective-permute-start.7 = (bf16[192,1664]{1,0:T(8,128)(2,1)S(1)}, bf16[192,1664]{1,0:T(8,128)(2,1)}, u32[]{:S(2)}, u32[]{:S(2)}) collective-permute-start(bf16[192,1664]{1,0:T(8,128)(2,1)S(1)} %pad_maximum_fusion.5.refs_1_), channel_id=1, source_target_pairs={{0,1},{1,0},{2,3},{3,2},{4,5},{5,4},{6,7},{7,6},{8,9},{9,8},{10,11... | collective-permute-start | bytes 1916936 | tf_op jit(solution)/shard_map/ppermute | solution.py:682
  47.4 8.3 %collective-permute-done.12.refs_5_ = bf16[96,3072]{1,0:T(8,128)(2,1)} collective-permute-done((bf16[96,3072]{1,0:T(8,128)(2,1)S(1)}, bf16[96,3072]{1,0:T(8,128)(2,1)}, u32[]{:S(2)}, u32[]{:S(2)}) %collective-permute-start.12) | collective-permute-done | bytes 589856 | tf_op jit(solution)/shard_map/ppermute | solution.py:715
  68.1 5.9 %shard_map.230.w_qkv.w_out.w_small.refs_7_.refs_8_ = bf16[768,3328]{1,0:T(8,128)(2,1)} custom-call(s32[80]{0:T(128)} %stack.300.refs_0_, bf16[192,1664]{1,0:T(8,128)(2,1)} %copy-done.8, bf16[192,1664]{1,0:T(8,128)(2,1)} %collective-permute-done.3.refs_2_, bf16[192,1664]{1,0:T(8,128)(2,1)} %collective-permute-done.4.refs_3_, bf16[192,896]{1,0:T(8,128)(2,1)} %copy-done.24, ...), custom_call_target="tpu_custom_call" | custom-call | flops 1 | tf_op jit(solution)/shard_map/pallas_call | solution.py:640
  84.1 7.3 %collective-permute-start.17 = (bf16[96,3072]{1,0:T(8,128)(2,1)}, bf16[96,3072]{1,0:T(8,128)(2,1)}, u32[]{:S(2)}, u32[]{:S(2)}) collective-permute-start(bf16[96,3072]{1,0:T(8,128)(2,1)} %get-tuple-element.323), channel_id=1, source_target_pairs={{0,16},{1,24},{4,17},{5,25},{8,20},{9,28},{12,21},{13,29},{16,0},{... | collective-permute-start | bytes 1769480 | tf_op jit(solution)/shard_map/ppermute | solution.py:715
  92.0 20.3 %shard_map.231 = (bf16[8,2,128,768]{3,2,1,0:T(8,128)(2,1)}, bf16[512,2304]{1,0:T(8,128)(2,1)}, bf16[512,768]{1,0:T(8,128)(2,1)}, f32[512,768]{1,0:T(8,128)}, f32[16,512]{1,0:T(8,128)}, /*index=5*/f32[512,128]{1,0:T(8,128)}) custom-call(bf16[1024,768]{1,0:T(8,128)(2,1)} %tok.3, bf16[1024,768]{1,0:T(8,128)(2,1)} %cot.2, bf16[1024,128]{1,0:T(8,128)(2,1)} %pad.4.prev, ...), custom_call_target="tpu_custom_call" | custom-call | flops 99999997952 | tf_op jit(solution)/shard_map/pallas_call | solution.py:180
  125.8 20.2 %shard_map.232 = (bf16[8,2,128,768]{3,2,1,0:T(8,128)(2,1)}, bf16[512,2304]{1,0:T(8,128)(2,1)}, bf16[512,768]{1,0:T(8,128)(2,1)}, f32[512,768]{1,0:T(8,128)}, f32[16,512]{1,0:T(8,128)}, /*index=5*/f32[512,128]{1,0:T(8,128)}) custom-call(bf16[1024,768]{1,0:T(8,128)(2,1)} %tok.3, bf16[1024,768]{1,0:T(8,128)(2,1)} %cot.2, bf16[1024,128]{1,0:T(8,128)(2,1)} %pad.4.prev, ...), custom_call_target="tpu_custom_call" | custom-call | flops 99999997952 | tf_op jit(solution)/shard_map/pallas_call | solution.py:180
  146.0 32.6 %collective-permute-done.20.refs_4_ = bf16[96,3072]{1,0:T(8,128)(2,1)S(1)} collective-permute-done((bf16[96,3072]{1,0:T(8,128)(2,1)S(1)}, bf16[96,3072]{1,0:T(8,128)(2,1)S(1)}, u32[]{:S(2)}, u32[]{:S(2)}) %collective-permute-start.20) | collective-permute-done | bytes 589856 | tf_op jit(solution)/shard_map/ppermute | solution.py:715
  178.6 12.6 %collective-permute-done.22.refs_8_ = bf16[96,3072]{1,0:T(8,128)(2,1)S(1)} collective-permute-done((bf16[96,3072]{1,0:T(8,128)(2,1)S(1)}, bf16[96,3072]{1,0:T(8,128)(2,1)S(1)}, u32[]{:S(2)}, u32[]{:S(2)}) %collective-permute-start.22) | collective-permute-done | bytes 589856 | tf_op jit(solution)/shard_map/ppermute | solution.py:715
  191.2 8.6 %collective-permute-done.21.refs_7_ = bf16[96,3072]{1,0:T(8,128)(2,1)S(1)} collective-permute-done((bf16[96,3072]{1,0:T(8,128)(2,1)S(1)}, bf16[96,3072]{1,0:T(8,128)(2,1)S(1)}, u32[]{:S(2)}, u32[]{:S(2)}) %collective-permute-start.21) | collective-permute-done | bytes 589856 | tf_op jit(solution)/shard_map/ppermute | solution.py:715
  214.9 8.6 %shard_map.233 = (bf16[768,4096]{1,0:T(8,128)(2,1)}, bf16[2048,768]{1,0:T(8,128)(2,1)}) custom-call(s32[112]{0:T(128)} %stack.341.refs_0_, bf16[96,3072]{1,0:T(8,128)(2,1)} %collective-permute-done.13.refs_1_, bf16[96,3072]{1,0:T(8,128)(2,1)} %collective-permute-done.14.refs_2_, bf16[96,3072]{1,0:T(8,128)(2,1)} %collective-permute-done.15.refs_3_, ...), custom_call_target="tpu_custom_call" | custom-call | flops 1 | tf_op jit(solution)/shard_map/pallas_call | solution.py:640
  223.5 28.6 %shard_map.234 = (bf16[1024,2048]{1,0:T(8,128)(2,1)}, bf16[1024,2048]{1,0:T(8,128)(2,1)}, bf16[1024,2048]{1,0:T(8,128)(2,1)}, bf16[8,2,128,768]{3,2,1,0:T(8,128)(2,1)}) custom-call(bf16[8,2,128,768]{3,2,1,0:T(8,128)(2,1)} %copy-done, bf16[8,2,128,768]{3,2,1,0:T(8,128)(2,1)} %copy-done, bf16[768,4096]{1,0:T(8,128)(2,1)} %get-tuple-element.176.wg_ref.wu_ref, ...), custom_call_target="tpu_custom_call" | custom-call | flops 28000000000 | tf_op jit(solution)/shard_map/pallas_call | solution.py:547
  256.9 28.6 %shard_map.235 = (bf16[1024,2048]{1,0:T(8,128)(2,1)}, bf16[1024,2048]{1,0:T(8,128)(2,1)}, bf16[1024,2048]{1,0:T(8,128)(2,1)}, bf16[8,2,128,768]{3,2,1,0:T(8,128)(2,1)}) custom-call(bf16[8,2,128,768]{3,2,1,0:T(8,128)(2,1)} %all-to-all-done.2.x_ref.g_ref.refs_1_.refs_3_, bf16[8,2,128,768]{3,2,1,0:T(8,128)(2,1)} %all-to-all-done.2.x_ref.g_ref.refs_1_.refs_3_, ...), custom_call_target="tpu_custom_call" | custom-call | flops 28000000000 | tf_op jit(solution)/shard_map/pallas_call | solution.py:547
  285.5 19.1 %shard_map.236 = bf16[2,768,2048]{2,1,0:T(8,128)(2,1)} custom-call(bf16[8,2,128,768]{3,2,1,0:T(8,128)(2,1)} %copy-done, bf16[8,2,128,768]{3,2,1,0:T(8,128)(2,1)} %all-to-all-done.2.x_ref.g_ref.refs_1_.refs_3_, bf16[1024,2048]{1,0:T(8,128)(2,1)} %get-tuple-element.183.refs_2_, bf16[1024,2048]{1,0:T(8,128)(2,1)} %get-tuple-element.184.refs_3_, ...), custom_call_target="tpu_custom_call" | custom-call | flops 1 | tf_op jit(solution)/shard_map/pallas_call | solution.py:606
  315.9 11.0 %shard_map.237 = bf16[2048,768]{1,0:T(8,128)(2,1)} custom-call(bf16[1024,2048]{1,0:T(8,128)(2,1)} %get-tuple-element.188.refs_0_, bf16[1024,2048]{1,0:T(8,128)(2,1)} %get-tuple-element.189.refs_1_, bf16[8,2,128,768]{3,2,1,0:T(8,128)(2,1)} %copy-done, bf16[8,2,128,768]{3,2,1,0:T(8,128)(2,1)} %all-to-all-done.2.x_ref.g_ref.refs_1_.refs_3_), custom_call_target="tpu_custom_call" | custom-call | flops 10000000000 | tf_op jit(solution)/shard_map/pallas_call | solution.py:578
  341.3 6.0 %collective-permute-start.31 = (bf16[2,96,2048]{2,1,0:T(8,128)(2,1)}, bf16[2,96,2048]{2,1,0:T(8,128)(2,1)S(1)}, u32[]{:S(2)}, u32[]{:S(2)}) collective-permute-start(bf16[2,96,2048]{2,1,0:T(8,128)(2,1)} %get-tuple-element.309), channel_id=1, source_target_pairs={{16,0},{24,1},{17,4},{25,5},{20,8},{28,9},{21,12},{29,13},{0,16},{... | collective-permute-start | bytes 2359304 | tf_op jit(solution)/shard_map/ppermute | solution.py:812
  349.7 14.4 %shard_map.238 = (bf16[512,768]{1,0:T(8,128)(2,1)}, f32[512,768]{1,0:T(8,128)}, f32[512,12]{1,0:T(8,128)}, bf16[512,768]{1,0:T(8,128)(2,1)}, f32[768,768]{1,0:T(...) custom-call(bf16[8,2,128,768]{3,2,1,0:T(8,128)(2,1)} %copy-done.1, f32[512,768]{1,0:T(8,128)} %get-tuple-element.191.refs_1_, ...), custom_call_target="tpu_custom_call" | custom-call | flops 1 | tf_op jit(solution)/shard_map/pallas_call | solution.py:311
  364.1 18.0 %shard_map.239 = (f32[512,768]{1,0:T(8,128)}, bf16[512,2304]{1,0:T(8,128)(2,1)}, bf16[512,768]{1,0:T(8,128)(2,1)}, f32[8,768]{1,0:T(8,128)}) custom-call(bf16[512,2304]{1,0:T(8,128)(2,1)} %get-tuple-element.200.qkv, bf16[512,768]{1,0:T(8,128)(2,1)} %get-tuple-element.201.agrad, f32[16,512]{1,0:T(8,128)} %get-tuple-element.202.lse, s32[1024,1]{1,0:T(8,128)} %copy.160.seg_col, ...), custom_call_target="tpu_custom_call" | custom-call | flops 1 | tf_op jit(solution)/shard_map/pallas_call | solution.py:400
  382.9 15.7 %shard_map.240 = (bf16[512,768]{1,0:T(8,128)(2,1)}, f32[512,768]{1,0:T(8,128)}, f32[512,12]{1,0:T(8,128)}, bf16[512,768]{1,0:T(8,128)(2,1)}, f32[768,768]{1,0:T(...) custom-call(bf16[8,2,128,768]{3,2,1,0:T(8,128)(2,1)} %all-to-all-done.3.back, f32[512,768]{1,0:T(8,128)} %get-tuple-element.206.resid, ...), custom_call_target="tpu_custom_call" | custom-call | flops 1 | tf_op jit(solution)/shard_map/pallas_call | solution.py:311
  410.3 9.4 %collective-permute-start.34 = (bf16[256,768]{1,0:T(8,128)(2,1)}, bf16[256,768]{1,0:T(8,128)(2,1)}, u32[]{:S(2)}, u32[]{:S(2)}) collective-permute-start(bf16[256,768]{1,0:T(8,128)(2,1)} %get-tuple-element.320), channel_id=1, source_target_pairs={{0,0},{8,1},{1,4},{9,5},{4,8},{12,9},{5,12},{13,13},{16,16},{24,17... | collective-permute-start | bytes 1179656 | tf_op jit(solution)/shard_map/ppermute | solution.py:812
  427.4 18.2 %shard_map.241 = (f32[512,768]{1,0:T(8,128)}, bf16[512,2304]{1,0:T(8,128)(2,1)}, bf16[512,768]{1,0:T(8,128)(2,1)}, f32[8,768]{1,0:T(8,128)}) custom-call(bf16[512,2304]{1,0:T(8,128)(2,1)} %get-tuple-element.214.qkv, bf16[512,768]{1,0:T(8,128)(2,1)} %get-tuple-element.215.agrad, f32[16,512]{1,0:T(8,128)} %get-tuple-element.216.lse, s32[1024,1]{1,0:T(8,128)} %copy.160.seg_col, ...), custom_call_target="tpu_custom_call" | custom-call | flops 1 | tf_op jit(solution)/shard_map/pallas_call | solution.py:400
  445.6 11.0 %shard_map.242 = (bf16[384,2560]{1,0:T(8,128)(2,1)}, bf16[384,2560]{1,0:T(8,128)(2,1)}) custom-call(s32[1]{0:T(128)} %bitcast.84.refs_0_, bf16[512,768]{1,0:T(8,128)(2,1)} %get-tuple-element.224.refs_1_, bf16[512,768]{1,0:T(8,128)(2,1)} %get-tuple-element.225.refs_2_, bf16[512,2304]{1,0:T(8,128)(2,1)} %get-tuple-element.226.refs_3_, ...), custom_call_target="tpu_custom_call" | custom-call | flops 1 | tf_op jit(solution)/shard_map/pallas_call | solution.py:464
  478.3 5.9 %collective-permute-done.39 = bf16[4,2,48,640]{3,2,1,0:T(8,128)(2,1)S(1)} collective-permute-done((bf16[4,2,48,640]{3,2,1,0:T(8,128)(2,1)S(1)}, bf16[4,2,48,640]{3,2,1,0:T(8,128)(2,1)S(1)}, u32[]{:S(2)}, u32[]{:S(2)}) %collective-permute-start.39) | collective-permute-done | bytes 491552 | tf_op jit(solution)/shard_map/ppermute | solution.py:682
  (282 shorter events, 191.3 us)
Async XLA Ops:
  23.6 32.0 %collective-permute-start.12 = (bf16[96,3072]{1,0:T(8,128)(2,1)S(1)}, bf16[96,3072]{1,0:T(8,128)(2,1)}, u32[]{:S(2)}, u32[]{:S(2)}) collective-permute-start(bf16[96,3072]{1,0:T(8,128)(2,1)S(1)} %dynamic-slice_bitcast_fusion.14), channel_id=1, source_target_pairs={{0,16},{1,24},{4,17},{5,25},{8,20},{9,28},{12,21},{13,29},{16,0},{... | collective-permute-start | bytes 1769480 | tf_op jit(solution)/shard_map/ppermute | solution.py:715
  76.3 39.7 %collective-permute-start.13 = (bf16[96,3072]{1,0:T(8,128)(2,1)}, bf16[96,3072]{1,0:T(8,128)(2,1)}, u32[]{:S(2)}, u32[]{:S(2)}) collective-permute-start(bf16[96,3072]{1,0:T(8,128)(2,1)} %get-tuple-element.326), channel_id=1, source_target_pairs={{0,0},{1,8},{4,1},{5,9},{8,4},{9,12},{12,5},{13,13},{16,16},{17,24... | collective-permute-start | bytes 1769480 | tf_op jit(solution)/shard_map/ppermute | solution.py:715
  79.4 36.6 %collective-permute-start.14 = (bf16[96,3072]{1,0:T(8,128)(2,1)}, bf16[96,3072]{1,0:T(8,128)(2,1)}, u32[]{:S(2)}, u32[]{:S(2)}) collective-permute-start(bf16[96,3072]{1,0:T(8,128)(2,1)} %get-tuple-element.324), channel_id=1, source_target_pairs={{0,0},{1,8},{4,1},{5,9},{8,4},{9,12},{12,5},{13,13},{16,16},{17,24... | collective-permute-start | bytes 1769480 | tf_op jit(solution)/shard_map/ppermute | solution.py:715
  82.6 33.4 %collective-permute-start.15 = (bf16[96,3072]{1,0:T(8,128)(2,1)}, bf16[96,3072]{1,0:T(8,128)(2,1)}, u32[]{:S(2)}, u32[]{:S(2)}) collective-permute-start(bf16[96,3072]{1,0:T(8,128)(2,1)} %get-tuple-element.325), channel_id=1, source_target_pairs={{0,4},{1,12},{4,5},{5,13},{8,0},{9,8},{12,1},{13,9},{16,20},{17,28... | collective-permute-start | bytes 1769480 | tf_op jit(solution)/shard_map/ppermute | solution.py:715
  84.1 31.9 %collective-permute-start.17 = (bf16[96,3072]{1,0:T(8,128)(2,1)}, bf16[96,3072]{1,0:T(8,128)(2,1)}, u32[]{:S(2)}, u32[]{:S(2)}) collective-permute-start(bf16[96,3072]{1,0:T(8,128)(2,1)} %get-tuple-element.323), channel_id=1, source_target_pairs={{0,16},{1,24},{4,17},{5,25},{8,20},{9,28},{12,21},{13,29},{16,0},{... | collective-permute-start | bytes 1769480 | tf_op jit(solution)/shard_map/ppermute | solution.py:715
  112.3 89.5 %all-to-all-start = ((bf16[8,2,128,768]{3,2,1,0:T(8,128)(2,1)}), bf16[8,2,128,768]{3,2,1,0:T(8,128)(2,1)S(1)}, u32[]{:S(2)}, u32[]{:S(2)}) async-start(bf16[8,2,128,768]{3,2,1,0:T(8,128)(2,1)} %get-tuple-element.150), calls=%async_computation | async-start | bytes 6291456 | tf_op jit(solution)/shard_map/all_to_all | solution.py:900
  117.4 61.2 %collective-permute-start.20 = (bf16[96,3072]{1,0:T(8,128)(2,1)S(1)}, bf16[96,3072]{1,0:T(8,128)(2,1)S(1)}, u32[]{:S(2)}, u32[]{:S(2)}) collective-permute-start(bf16[96,3072]{1,0:T(8,128)(2,1)S(1)} %get-tuple-element.322), channel_id=1, source_target_pairs={{0,4},{1,12},{4,5},{5,13},{8,0},{9,8},{12,1},{13,9},{16,20},{17,28... | collective-permute-start | bytes 1769480 | tf_op jit(solution)/shard_map/ppermute | solution.py:715
  120.4 70.8 %collective-permute-start.22 = (bf16[96,3072]{1,0:T(8,128)(2,1)S(1)}, bf16[96,3072]{1,0:T(8,128)(2,1)S(1)}, u32[]{:S(2)}, u32[]{:S(2)}) collective-permute-start(bf16[96,3072]{1,0:T(8,128)(2,1)S(1)} %get-tuple-element.321), channel_id=1, source_target_pairs={{0,20},{1,28},{4,21},{5,29},{8,16},{9,24},{12,17},{13,25},{16,4},{... | collective-permute-start | bytes 1769480 | tf_op jit(solution)/shard_map/ppermute | solution.py:715
  121.0 78.9 %collective-permute-start.21 = (bf16[96,3072]{1,0:T(8,128)(2,1)S(1)}, bf16[96,3072]{1,0:T(8,128)(2,1)S(1)}, u32[]{:S(2)}, u32[]{:S(2)}) collective-permute-start(bf16[96,3072]{1,0:T(8,128)(2,1)S(1)} %dynamic-slice_bitcast_fusion.8), channel_id=1, source_target_pairs={{0,20},{1,28},{4,21},{5,29},{8,16},{9,24},{12,17},{13,25},{16,4},{... | collective-permute-start | bytes 1769480 | tf_op jit(solution)/shard_map/ppermute | solution.py:715
  125.3 74.6 %collective-permute-start.18 = (bf16[96,3072]{1,0:T(8,128)(2,1)}, bf16[96,3072]{1,0:T(8,128)(2,1)S(1)}, u32[]{:S(2)}, u32[]{:S(2)}) collective-permute-start(bf16[96,3072]{1,0:T(8,128)(2,1)} %collective-permute-done.13.refs_1_), channel_id=1, source_target_pairs={{0,1},{1,0},{2,3},{3,2},{4,5},{5,4},{6,7},{7,6},{8,9},{9,8},{10,11... | collective-permute-start | bytes 1769480 | tf_op jit(solution)/shard_map/ppermute | solution.py:682
  125.3 74.6 %collective-permute-start.19 = (bf16[96,3072]{1,0:T(8,128)(2,1)}, bf16[96,3072]{1,0:T(8,128)(2,1)S(1)}, u32[]{:S(2)}, u32[]{:S(2)}) collective-permute-start(bf16[96,3072]{1,0:T(8,128)(2,1)} %collective-permute-done.14.refs_2_), channel_id=1, source_target_pairs={{0,1},{1,0},{2,3},{3,2},{4,5},{5,4},{6,7},{7,6},{8,9},{9,8},{10,11... | collective-permute-start | bytes 1769480 | tf_op jit(solution)/shard_map/ppermute | solution.py:682
  203.4 48.7 %all-to-all-start.2 = ((bf16[8,2,128,768]{3,2,1,0:T(8,128)(2,1)}), bf16[8,2,128,768]{3,2,1,0:T(8,128)(2,1)}, u32[]{:S(2)}, u32[]{:S(2)}) async-start(bf16[8,2,128,768]{3,2,1,0:T(8,128)(2,1)} %get-tuple-element.179), calls=%async_computation.2 | async-start | bytes 6291456 | tf_op jit(solution)/shard_map/all_to_all | solution.py:900
  252.2 52.4 %all-to-all-start.1 = ((bf16[8,2,128,768]{3,2,1,0:T(8,128)(2,1)}), bf16[8,2,128,768]{3,2,1,0:T(8,128)(2,1)S(1)}, u32[]{:S(2)}, u32[]{:S(2)}) async-start(bf16[8,2,128,768]{3,2,1,0:T(8,128)(2,1)} %get-tuple-element.178), calls=%async_computation.1 | async-start | bytes 6291456 | tf_op jit(solution)/shard_map/all_to_all | solution.py:906
  306.3 76.6 %all-to-all-start.3 = ((bf16[8,2,128,768]{3,2,1,0:T(8,128)(2,1)}), bf16[8,2,128,768]{3,2,1,0:T(8,128)(2,1)}, u32[]{:S(2)}, u32[]{:S(2)}) async-start(bf16[8,2,128,768]{3,2,1,0:T(8,128)(2,1)} %get-tuple-element.196), calls=%async_computation.3 | async-start | bytes 6291456 | tf_op jit(solution)/shard_map/all_to_all | solution.py:906
  333.3 73.9 %collective-permute-start.33 = (bf16[4,256,768]{2,1,0:T(8,128)(2,1)}, bf16[4,256,768]{2,1,0:T(8,128)(2,1)}, u32[]{:S(2)}, u32[]{:S(2)}) collective-permute-start(bf16[4,256,768]{2,1,0:T(8,128)(2,1)} %dynamic-slice_bitcast_fusion.1), channel_id=1, source_target_pairs={{0,1},{1,0},{2,3},{3,2},{4,5},{5,4},{6,7},{7,6},{8,9},{9,8},{10,11... | collective-permute-start | bytes 4718600 | tf_op jit(solution)/shard_map/ppermute | solution.py:682
  336.1 72.9 %collective-permute-start.29 = (bf16[2,96,2048]{2,1,0:T(8,128)(2,1)}, bf16[2,96,2048]{2,1,0:T(8,128)(2,1)S(1)}, u32[]{:S(2)}, u32[]{:S(2)}) collective-permute-start(bf16[2,96,2048]{2,1,0:T(8,128)(2,1)} %get-tuple-element.311), channel_id=1, source_target_pairs={{0,0},{8,1},{1,4},{9,5},{4,8},{12,9},{5,12},{13,13},{16,16},{24,17... | collective-permute-start | bytes 2359304 | tf_op jit(solution)/shard_map/ppermute | solution.py:812
  339.7 69.4 %collective-permute-start.30 = (bf16[2,96,2048]{2,1,0:T(8,128)(2,1)}, bf16[2,96,2048]{2,1,0:T(8,128)(2,1)S(1)}, u32[]{:S(2)}, u32[]{:S(2)}) collective-permute-start(bf16[2,96,2048]{2,1,0:T(8,128)(2,1)} %get-tuple-element.310), channel_id=1, source_target_pairs={{4,0},{12,1},{5,4},{13,5},{0,8},{8,9},{1,12},{9,13},{20,16},{28,17... | collective-permute-start | bytes 2359304 | tf_op jit(solution)/shard_map/ppermute | solution.py:812
  341.3 67.8 %collective-permute-start.31 = (bf16[2,96,2048]{2,1,0:T(8,128)(2,1)}, bf16[2,96,2048]{2,1,0:T(8,128)(2,1)S(1)}, u32[]{:S(2)}, u32[]{:S(2)}) collective-permute-start(bf16[2,96,2048]{2,1,0:T(8,128)(2,1)} %get-tuple-element.309), channel_id=1, source_target_pairs={{16,0},{24,1},{17,4},{25,5},{20,8},{28,9},{21,12},{29,13},{0,16},{... | collective-permute-start | bytes 2359304 | tf_op jit(solution)/shard_map/ppermute | solution.py:812
  347.3 61.8 %collective-permute-start.32 = (bf16[2,96,2048]{2,1,0:T(8,128)(2,1)}, bf16[2,96,2048]{2,1,0:T(8,128)(2,1)}, u32[]{:S(2)}, u32[]{:S(2)}) collective-permute-start(bf16[2,96,2048]{2,1,0:T(8,128)(2,1)} %get-tuple-element.308), channel_id=1, source_target_pairs={{20,0},{28,1},{21,4},{29,5},{16,8},{24,9},{17,12},{25,13},{4,16},{... | collective-permute-start | bytes 2359304 | tf_op jit(solution)/shard_map/ppermute | solution.py:812
  407.2 51.5 %collective-permute-start.48 = (bf16[8,48,768]{2,1,0:T(8,128)(2,1)}, bf16[8,48,768]{2,1,0:T(8,128)(2,1)}, u32[]{:S(2)}, u32[]{:S(2)}) collective-permute-start(bf16[8,48,768]{2,1,0:T(8,128)(2,1)} %dynamic-slice_bitcast_fusion.6), channel_id=1, source_target_pairs={{0,1},{1,0},{2,3},{3,2},{4,5},{5,4},{6,7},{7,6},{8,9},{9,8},{10,11... | collective-permute-start | bytes 1769480 | tf_op jit(solution)/shard_map/ppermute | solution.py:682
  410.3 46.3 %collective-permute-start.34 = (bf16[256,768]{1,0:T(8,128)(2,1)}, bf16[256,768]{1,0:T(8,128)(2,1)}, u32[]{:S(2)}, u32[]{:S(2)}) collective-permute-start(bf16[256,768]{1,0:T(8,128)(2,1)} %get-tuple-element.320), channel_id=1, source_target_pairs={{0,0},{8,1},{1,4},{9,5},{4,8},{12,9},{5,12},{13,13},{16,16},{24,17... | collective-permute-start | bytes 1179656 | tf_op jit(solution)/shard_map/ppermute | solution.py:812
  419.7 36.9 %collective-permute-start.35 = (bf16[256,768]{1,0:T(8,128)(2,1)}, bf16[256,768]{1,0:T(8,128)(2,1)}, u32[]{:S(2)}, u32[]{:S(2)}) collective-permute-start(bf16[256,768]{1,0:T(8,128)(2,1)} %get-tuple-element.319), channel_id=1, source_target_pairs={{4,0},{12,1},{5,4},{13,5},{0,8},{8,9},{1,12},{9,13},{20,16},{28,17... | collective-permute-start | bytes 1179656 | tf_op jit(solution)/shard_map/ppermute | solution.py:812
  420.4 36.2 %collective-permute-start.36 = (bf16[256,768]{1,0:T(8,128)(2,1)}, bf16[256,768]{1,0:T(8,128)(2,1)}, u32[]{:S(2)}, u32[]{:S(2)}) collective-permute-start(bf16[256,768]{1,0:T(8,128)(2,1)} %get-tuple-element.318), channel_id=1, source_target_pairs={{16,0},{24,1},{17,4},{25,5},{20,8},{28,9},{21,12},{29,13},{0,16},{... | collective-permute-start | bytes 1179656 | tf_op jit(solution)/shard_map/ppermute | solution.py:812
  421.8 34.8 %collective-permute-start.37 = (bf16[256,768]{1,0:T(8,128)(2,1)}, bf16[256,768]{1,0:T(8,128)(2,1)}, u32[]{:S(2)}, u32[]{:S(2)}) collective-permute-start(bf16[256,768]{1,0:T(8,128)(2,1)} %get-tuple-element.317), channel_id=1, source_target_pairs={{20,0},{28,1},{21,4},{29,5},{16,8},{24,9},{17,12},{25,13},{4,16},{... | collective-permute-start | bytes 1179656 | tf_op jit(solution)/shard_map/ppermute | solution.py:812
  (73 other events, 803.7 us)

commit v5 on v4

--- a/solution.py
+++ b/solution.py
@@ -420,7 +420,7 @@
 
 def mixer_wgrad_body(parts, groups, *refs):
     core, acts, grads, gains = refs[0], refs[1 : 1 + parts], refs[1 + parts : 1 + 2 * parts], refs[1 + 2 * parts : 1 + 3 * parts]
-    small, rows, give, keep, turned, last = refs[1 + 3 * parts :]
+    out_w, small, rows, give, keep, turned, last = refs[1 + 3 * parts :]
     step, half = pl.program_id(0), D // 2
     chunk = half // groups
 
@@ -443,7 +443,13 @@
         give[...] = made[:half, :]
         keep[...] = made[half:, :]
 
-    @pl.when(step == 9)
+    @pl.when((step >= 9) & (step < 12))
+    def _():
+        scattered(last, slice(0, 256), out_w[...].astype(BF))
+        give[...] = last[:half, :]
+        keep[...] = last[half:, :]
+
+    @pl.when(step == 12)
     def _():
         gain_one = sum(v[0:1, :] for v in gains)
         line = lax.broadcasted_iota(jnp.int32, (128, D), 0)
@@ -451,30 +457,30 @@
         for i, row in enumerate((rows[0:1, :], rows[1:2, :], gain_one, rows[2:3, :])):
             stacked += jnp.where(line == 16 + i, row, 0.0)
         scattered(last, slice(0, 128), (small[...] + stacked.T).astype(BF))
-        give[:, :128] = last[:half, :]
-        keep[:, :128] = last[half:, :]
+        give[:, :128] = last[:half, :128]
+        keep[:, :128] = last[half:, :128]
         give[:, 128:] = jnp.zeros((half, 128), BF)
         keep[:, 128:] = jnp.zeros((half, 128), BF)
 
 
-def mixer_wgrad(acts, grads, gains, small, rows, groups, core):
+def mixer_wgrad(acts, grads, gains, out_w, small, rows, groups, core):
     parts = len(acts)
     half = pl.BlockSpec((D // 2, 256), lambda i: (0, i))
-    out = jax.ShapeDtypeStruct((D // 2, 3 * D + 256), BF)
+    out = jax.ShapeDtypeStruct((D // 2, 4 * D + 256), BF)
     return pl.pallas_call(
         functools.partial(mixer_wgrad_body, parts, groups),
-        grid=(10,),
+        grid=(13,),
         in_specs=[pl.BlockSpec(memory_space=pltpu.SMEM)]
         + [fixed((SEQ, D))] * parts
         + [pl.BlockSpec((SEQ, 256), lambda i: (0, jnp.minimum(i, 8)))] * parts
         + [fixed((8, D))] * parts
-        + [fixed((D, 128)), fixed((8, D))],
+        + [pl.BlockSpec((D, 256), lambda i: (0, jnp.clip(i - 9, 0, 2))), fixed((D, 128)), fixed((8, D))],
         out_specs=[half, half],
         out_shape=[out, out],
-        scratch_shapes=[pltpu.VMEM((D, parts * SEQ), BF), pltpu.VMEM((D, 128), BF)],
+        scratch_shapes=[pltpu.VMEM((D, parts * SEQ), BF), pltpu.VMEM((D, 256), BF)],
         compiler_params=kernel_params(),
         cost_estimate=lasting(0),
-    )(jnp.stack([core]).astype(jnp.int32), *acts, *grads, *gains, small, rows)
+    )(jnp.stack([core]).astype(jnp.int32), *acts, *grads, *gains, out_w, small, rows)
 
 
 def tables(tokens, cotangent, prev_logits, routes, capacity, segments, positions):
@@ -748,11 +754,6 @@
     def split(self):
         return 8, lax.axis_index("core")
 
-    def halves(self, total):
-        c = lax.axis_index("core")
-        total = total.reshape(8, 2, total.shape[0] // 16, total.shape[1])
-        return pick(total, 1 - c, 1), pick(total, c, 1)
-
     def reduce_first(self, give, keep):
         z, y, x, c = self.spot()
         width = give.shape[-1] // 2
@@ -837,9 +838,6 @@
 
     def split(self):
         return 1, jnp.int32(1)
-
-    def halves(self, total):
-        return jnp.split(total, 2)
 
     def reduce_first(self, give, keep):
         return jnp.concatenate([give, keep]), None
@@ -915,20 +913,20 @@
             sums = (out_w, small_w, rows_w)
             firsts.append(first)
             if i == parts - 1:
-                held = (gate_up_got, down_sums, first[1], [v[3] for v in lasts])
-                gate_up_got, down_sums, first[1], _ = lax.optimization_barrier(held)
-                down_got = plan.scatter_send(down_sums, 0)
+                held = (down_sums, first[1], [v[3] for v in lasts])
+                down_sums, first[1], _ = lax.optimization_barrier(held)
             lasts.append(attention_back(i, kept[i], first[1], first[3], t, packed, vecs))
             if i == 0:
                 returned[-1], sums, _ = lax.optimization_barrier((returned[-1], sums, lasts[0][3]))
-        out_total = plan.reduce_last(*plan.reduce_first(*plan.halves(sums[0].astype(BF))))
-        acts = [v[2] for v in lasts]
+        held = ([v[2] for v in lasts], gate_up_got, down_sums)
+        acts, gate_up_got, down_sums = lax.optimization_barrier(held)
         halves = mixer_wgrad(
-            acts, [v[1] for v in lasts], [v[3] for v in lasts], sums[1], sums[2], *plan.split()
+            acts, [v[1] for v in lasts], [v[3] for v in lasts], *sums, *plan.split()
         )
-        halves, down_got = lax.optimization_barrier((halves, down_got))
+        down_got = plan.scatter_send(down_sums, 0)
+        near = plan.reduce_first(*halves)
+        total = plan.reduce_last(*near)
         down_total = plan.scatter_end(down_got, 0)
-        total = plan.reduce_last(*plan.reduce_first(*halves))
         gate_up_total = plan.scatter_end(gate_up_got, 1)
         gate_up_total = jnp.concatenate([gate_up_total[:, 0], gate_up_total[:, 1]], axis=2)
         return (
@@ -936,11 +934,11 @@
             jnp.concatenate([v[0] for v in lasts]),
             jnp.concatenate([v[2] for v in firsts]),
             total[:, : 3 * D],
-            out_total,
-            total[:, 3 * D : 3 * D + 16],
-            total[:, 3 * D + 16 : 3 * D + 18],
-            total[:, 3 * D + 18],
-            total[:, 3 * D + 19],
+            total[:, 3 * D : 4 * D],
+            total[:, 4 * D : 4 * D + 16],
+            total[:, 4 * D + 16 : 4 * D + 18],
+            total[:, 4 * D + 18],
+            total[:, 4 * D + 19],
             gate_up_total,
             down_total,
         )

time: 533 us -> 537 us (level)
  waiting for transfers between devices: 100 us -> 122 us
  starting transfers between devices: 129 us -> 117 us
    ppermute x33 -> x26, starting transfers between devices: 40.5 us -> 25.6 us  [swap(): return lax.ppermute(value, axis, [(0, 1), (1, 0)])]
    ppermute x8, waiting for transfers between devices: 0.02 us -> 13.1 us  [scatter_send(): lax.ppermute(pick(parts, here ^ turn, axis), self.route_axes, back)]
    ppermute x33 -> x26, waiting for transfers between devices: 29.8 us -> 41.4 us  [swap(): return lax.ppermute(value, axis, [(0, 1), (1, 0)])]
    ppermute x8, starting transfers between devices: 27.7 us -> 38.1 us  [scatter_send(): lax.ppermute(pick(parts, here ^ turn, axis), self.route_axes, back)]
    ppermute x9 -> x6, starting transfers between devices: 15.9 us -> 8.25 us  [along(): lax.ppermute(value, ('half', 'low'), [(i, i ^ turn) for i in range(4)])]
    squeeze x12 -> x10, local copies, waits for them, and re-layouts: 12.9 us -> 11 us  [pick(): return lax.dynamic_index_in_dim(value, index, axis, False)]
  transfers between devices with their start and end apart: 62 -> 52, of which waited for: 19 -> 18; matrix products, arithmetic and copies ran while one was open for 10% -> 9% of each run, Pallas kernels for 41% -> 38%
where the time goes in v5:
time: 537 us; the launch traced here: 527 us
  Pallas kernels  222 us (41%)
  waiting for transfers between devices  122 us (23%)
  starting transfers between devices  117 us (22%)
  local copies, waits for them, and re-layouts  36.5 us (7%)
  other arithmetic  27.5 us (5%)
    ppermute x8, waiting for transfers between devices, send(): return lax.ppermute(mine, self.route_axes, self.routes[turn])  62.3 us
    pallas_call x2, Pallas kernels, expert_rows(): pl.pallas_call(expert_rows_body, grid=(steps,), in_specs=[pl.BlockSpec((n...  57.2 us
    ppermute x26, waiting for transfers between devices, swap(): return lax.ppermute(value, axis, [(0, 1), (1, 0)])  41.4 us
    pallas_call x2, Pallas kernels, forward_part(): pl.pallas_call(forward_body, grid=(1,), in_specs=[seq_block(D, part), seq...  40.5 us
    ppermute x8, starting transfers between devices, scatter_send(): lax.ppermute(pick(parts, here ^ turn, axis), self.route_axes, back)  38.1 us
    pallas_call x2, Pallas kernels, attention_back(): pl.pallas_call(attention_back_body, grid=(1,), in_specs=[fixed((SEQ, 3 *...  36 us
    pallas_call x2, Pallas kernels, combine_part(): pl.pallas_call(body, grid=(2,), in_specs=[fixed((EXPERTS, 2, CAP, D)), ti...  30 us
    ppermute x8, starting transfers between devices, send(): return lax.ppermute(mine, self.route_axes, self.routes[turn])  27.2 us
  transfers between devices with their start and end apart: 52, of which 18 were waited for; matrix products, arithmetic and copies ran while one was open for 9% of the time, Pallas kernels for 38%

profile of v5, /device:TPU:1, one launch (start us, length us, event | category | flops | bytes accessed | tf_op | source)
XLA Modules:
  0.0 527.2 jit_solution(6370847640496365006)
XLA Ops:
  38.1 7.8 %collective-permute-start.7 = (bf16[192,1664]{1,0:T(8,128)(2,1)S(1)}, bf16[192,1664]{1,0:T(8,128)(2,1)}, u32[]{:S(2)}, u32[]{:S(2)}) collective-permute-start(bf16[192,1664]{1,0:T(8,128)(2,1)S(1)} %pad_maximum_fusion.5.refs_1_), channel_id=1, source_target_pairs={{0,1},{1,0},{2,3},{3,2},{4,5},{5,4},{6,7},{7,6},{8,9},{9,8},{10,11... | collective-permute-start | bytes 1916936 | tf_op jit(solution)/shard_map/ppermute | solution.py:688
  47.4 8.3 %collective-permute-done.12.refs_5_ = bf16[96,3072]{1,0:T(8,128)(2,1)} collective-permute-done((bf16[96,3072]{1,0:T(8,128)(2,1)S(1)}, bf16[96,3072]{1,0:T(8,128)(2,1)}, u32[]{:S(2)}, u32[]{:S(2)}) %collective-permute-start.12) | collective-permute-done | bytes 589856 | tf_op jit(solution)/shard_map/ppermute | solution.py:721
  68.1 5.8 %shard_map.230.w_qkv.w_out.w_small.refs_7_.refs_8_ = bf16[768,3328]{1,0:T(8,128)(2,1)} custom-call(s32[80]{0:T(128)} %stack.300.refs_0_, bf16[192,1664]{1,0:T(8,128)(2,1)} %copy-done.8, bf16[192,1664]{1,0:T(8,128)(2,1)} %collective-permute-done.3.refs_2_, bf16[192,1664]{1,0:T(8,128)(2,1)} %collective-permute-done.4.refs_3_, bf16[192,896]{1,0:T(8,128)(2,1)} %copy-done.24, ...), custom_call_target="tpu_custom_call" | custom-call | flops 1 | tf_op jit(solution)/shard_map/pallas_call | solution.py:646
  84.1 7.3 %collective-permute-start.17 = (bf16[96,3072]{1,0:T(8,128)(2,1)}, bf16[96,3072]{1,0:T(8,128)(2,1)}, u32[]{:S(2)}, u32[]{:S(2)}) collective-permute-start(bf16[96,3072]{1,0:T(8,128)(2,1)} %get-tuple-element.316), channel_id=1, source_target_pairs={{0,16},{1,24},{4,17},{5,25},{8,20},{9,28},{12,21},{13,29},{16,0},{... | collective-permute-start | bytes 1769480 | tf_op jit(solution)/shard_map/ppermute | solution.py:721
  92.1 20.3 %shard_map.231 = (bf16[8,2,128,768]{3,2,1,0:T(8,128)(2,1)}, bf16[512,2304]{1,0:T(8,128)(2,1)}, bf16[512,768]{1,0:T(8,128)(2,1)}, f32[512,768]{1,0:T(8,128)}, f32[16,512]{1,0:T(8,128)}, /*index=5*/f32[512,128]{1,0:T(8,128)}) custom-call(bf16[1024,768]{1,0:T(8,128)(2,1)} %tok.3, bf16[1024,768]{1,0:T(8,128)(2,1)} %cot.2, bf16[1024,128]{1,0:T(8,128)(2,1)} %pad.4.prev, ...), custom_call_target="tpu_custom_call" | custom-call | flops 99999997952 | tf_op jit(solution)/shard_map/pallas_call | solution.py:180
  125.7 20.2 %shard_map.232 = (bf16[8,2,128,768]{3,2,1,0:T(8,128)(2,1)}, bf16[512,2304]{1,0:T(8,128)(2,1)}, bf16[512,768]{1,0:T(8,128)(2,1)}, f32[512,768]{1,0:T(8,128)}, f32[16,512]{1,0:T(8,128)}, /*index=5*/f32[512,128]{1,0:T(8,128)}) custom-call(bf16[1024,768]{1,0:T(8,128)(2,1)} %tok.3, bf16[1024,768]{1,0:T(8,128)(2,1)} %cot.2, bf16[1024,128]{1,0:T(8,128)(2,1)} %pad.4.prev, ...), custom_call_target="tpu_custom_call" | custom-call | flops 99999997952 | tf_op jit(solution)/shard_map/pallas_call | solution.py:180
  146.0 32.7 %collective-permute-done.20.refs_4_ = bf16[96,3072]{1,0:T(8,128)(2,1)S(1)} collective-permute-done((bf16[96,3072]{1,0:T(8,128)(2,1)S(1)}, bf16[96,3072]{1,0:T(8,128)(2,1)S(1)}, u32[]{:S(2)}, u32[]{:S(2)}) %collective-permute-start.20) | collective-permute-done | bytes 589856 | tf_op jit(solution)/shard_map/ppermute | solution.py:721
  178.6 12.6 %collective-permute-done.22.refs_8_ = bf16[96,3072]{1,0:T(8,128)(2,1)S(1)} collective-permute-done((bf16[96,3072]{1,0:T(8,128)(2,1)S(1)}, bf16[96,3072]{1,0:T(8,128)(2,1)S(1)}, u32[]{:S(2)}, u32[]{:S(2)}) %collective-permute-start.22) | collective-permute-done | bytes 589856 | tf_op jit(solution)/shard_map/ppermute | solution.py:721
  191.3 8.8 %collective-permute-done.21.refs_7_ = bf16[96,3072]{1,0:T(8,128)(2,1)S(1)} collective-permute-done((bf16[96,3072]{1,0:T(8,128)(2,1)S(1)}, bf16[96,3072]{1,0:T(8,128)(2,1)S(1)}, u32[]{:S(2)}, u32[]{:S(2)}) %collective-permute-start.21) | collective-permute-done | bytes 589856 | tf_op jit(solution)/shard_map/ppermute | solution.py:721
  214.8 8.6 %shard_map.233 = (bf16[768,4096]{1,0:T(8,128)(2,1)}, bf16[2048,768]{1,0:T(8,128)(2,1)}) custom-call(s32[112]{0:T(128)} %stack.341.refs_0_, bf16[96,3072]{1,0:T(8,128)(2,1)} %collective-permute-done.13.refs_1_, bf16[96,3072]{1,0:T(8,128)(2,1)} %collective-permute-done.14.refs_2_, bf16[96,3072]{1,0:T(8,128)(2,1)} %collective-permute-done.15.refs_3_, ...), custom_call_target="tpu_custom_call" | custom-call | flops 1 | tf_op jit(solution)/shard_map/pallas_call | solution.py:646
  223.4 28.6 %shard_map.234 = (bf16[1024,2048]{1,0:T(8,128)(2,1)}, bf16[1024,2048]{1,0:T(8,128)(2,1)}, bf16[1024,2048]{1,0:T(8,128)(2,1)}, bf16[8,2,128,768]{3,2,1,0:T(8,128)(2,1)}) custom-call(bf16[8,2,128,768]{3,2,1,0:T(8,128)(2,1)} %copy-done, bf16[8,2,128,768]{3,2,1,0:T(8,128)(2,1)} %copy-done, bf16[768,4096]{1,0:T(8,128)(2,1)} %get-tuple-element.173.wg_ref.wu_ref, ...), custom_call_target="tpu_custom_call" | custom-call | flops 28000000000 | tf_op jit(solution)/shard_map/pallas_call | solution.py:553
  257.1 28.6 %shard_map.235 = (bf16[1024,2048]{1,0:T(8,128)(2,1)}, bf16[1024,2048]{1,0:T(8,128)(2,1)}, bf16[1024,2048]{1,0:T(8,128)(2,1)}, bf16[8,2,128,768]{3,2,1,0:T(8,128)(2,1)}) custom-call(bf16[8,2,128,768]{3,2,1,0:T(8,128)(2,1)} %all-to-all-done.2.x_ref.g_ref.refs_1_.refs_3_, bf16[8,2,128,768]{3,2,1,0:T(8,128)(2,1)} %all-to-all-done.2.x_ref.g_ref.refs_1_.refs_3_, ...), custom_call_target="tpu_custom_call" | custom-call | flops 28000000000 | tf_op jit(solution)/shard_map/pallas_call | solution.py:553
  285.6 19.1 %shard_map.236 = bf16[2,768,2048]{2,1,0:T(8,128)(2,1)} custom-call(bf16[8,2,128,768]{3,2,1,0:T(8,128)(2,1)} %copy-done, bf16[8,2,128,768]{3,2,1,0:T(8,128)(2,1)} %all-to-all-done.2.x_ref.g_ref.refs_1_.refs_3_, bf16[1024,2048]{1,0:T(8,128)(2,1)} %get-tuple-element.180.refs_2_, bf16[1024,2048]{1,0:T(8,128)(2,1)} %get-tuple-element.181.refs_3_, ...), custom_call_target="tpu_custom_call" | custom-call | flops 1 | tf_op jit(solution)/shard_map/pallas_call | solution.py:612
  316.3 11.0 %shard_map.237 = bf16[2048,768]{1,0:T(8,128)(2,1)} custom-call(bf16[1024,2048]{1,0:T(8,128)(2,1)} %get-tuple-element.185.refs_0_, bf16[1024,2048]{1,0:T(8,128)(2,1)} %get-tuple-element.186.refs_1_, bf16[8,2,128,768]{3,2,1,0:T(8,128)(2,1)} %copy-done, bf16[8,2,128,768]{3,2,1,0:T(8,128)(2,1)} %all-to-all-done.2.x_ref.g_ref.refs_1_.refs_3_), custom_call_target="tpu_custom_call" | custom-call | flops 10000000000 | tf_op jit(solution)/shard_map/pallas_call | solution.py:584
  341.8 6.1 %collective-permute-start.32 = (bf16[2,96,2048]{2,1,0:T(8,128)(2,1)}, bf16[2,96,2048]{2,1,0:T(8,128)(2,1)}, u32[]{:S(2)}, u32[]{:S(2)}) collective-permute-start(bf16[2,96,2048]{2,1,0:T(8,128)(2,1)} %get-tuple-element.303), channel_id=1, source_target_pairs={{16,0},{24,1},{17,4},{25,5},{20,8},{28,9},{21,12},{29,13},{0,16},{... | collective-permute-start | bytes 2359304 | tf_op jit(solution)/shard_map/ppermute | solution.py:813
  350.0 14.4 %shard_map.238 = (bf16[512,768]{1,0:T(8,128)(2,1)}, f32[512,768]{1,0:T(8,128)}, f32[512,12]{1,0:T(8,128)}, bf16[512,768]{1,0:T(8,128)(2,1)}, f32[768,768]{1,0:T(...) custom-call(bf16[8,2,128,768]{3,2,1,0:T(8,128)(2,1)} %copy-done.1, f32[512,768]{1,0:T(8,128)} %get-tuple-element.188.refs_1_, ...), custom_call_target="tpu_custom_call" | custom-call | flops 1 | tf_op jit(solution)/shard_map/pallas_call | solution.py:311
  364.4 18.0 %shard_map.239 = (f32[512,768]{1,0:T(8,128)}, bf16[512,2304]{1,0:T(8,128)(2,1)}, bf16[512,768]{1,0:T(8,128)(2,1)}, f32[8,768]{1,0:T(8,128)}) custom-call(bf16[512,2304]{1,0:T(8,128)(2,1)} %get-tuple-element.197.qkv, bf16[512,768]{1,0:T(8,128)(2,1)} %get-tuple-element.198.agrad, f32[16,512]{1,0:T(8,128)} %get-tuple-element.199.lse, s32[1024,1]{1,0:T(8,128)} %copy.159.seg_col, ...), custom_call_target="tpu_custom_call" | custom-call | flops 1 | tf_op jit(solution)/shard_map/pallas_call | solution.py:400
  382.4 15.6 %shard_map.240 = (bf16[512,768]{1,0:T(8,128)(2,1)}, f32[512,768]{1,0:T(8,128)}, f32[512,12]{1,0:T(8,128)}, bf16[512,768]{1,0:T(8,128)(2,1)}, f32[768,768]{1,0:T(...) custom-call(bf16[8,2,128,768]{3,2,1,0:T(8,128)(2,1)} %all-to-all-done.3.back, f32[512,768]{1,0:T(8,128)} %get-tuple-element.203.resid, ...), custom_call_target="tpu_custom_call" | custom-call | flops 1 | tf_op jit(solution)/shard_map/pallas_call | solution.py:311
  399.8 18.0 %shard_map.241 = (f32[512,768]{1,0:T(8,128)}, bf16[512,2304]{1,0:T(8,128)(2,1)}, bf16[512,768]{1,0:T(8,128)(2,1)}, f32[8,768]{1,0:T(8,128)}) custom-call(bf16[512,2304]{1,0:T(8,128)(2,1)} %get-tuple-element.211.qkv, bf16[512,768]{1,0:T(8,128)(2,1)} %get-tuple-element.212.agrad, f32[16,512]{1,0:T(8,128)} %get-tuple-element.213.lse, s32[1024,1]{1,0:T(8,128)} %copy.159.seg_col, ...), custom_call_target="tpu_custom_call" | custom-call | flops 1 | tf_op jit(solution)/shard_map/pallas_call | solution.py:400
  417.9 13.6 %shard_map.242 = (bf16[384,3328]{1,0:T(8,128)(2,1)}, bf16[384,3328]{1,0:T(8,128)(2,1)}) custom-call(s32[1]{0:T(128)} %bitcast.80.refs_0_, bf16[512,768]{1,0:T(8,128)(2,1)} %get-tuple-element.224.refs_1_, bf16[512,768]{1,0:T(8,128)(2,1)} %get-tuple-element.225.refs_2_, bf16[512,2304]{1,0:T(8,128)(2,1)} %get-tuple-element.226.refs_3_, ...), custom_call_target="tpu_custom_call" | custom-call | flops 1 | tf_op jit(solution)/shard_map/pallas_call | solution.py:470
  438.8 9.8 %collective-permute-start.45 = (bf16[256,768]{1,0:T(8,128)(2,1)S(1)}, bf16[256,768]{1,0:T(8,128)(2,1)S(1)}, u32[]{:S(2)}, u32[]{:S(2)}) collective-permute-start(bf16[256,768]{1,0:T(8,128)(2,1)S(1)} %get-tuple-element.312), channel_id=1, source_target_pairs={{16,0},{24,1},{17,4},{25,5},{20,8},{28,9},{21,12},{29,13},{0,16},{... | collective-permute-start | bytes 1179656 | tf_op jit(solution)/shard_map/ppermute | solution.py:813
  453.6 17.5 %collective-permute-done.37 = bf16[4,48,1536]{2,1,0:T(8,128)(2,1)S(1)} collective-permute-done((bf16[4,48,1536]{2,1,0:T(8,128)(2,1)S(1)}, bf16[4,48,1536]{2,1,0:T(8,128)(2,1)S(1)}, u32[]{:S(2)}, u32[]{:S(2)}) %collective-permute-start.37) | collective-permute-done | bytes 589856 | tf_op jit(solution)/shard_map/ppermute | solution.py:688
  491.1 10.6 %collective-permute-start.47 = (bf16[256,768]{1,0:T(8,128)(2,1)S(1)}, bf16[256,768]{1,0:T(8,128)(2,1)S(1)}, u32[]{:S(2)}, u32[]{:S(2)}) collective-permute-start(bf16[256,768]{1,0:T(8,128)(2,1)S(1)} %get-tuple-element.311), channel_id=1, source_target_pairs={{20,0},{28,1},{21,4},{29,5},{16,8},{24,9},{17,12},{25,13},{4,16},{... | collective-permute-start | bytes 1179656 | tf_op jit(solution)/shard_map/ppermute | solution.py:813
  508.3 13.1 %collective-permute-done.46 = bf16[256,768]{1,0:T(8,128)(2,1)S(1)} collective-permute-done((bf16[256,768]{1,0:T(8,128)(2,1)S(1)}, bf16[256,768]{1,0:T(8,128)(2,1)S(1)}, u32[]{:S(2)}, u32[]{:S(2)}) %collective-permute-start.46) | collective-permute-done | bytes 393248 | tf_op jit(solution)/shard_map/ppermute | solution.py:813
  (248 shorter events, 168.8 us)
Async XLA Ops:
  23.6 32.0 %collective-permute-start.12 = (bf16[96,3072]{1,0:T(8,128)(2,1)S(1)}, bf16[96,3072]{1,0:T(8,128)(2,1)}, u32[]{:S(2)}, u32[]{:S(2)}) collective-permute-start(bf16[96,3072]{1,0:T(8,128)(2,1)S(1)} %dynamic-slice_bitcast_fusion.13), channel_id=1, source_target_pairs={{0,16},{1,24},{4,17},{5,25},{8,20},{9,28},{12,21},{13,29},{16,0},{... | collective-permute-start | bytes 1769480 | tf_op jit(solution)/shard_map/ppermute | solution.py:721
  38.1 30.0 %collective-permute-start.7 = (bf16[192,1664]{1,0:T(8,128)(2,1)S(1)}, bf16[192,1664]{1,0:T(8,128)(2,1)}, u32[]{:S(2)}, u32[]{:S(2)}) collective-permute-start(bf16[192,1664]{1,0:T(8,128)(2,1)S(1)} %pad_maximum_fusion.5.refs_1_), channel_id=1, source_target_pairs={{0,1},{1,0},{2,3},{3,2},{4,5},{5,4},{6,7},{7,6},{8,9},{9,8},{10,11... | collective-permute-start | bytes 1916936 | tf_op jit(solution)/shard_map/ppermute | solution.py:688
  76.3 39.7 %collective-permute-start.13 = (bf16[96,3072]{1,0:T(8,128)(2,1)}, bf16[96,3072]{1,0:T(8,128)(2,1)}, u32[]{:S(2)}, u32[]{:S(2)}) collective-permute-start(bf16[96,3072]{1,0:T(8,128)(2,1)} %get-tuple-element.319), channel_id=1, source_target_pairs={{0,0},{1,8},{4,1},{5,9},{8,4},{9,12},{12,5},{13,13},{16,16},{17,24... | collective-permute-start | bytes 1769480 | tf_op jit(solution)/shard_map/ppermute | solution.py:721
  79.4 36.6 %collective-permute-start.14 = (bf16[96,3072]{1,0:T(8,128)(2,1)}, bf16[96,3072]{1,0:T(8,128)(2,1)}, u32[]{:S(2)}, u32[]{:S(2)}) collective-permute-start(bf16[96,3072]{1,0:T(8,128)(2,1)} %get-tuple-element.317), channel_id=1, source_target_pairs={{0,0},{1,8},{4,1},{5,9},{8,4},{9,12},{12,5},{13,13},{16,16},{17,24... | collective-permute-start | bytes 1769480 | tf_op jit(solution)/shard_map/ppermute | solution.py:721
  82.6 33.4 %collective-permute-start.15 = (bf16[96,3072]{1,0:T(8,128)(2,1)}, bf16[96,3072]{1,0:T(8,128)(2,1)}, u32[]{:S(2)}, u32[]{:S(2)}) collective-permute-start(bf16[96,3072]{1,0:T(8,128)(2,1)} %get-tuple-element.318), channel_id=1, source_target_pairs={{0,4},{1,12},{4,5},{5,13},{8,0},{9,8},{12,1},{13,9},{16,20},{17,28... | collective-permute-start | bytes 1769480 | tf_op jit(solution)/shard_map/ppermute | solution.py:721
  84.1 31.9 %collective-permute-start.17 = (bf16[96,3072]{1,0:T(8,128)(2,1)}, bf16[96,3072]{1,0:T(8,128)(2,1)}, u32[]{:S(2)}, u32[]{:S(2)}) collective-permute-start(bf16[96,3072]{1,0:T(8,128)(2,1)} %get-tuple-element.316), channel_id=1, source_target_pairs={{0,16},{1,24},{4,17},{5,25},{8,20},{9,28},{12,21},{13,29},{16,0},{... | collective-permute-start | bytes 1769480 | tf_op jit(solution)/shard_map/ppermute | solution.py:721
  112.3 89.6 %all-to-all-start = ((bf16[8,2,128,768]{3,2,1,0:T(8,128)(2,1)}), bf16[8,2,128,768]{3,2,1,0:T(8,128)(2,1)S(1)}, u32[]{:S(2)}, u32[]{:S(2)}) async-start(bf16[8,2,128,768]{3,2,1,0:T(8,128)(2,1)} %get-tuple-element.147), calls=%async_computation | async-start | bytes 6291456 | tf_op jit(solution)/shard_map/all_to_all | solution.py:898
  117.5 61.2 %collective-permute-start.20 = (bf16[96,3072]{1,0:T(8,128)(2,1)S(1)}, bf16[96,3072]{1,0:T(8,128)(2,1)S(1)}, u32[]{:S(2)}, u32[]{:S(2)}) collective-permute-start(bf16[96,3072]{1,0:T(8,128)(2,1)S(1)} %get-tuple-element.315), channel_id=1, source_target_pairs={{0,4},{1,12},{4,5},{5,13},{8,0},{9,8},{12,1},{13,9},{16,20},{17,28... | collective-permute-start | bytes 1769480 | tf_op jit(solution)/shard_map/ppermute | solution.py:721
  120.5 70.8 %collective-permute-start.22 = (bf16[96,3072]{1,0:T(8,128)(2,1)S(1)}, bf16[96,3072]{1,0:T(8,128)(2,1)S(1)}, u32[]{:S(2)}, u32[]{:S(2)}) collective-permute-start(bf16[96,3072]{1,0:T(8,128)(2,1)S(1)} %get-tuple-element.314), channel_id=1, source_target_pairs={{0,20},{1,28},{4,21},{5,29},{8,16},{9,24},{12,17},{13,25},{16,4},{... | collective-permute-start | bytes 1769480 | tf_op jit(solution)/shard_map/ppermute | solution.py:721
  121.0 79.0 %collective-permute-start.21 = (bf16[96,3072]{1,0:T(8,128)(2,1)S(1)}, bf16[96,3072]{1,0:T(8,128)(2,1)S(1)}, u32[]{:S(2)}, u32[]{:S(2)}) collective-permute-start(bf16[96,3072]{1,0:T(8,128)(2,1)S(1)} %dynamic-slice_bitcast_fusion.7), channel_id=1, source_target_pairs={{0,20},{1,28},{4,21},{5,29},{8,16},{9,24},{12,17},{13,25},{16,4},{... | collective-permute-start | bytes 1769480 | tf_op jit(solution)/shard_map/ppermute | solution.py:721
  125.2 74.8 %collective-permute-start.18 = (bf16[96,3072]{1,0:T(8,128)(2,1)}, bf16[96,3072]{1,0:T(8,128)(2,1)S(1)}, u32[]{:S(2)}, u32[]{:S(2)}) collective-permute-start(bf16[96,3072]{1,0:T(8,128)(2,1)} %collective-permute-done.13.refs_1_), channel_id=1, source_target_pairs={{0,1},{1,0},{2,3},{3,2},{4,5},{5,4},{6,7},{7,6},{8,9},{9,8},{10,11... | collective-permute-start | bytes 1769480 | tf_op jit(solution)/shard_map/ppermute | solution.py:688
  125.2 74.8 %collective-permute-start.19 = (bf16[96,3072]{1,0:T(8,128)(2,1)}, bf16[96,3072]{1,0:T(8,128)(2,1)S(1)}, u32[]{:S(2)}, u32[]{:S(2)}) collective-permute-start(bf16[96,3072]{1,0:T(8,128)(2,1)} %collective-permute-done.14.refs_2_), channel_id=1, source_target_pairs={{0,1},{1,0},{2,3},{3,2},{4,5},{5,4},{6,7},{7,6},{8,9},{9,8},{10,11... | collective-permute-start | bytes 1769480 | tf_op jit(solution)/shard_map/ppermute | solution.py:688
  203.6 48.4 %all-to-all-start.2 = ((bf16[8,2,128,768]{3,2,1,0:T(8,128)(2,1)}), bf16[8,2,128,768]{3,2,1,0:T(8,128)(2,1)}, u32[]{:S(2)}, u32[]{:S(2)}) async-start(bf16[8,2,128,768]{3,2,1,0:T(8,128)(2,1)} %get-tuple-element.176), calls=%async_computation.2 | async-start | bytes 6291456 | tf_op jit(solution)/shard_map/all_to_all | solution.py:898
  252.0 52.7 %all-to-all-start.1 = ((bf16[8,2,128,768]{3,2,1,0:T(8,128)(2,1)}), bf16[8,2,128,768]{3,2,1,0:T(8,128)(2,1)S(1)}, u32[]{:S(2)}, u32[]{:S(2)}) async-start(bf16[8,2,128,768]{3,2,1,0:T(8,128)(2,1)} %get-tuple-element.175), calls=%async_computation.1 | async-start | bytes 6291456 | tf_op jit(solution)/shard_map/all_to_all | solution.py:904
  306.4 76.0 %all-to-all-start.3 = ((bf16[8,2,128,768]{3,2,1,0:T(8,128)(2,1)}), bf16[8,2,128,768]{3,2,1,0:T(8,128)(2,1)}, u32[]{:S(2)}, u32[]{:S(2)}) async-start(bf16[8,2,128,768]{3,2,1,0:T(8,128)(2,1)} %get-tuple-element.193), calls=%async_computation.3 | async-start | bytes 6291456 | tf_op jit(solution)/shard_map/all_to_all | solution.py:904
  333.6 64.4 %collective-permute-start.29 = (bf16[4,256,768]{2,1,0:T(8,128)(2,1)}, bf16[4,256,768]{2,1,0:T(8,128)(2,1)}, u32[]{:S(2)}, u32[]{:S(2)}) collective-permute-start(bf16[4,256,768]{2,1,0:T(8,128)(2,1)} %dynamic-slice_bitcast_fusion.1), channel_id=1, source_target_pairs={{0,1},{1,0},{2,3},{3,2},{4,5},{5,4},{6,7},{7,6},{8,9},{9,8},{10,11... | collective-permute-start | bytes 4718600 | tf_op jit(solution)/shard_map/ppermute | solution.py:688
  336.6 81.2 %collective-permute-start.30 = (bf16[2,96,2048]{2,1,0:T(8,128)(2,1)}, bf16[2,96,2048]{2,1,0:T(8,128)(2,1)S(1)}, u32[]{:S(2)}, u32[]{:S(2)}) collective-permute-start(bf16[2,96,2048]{2,1,0:T(8,128)(2,1)} %get-tuple-element.305), channel_id=1, source_target_pairs={{0,0},{8,1},{1,4},{9,5},{4,8},{12,9},{5,12},{13,13},{16,16},{24,17... | collective-permute-start | bytes 2359304 | tf_op jit(solution)/shard_map/ppermute | solution.py:813
  340.2 77.7 %collective-permute-start.31 = (bf16[2,96,2048]{2,1,0:T(8,128)(2,1)}, bf16[2,96,2048]{2,1,0:T(8,128)(2,1)S(1)}, u32[]{:S(2)}, u32[]{:S(2)}) collective-permute-start(bf16[2,96,2048]{2,1,0:T(8,128)(2,1)} %get-tuple-element.304), channel_id=1, source_target_pairs={{4,0},{12,1},{5,4},{13,5},{0,8},{8,9},{1,12},{9,13},{20,16},{28,17... | collective-permute-start | bytes 2359304 | tf_op jit(solution)/shard_map/ppermute | solution.py:813
  341.8 76.1 %collective-permute-start.32 = (bf16[2,96,2048]{2,1,0:T(8,128)(2,1)}, bf16[2,96,2048]{2,1,0:T(8,128)(2,1)}, u32[]{:S(2)}, u32[]{:S(2)}) collective-permute-start(bf16[2,96,2048]{2,1,0:T(8,128)(2,1)} %get-tuple-element.303), channel_id=1, source_target_pairs={{16,0},{24,1},{17,4},{25,5},{20,8},{28,9},{21,12},{29,13},{0,16},{... | collective-permute-start | bytes 2359304 | tf_op jit(solution)/shard_map/ppermute | solution.py:813
  347.9 70.0 %collective-permute-start.33 = (bf16[2,96,2048]{2,1,0:T(8,128)(2,1)}, bf16[2,96,2048]{2,1,0:T(8,128)(2,1)}, u32[]{:S(2)}, u32[]{:S(2)}) collective-permute-start(bf16[2,96,2048]{2,1,0:T(8,128)(2,1)} %get-tuple-element.302), channel_id=1, source_target_pairs={{20,0},{28,1},{21,4},{29,5},{16,8},{24,9},{17,12},{25,13},{4,16},{... | collective-permute-start | bytes 2359304 | tf_op jit(solution)/shard_map/ppermute | solution.py:813
  436.1 72.2 %collective-permute-start.44 = (bf16[256,768]{1,0:T(8,128)(2,1)S(1)}, bf16[256,768]{1,0:T(8,128)(2,1)S(1)}, u32[]{:S(2)}, u32[]{:S(2)}) collective-permute-start(bf16[256,768]{1,0:T(8,128)(2,1)S(1)} %get-tuple-element.313), channel_id=1, source_target_pairs={{0,0},{8,1},{1,4},{9,5},{4,8},{12,9},{5,12},{13,13},{16,16},{24,17... | collective-permute-start | bytes 1179656 | tf_op jit(solution)/shard_map/ppermute | solution.py:813
  438.8 69.5 %collective-permute-start.45 = (bf16[256,768]{1,0:T(8,128)(2,1)S(1)}, bf16[256,768]{1,0:T(8,128)(2,1)S(1)}, u32[]{:S(2)}, u32[]{:S(2)}) collective-permute-start(bf16[256,768]{1,0:T(8,128)(2,1)S(1)} %get-tuple-element.312), channel_id=1, source_target_pairs={{16,0},{24,1},{17,4},{25,5},{20,8},{28,9},{21,12},{29,13},{0,16},{... | collective-permute-start | bytes 1179656 | tf_op jit(solution)/shard_map/ppermute | solution.py:813
  488.4 33.0 %collective-permute-start.46 = (bf16[256,768]{1,0:T(8,128)(2,1)S(1)}, bf16[256,768]{1,0:T(8,128)(2,1)S(1)}, u32[]{:S(2)}, u32[]{:S(2)}) collective-permute-start(bf16[256,768]{1,0:T(8,128)(2,1)S(1)} %get-tuple-element.310), channel_id=1, source_target_pairs={{4,0},{12,1},{5,4},{13,5},{0,8},{8,9},{1,12},{9,13},{20,16},{28,17... | collective-permute-start | bytes 1179656 | tf_op jit(solution)/shard_map/ppermute | solution.py:813
  491.1 30.3 %collective-permute-start.47 = (bf16[256,768]{1,0:T(8,128)(2,1)S(1)}, bf16[256,768]{1,0:T(8,128)(2,1)S(1)}, u32[]{:S(2)}, u32[]{:S(2)}) collective-permute-start(bf16[256,768]{1,0:T(8,128)(2,1)S(1)} %get-tuple-element.311), channel_id=1, source_target_pairs={{20,0},{28,1},{21,4},{29,5},{16,8},{24,9},{17,12},{25,13},{4,16},{... | collective-permute-start | bytes 1179656 | tf_op jit(solution)/shard_map/ppermute | solution.py:813
  (63 other events, 782.1 us)

commit v6 on v5

--- a/solution.py
+++ b/solution.py
@@ -913,20 +913,19 @@
             sums = (out_w, small_w, rows_w)
             firsts.append(first)
             if i == parts - 1:
-                held = (down_sums, first[1], [v[3] for v in lasts])
-                down_sums, first[1], _ = lax.optimization_barrier(held)
+                held = (gate_up_got, down_sums, first[1], [v[3] for v in lasts])
+                gate_up_got, down_sums, first[1], _ = lax.optimization_barrier(held)
+                down_got = plan.scatter_send(down_sums, 0)
             lasts.append(attention_back(i, kept[i], first[1], first[3], t, packed, vecs))
             if i == 0:
                 returned[-1], sums, _ = lax.optimization_barrier((returned[-1], sums, lasts[0][3]))
-        held = ([v[2] for v in lasts], gate_up_got, down_sums)
-        acts, gate_up_got, down_sums = lax.optimization_barrier(held)
+        acts = [v[2] for v in lasts]
         halves = mixer_wgrad(
             acts, [v[1] for v in lasts], [v[3] for v in lasts], *sums, *plan.split()
         )
-        down_got = plan.scatter_send(down_sums, 0)
-        near = plan.reduce_first(*halves)
-        total = plan.reduce_last(*near)
+        halves, down_got = lax.optimization_barrier((halves, down_got))
         down_total = plan.scatter_end(down_got, 0)
+        total = plan.reduce_last(*plan.reduce_first(*halves))
         gate_up_total = plan.scatter_end(gate_up_got, 1)
         gate_up_total = jnp.concatenate([gate_up_total[:, 0], gate_up_total[:, 1]], axis=2)
         return (

time: 537 us -> 530 us (0.987)
  waiting for transfers between devices: 122 us -> 115 us
    ppermute x8, starting transfers between devices: 38.1 us -> 29.4 us  [scatter_send(): lax.ppermute(pick(parts, here ^ turn, axis), self.route_axes, back)]
    ppermute x6, waiting for transfers between devices: 4.69 us -> 12.6 us  [along(): lax.ppermute(value, ('half', 'low'), [(i, i ^ turn) for i in range(4)])]
    ppermute x8, waiting for transfers between devices: 13.1 us -> 5.63 us  [scatter_send(): lax.ppermute(pick(parts, here ^ turn, axis), self.route_axes, back)]
    ppermute x26, waiting for transfers between devices: 41.4 us -> 34.4 us  [swap(): return lax.ppermute(value, axis, [(0, 1), (1, 0)])]
    ppermute x26, starting transfers between devices: 25.6 us -> 31.8 us  [swap(): return lax.ppermute(value, axis, [(0, 1), (1, 0)])]
    unnamed x74 -> x100, local copies, waits for them, and re-layouts: 11.2 us -> 13.5 us
  transfers between devices with their start and end apart: 52 -> 52, of which waited for: 18 -> 19; matrix products, arithmetic and copies ran while one was open for 9% -> 8% of each run, Pallas kernels for 38% -> 42%
where the time goes in v6:
time: 530 us; the launch traced here: 519 us
  Pallas kernels  222 us (42%)
  starting transfers between devices  115 us (22%)
  waiting for transfers between devices  115 us (22%)
  local copies, waits for them, and re-layouts  39.7 us (7%)
  other arithmetic  24.7 us (5%)
    ppermute x8, waiting for transfers between devices, send(): return lax.ppermute(mine, self.route_axes, self.routes[turn])  62.3 us
    pallas_call x2, Pallas kernels, expert_rows(): pl.pallas_call(expert_rows_body, grid=(steps,), in_specs=[pl.BlockSpec((n...  57.2 us
    pallas_call x2, Pallas kernels, forward_part(): pl.pallas_call(forward_body, grid=(1,), in_specs=[seq_block(D, part), seq...  40.5 us
    pallas_call x2, Pallas kernels, attention_back(): pl.pallas_call(attention_back_body, grid=(1,), in_specs=[fixed((SEQ, 3 *...  36.2 us
    ppermute x26, waiting for transfers between devices, swap(): return lax.ppermute(value, axis, [(0, 1), (1, 0)])  34.4 us
    ppermute x26, starting transfers between devices, swap(): return lax.ppermute(value, axis, [(0, 1), (1, 0)])  31.8 us
    pallas_call x2, Pallas kernels, combine_part(): pl.pallas_call(body, grid=(2,), in_specs=[fixed((EXPERTS, 2, CAP, D)), ti...  30.1 us
    ppermute x8, starting transfers between devices, scatter_send(): lax.ppermute(pick(parts, here ^ turn, axis), self.route_axes, back)  29.4 us
  transfers between devices with their start and end apart: 52, of which 19 were waited for; matrix products, arithmetic and copies ran while one was open for 8% of the time, Pallas kernels for 42%

profile of v6, /device:TPU:1, one launch (start us, length us, event | category | flops | bytes accessed | tf_op | source)
XLA Modules:
  0.0 519.5 jit_solution(18175382283889792855)
XLA Ops:
  29.2 5.6 %collective-permute-done.3.refs_2_ = bf16[192,1664]{1,0:T(8,128)(2,1)} collective-permute-done((bf16[192,1664]{1,0:T(8,128)(2,1)S(1)}, bf16[192,1664]{1,0:T(8,128)(2,1)}, u32[]{:S(2)}, u32[]{:S(2)}) %collective-permute-start.3) | collective-permute-done | bytes 639008 | tf_op jit(solution)/shard_map/ppermute | solution.py:688
  38.1 7.8 %collective-permute-start.7 = (bf16[192,1664]{1,0:T(8,128)(2,1)S(1)}, bf16[192,1664]{1,0:T(8,128)(2,1)}, u32[]{:S(2)}, u32[]{:S(2)}) collective-permute-start(bf16[192,1664]{1,0:T(8,128)(2,1)S(1)} %pad_maximum_fusion.5.refs_1_), channel_id=1, source_target_pairs={{0,1},{1,0},{2,3},{3,2},{4,5},{5,4},{6,7},{7,6},{8,9},{9,8},{10,11... | collective-permute-start | bytes 1916936 | tf_op jit(solution)/shard_map/ppermute | solution.py:688
  47.4 8.3 %collective-permute-done.12.refs_5_ = bf16[96,3072]{1,0:T(8,128)(2,1)} collective-permute-done((bf16[96,3072]{1,0:T(8,128)(2,1)S(1)}, bf16[96,3072]{1,0:T(8,128)(2,1)}, u32[]{:S(2)}, u32[]{:S(2)}) %collective-permute-start.12) | collective-permute-done | bytes 589856 | tf_op jit(solution)/shard_map/ppermute | solution.py:721
  68.1 5.9 %shard_map.230.w_qkv.w_out.w_small.refs_7_.refs_8_ = bf16[768,3328]{1,0:T(8,128)(2,1)} custom-call(s32[80]{0:T(128)} %stack.300.refs_0_, bf16[192,1664]{1,0:T(8,128)(2,1)} %copy-done.8, bf16[192,1664]{1,0:T(8,128)(2,1)} %collective-permute-done.3.refs_2_, bf16[192,1664]{1,0:T(8,128)(2,1)} %collective-permute-done.4.refs_3_, bf16[192,896]{1,0:T(8,128)(2,1)} %copy-done.38, ...), custom_call_target="tpu_custom_call" | custom-call | flops 1 | tf_op jit(solution)/shard_map/pallas_call | solution.py:646
  84.2 7.3 %collective-permute-start.17 = (bf16[96,3072]{1,0:T(8,128)(2,1)}, bf16[96,3072]{1,0:T(8,128)(2,1)}, u32[]{:S(2)}, u32[]{:S(2)}) collective-permute-start(bf16[96,3072]{1,0:T(8,128)(2,1)} %get-tuple-element.322), channel_id=1, source_target_pairs={{0,16},{1,24},{4,17},{5,25},{8,20},{9,28},{12,21},{13,29},{16,0},{... | collective-permute-start | bytes 1769480 | tf_op jit(solution)/shard_map/ppermute | solution.py:721
  92.1 20.2 %shard_map.231 = (bf16[8,2,128,768]{3,2,1,0:T(8,128)(2,1)}, bf16[512,2304]{1,0:T(8,128)(2,1)}, bf16[512,768]{1,0:T(8,128)(2,1)}, f32[512,768]{1,0:T(8,128)}, f32[16,512]{1,0:T(8,128)}, /*index=5*/f32[512,128]{1,0:T(8,128)}) custom-call(bf16[1024,768]{1,0:T(8,128)(2,1)} %tok.3, bf16[1024,768]{1,0:T(8,128)(2,1)} %cot.2, bf16[1024,128]{1,0:T(8,128)(2,1)} %pad.4.prev, ...), custom_call_target="tpu_custom_call" | custom-call | flops 99999997952 | tf_op jit(solution)/shard_map/pallas_call | solution.py:180
  125.8 20.2 %shard_map.232 = (bf16[8,2,128,768]{3,2,1,0:T(8,128)(2,1)}, bf16[512,2304]{1,0:T(8,128)(2,1)}, bf16[512,768]{1,0:T(8,128)(2,1)}, f32[512,768]{1,0:T(8,128)}, f32[16,512]{1,0:T(8,128)}, /*index=5*/f32[512,128]{1,0:T(8,128)}) custom-call(bf16[1024,768]{1,0:T(8,128)(2,1)} %tok.3, bf16[1024,768]{1,0:T(8,128)(2,1)} %cot.2, bf16[1024,128]{1,0:T(8,128)(2,1)} %pad.4.prev, ...), custom_call_target="tpu_custom_call" | custom-call | flops 99999997952 | tf_op jit(solution)/shard_map/pallas_call | solution.py:180
  146.0 32.6 %collective-permute-done.20.refs_4_ = bf16[96,3072]{1,0:T(8,128)(2,1)S(1)} collective-permute-done((bf16[96,3072]{1,0:T(8,128)(2,1)S(1)}, bf16[96,3072]{1,0:T(8,128)(2,1)S(1)}, u32[]{:S(2)}, u32[]{:S(2)}) %collective-permute-start.20) | collective-permute-done | bytes 589856 | tf_op jit(solution)/shard_map/ppermute | solution.py:721
  178.7 12.6 %collective-permute-done.22.refs_8_ = bf16[96,3072]{1,0:T(8,128)(2,1)S(1)} collective-permute-done((bf16[96,3072]{1,0:T(8,128)(2,1)S(1)}, bf16[96,3072]{1,0:T(8,128)(2,1)S(1)}, u32[]{:S(2)}, u32[]{:S(2)}) %collective-permute-start.22) | collective-permute-done | bytes 589856 | tf_op jit(solution)/shard_map/ppermute | solution.py:721
  191.3 8.7 %collective-permute-done.21.refs_7_ = bf16[96,3072]{1,0:T(8,128)(2,1)S(1)} collective-permute-done((bf16[96,3072]{1,0:T(8,128)(2,1)S(1)}, bf16[96,3072]{1,0:T(8,128)(2,1)S(1)}, u32[]{:S(2)}, u32[]{:S(2)}) %collective-permute-start.21) | collective-permute-done | bytes 589856 | tf_op jit(solution)/shard_map/ppermute | solution.py:721
  214.8 8.6 %shard_map.233 = (bf16[768,4096]{1,0:T(8,128)(2,1)}, bf16[2048,768]{1,0:T(8,128)(2,1)}) custom-call(s32[112]{0:T(128)} %stack.341.refs_0_, bf16[96,3072]{1,0:T(8,128)(2,1)} %collective-permute-done.13.refs_1_, bf16[96,3072]{1,0:T(8,128)(2,1)} %collective-permute-done.14.refs_2_, bf16[96,3072]{1,0:T(8,128)(2,1)} %collective-permute-done.15.refs_3_, ...), custom_call_target="tpu_custom_call" | custom-call | flops 1 | tf_op jit(solution)/shard_map/pallas_call | solution.py:646
  223.4 28.6 %shard_map.234 = (bf16[1024,2048]{1,0:T(8,128)(2,1)}, bf16[1024,2048]{1,0:T(8,128)(2,1)}, bf16[1024,2048]{1,0:T(8,128)(2,1)}, bf16[8,2,128,768]{3,2,1,0:T(8,128)(2,1)}) custom-call(bf16[8,2,128,768]{3,2,1,0:T(8,128)(2,1)} %copy-done, bf16[8,2,128,768]{3,2,1,0:T(8,128)(2,1)} %copy-done, bf16[768,4096]{1,0:T(8,128)(2,1)} %get-tuple-element.176.wg_ref.wu_ref, ...), custom_call_target="tpu_custom_call" | custom-call | flops 28000000000 | tf_op jit(solution)/shard_map/pallas_call | solution.py:553
  257.1 28.6 %shard_map.235 = (bf16[1024,2048]{1,0:T(8,128)(2,1)}, bf16[1024,2048]{1,0:T(8,128)(2,1)}, bf16[1024,2048]{1,0:T(8,128)(2,1)}, bf16[8,2,128,768]{3,2,1,0:T(8,128)(2,1)}) custom-call(bf16[8,2,128,768]{3,2,1,0:T(8,128)(2,1)} %all-to-all-done.2.x_ref.g_ref.refs_1_.refs_3_, bf16[8,2,128,768]{3,2,1,0:T(8,128)(2,1)} %all-to-all-done.2.x_ref.g_ref.refs_1_.refs_3_, ...), custom_call_target="tpu_custom_call" | custom-call | flops 28000000000 | tf_op jit(solution)/shard_map/pallas_call | solution.py:553
  285.7 19.2 %shard_map.236 = bf16[2,768,2048]{2,1,0:T(8,128)(2,1)} custom-call(bf16[8,2,128,768]{3,2,1,0:T(8,128)(2,1)} %copy-done, bf16[8,2,128,768]{3,2,1,0:T(8,128)(2,1)} %all-to-all-done.2.x_ref.g_ref.refs_1_.refs_3_, bf16[1024,2048]{1,0:T(8,128)(2,1)} %get-tuple-element.183.refs_2_, bf16[1024,2048]{1,0:T(8,128)(2,1)} %get-tuple-element.184.refs_3_, ...), custom_call_target="tpu_custom_call" | custom-call | flops 1 | tf_op jit(solution)/shard_map/pallas_call | solution.py:612
  316.4 11.0 %shard_map.237 = bf16[2048,768]{1,0:T(8,128)(2,1)} custom-call(bf16[1024,2048]{1,0:T(8,128)(2,1)} %get-tuple-element.188.refs_0_, bf16[1024,2048]{1,0:T(8,128)(2,1)} %get-tuple-element.189.refs_1_, bf16[8,2,128,768]{3,2,1,0:T(8,128)(2,1)} %copy-done, bf16[8,2,128,768]{3,2,1,0:T(8,128)(2,1)} %all-to-all-done.2.x_ref.g_ref.refs_1_.refs_3_), custom_call_target="tpu_custom_call" | custom-call | flops 10000000000 | tf_op jit(solution)/shard_map/pallas_call | solution.py:584
  341.9 6.1 %collective-permute-start.31 = (bf16[2,96,2048]{2,1,0:T(8,128)(2,1)}, bf16[2,96,2048]{2,1,0:T(8,128)(2,1)S(1)}, u32[]{:S(2)}, u32[]{:S(2)}) collective-permute-start(bf16[2,96,2048]{2,1,0:T(8,128)(2,1)} %get-tuple-element.309), channel_id=1, source_target_pairs={{16,0},{24,1},{17,4},{25,5},{20,8},{28,9},{21,12},{29,13},{0,16},{... | collective-permute-start | bytes 2359304 | tf_op jit(solution)/shard_map/ppermute | solution.py:813
  350.1 14.4 %shard_map.238 = (bf16[512,768]{1,0:T(8,128)(2,1)}, f32[512,768]{1,0:T(8,128)}, f32[512,12]{1,0:T(8,128)}, bf16[512,768]{1,0:T(8,128)(2,1)}, f32[768,768]{1,0:T(...) custom-call(bf16[8,2,128,768]{3,2,1,0:T(8,128)(2,1)} %copy-done.1, f32[512,768]{1,0:T(8,128)} %get-tuple-element.191.refs_1_, ...), custom_call_target="tpu_custom_call" | custom-call | flops 1 | tf_op jit(solution)/shard_map/pallas_call | solution.py:311
  364.5 18.0 %shard_map.239 = (f32[512,768]{1,0:T(8,128)}, bf16[512,2304]{1,0:T(8,128)(2,1)}, bf16[512,768]{1,0:T(8,128)(2,1)}, f32[8,768]{1,0:T(8,128)}) custom-call(bf16[512,2304]{1,0:T(8,128)(2,1)} %get-tuple-element.200.qkv, bf16[512,768]{1,0:T(8,128)(2,1)} %get-tuple-element.201.agrad, f32[16,512]{1,0:T(8,128)} %get-tuple-element.202.lse, s32[1024,1]{1,0:T(8,128)} %copy.159.seg_col, ...), custom_call_target="tpu_custom_call" | custom-call | flops 1 | tf_op jit(solution)/shard_map/pallas_call | solution.py:400
  382.5 15.6 %shard_map.240 = (bf16[512,768]{1,0:T(8,128)(2,1)}, f32[512,768]{1,0:T(8,128)}, f32[512,12]{1,0:T(8,128)}, bf16[512,768]{1,0:T(8,128)(2,1)}, f32[768,768]{1,0:T(...) custom-call(bf16[8,2,128,768]{3,2,1,0:T(8,128)(2,1)} %all-to-all-done.3.back, f32[512,768]{1,0:T(8,128)} %get-tuple-element.206.resid, ...), custom_call_target="tpu_custom_call" | custom-call | flops 1 | tf_op jit(solution)/shard_map/pallas_call | solution.py:311
  407.0 13.0 %collective-permute-start.34 = (bf16[256,768]{1,0:T(8,128)(2,1)S(1)}, bf16[256,768]{1,0:T(8,128)(2,1)S(1)}, u32[]{:S(2)}, u32[]{:S(2)}) collective-permute-start(bf16[256,768]{1,0:T(8,128)(2,1)S(1)} %get-tuple-element.319), channel_id=1, source_target_pairs={{0,0},{8,1},{1,4},{9,5},{4,8},{12,9},{5,12},{13,13},{16,16},{24,17... | collective-permute-start | bytes 1179656 | tf_op jit(solution)/shard_map/ppermute | solution.py:813
  424.1 18.2 %shard_map.241 = (f32[512,768]{1,0:T(8,128)}, bf16[512,2304]{1,0:T(8,128)(2,1)}, bf16[512,768]{1,0:T(8,128)(2,1)}, f32[8,768]{1,0:T(8,128)}) custom-call(bf16[512,2304]{1,0:T(8,128)(2,1)} %get-tuple-element.214.qkv, bf16[512,768]{1,0:T(8,128)(2,1)} %get-tuple-element.215.agrad, f32[16,512]{1,0:T(8,128)} %get-tuple-element.216.lse, s32[1024,1]{1,0:T(8,128)} %copy.159.seg_col, ...), custom_call_target="tpu_custom_call" | custom-call | flops 1 | tf_op jit(solution)/shard_map/pallas_call | solution.py:400
  442.3 13.6 %shard_map.242 = (bf16[384,3328]{1,0:T(8,128)(2,1)}, bf16[384,3328]{1,0:T(8,128)(2,1)}) custom-call(s32[1]{0:T(128)} %bitcast.84.refs_0_, bf16[512,768]{1,0:T(8,128)(2,1)} %get-tuple-element.224.refs_1_, bf16[512,768]{1,0:T(8,128)(2,1)} %get-tuple-element.225.refs_2_, bf16[512,2304]{1,0:T(8,128)(2,1)} %get-tuple-element.226.refs_3_, ...), custom_call_target="tpu_custom_call" | custom-call | flops 1 | tf_op jit(solution)/shard_map/pallas_call | solution.py:470
  467.5 11.5 %collective-permute-done.41 = bf16[4,48,1536]{2,1,0:T(8,128)(2,1)S(1)} collective-permute-done((bf16[4,48,1536]{2,1,0:T(8,128)(2,1)S(1)}, bf16[4,48,1536]{2,1,0:T(8,128)(2,1)S(1)}, u32[]{:S(2)}, u32[]{:S(2)}) %collective-permute-start.41) | collective-permute-done | bytes 589856 | tf_op jit(solution)/shard_map/ppermute | solution.py:688
  496.9 8.7 %collective-permute-done.44 = bf16[48,1664]{1,0:T(8,128)(2,1)S(1)} collective-permute-done((bf16[48,1664]{1,0:T(8,128)(2,1)S(1)}, bf16[48,1664]{1,0:T(8,128)(2,1)S(1)}, u32[]{:S(2)}, u32[]{:S(2)}) %collective-permute-start.44) | collective-permute-done | bytes 159776 | tf_op jit(solution)/shard_map/ppermute | solution.py:692
  (274 shorter events, 173.1 us)
Async XLA Ops:
  23.6 32.0 %collective-permute-start.12 = (bf16[96,3072]{1,0:T(8,128)(2,1)S(1)}, bf16[96,3072]{1,0:T(8,128)(2,1)}, u32[]{:S(2)}, u32[]{:S(2)}) collective-permute-start(bf16[96,3072]{1,0:T(8,128)(2,1)S(1)} %dynamic-slice_bitcast_fusion.13), channel_id=1, source_target_pairs={{0,16},{1,24},{4,17},{5,25},{8,20},{9,28},{12,21},{13,29},{16,0},{... | collective-permute-start | bytes 1769480 | tf_op jit(solution)/shard_map/ppermute | solution.py:721
  38.1 30.0 %collective-permute-start.7 = (bf16[192,1664]{1,0:T(8,128)(2,1)S(1)}, bf16[192,1664]{1,0:T(8,128)(2,1)}, u32[]{:S(2)}, u32[]{:S(2)}) collective-permute-start(bf16[192,1664]{1,0:T(8,128)(2,1)S(1)} %pad_maximum_fusion.5.refs_1_), channel_id=1, source_target_pairs={{0,1},{1,0},{2,3},{3,2},{4,5},{5,4},{6,7},{7,6},{8,9},{9,8},{10,11... | collective-permute-start | bytes 1916936 | tf_op jit(solution)/shard_map/ppermute | solution.py:688
  76.3 39.8 %collective-permute-start.13 = (bf16[96,3072]{1,0:T(8,128)(2,1)}, bf16[96,3072]{1,0:T(8,128)(2,1)}, u32[]{:S(2)}, u32[]{:S(2)}) collective-permute-start(bf16[96,3072]{1,0:T(8,128)(2,1)} %get-tuple-element.325), channel_id=1, source_target_pairs={{0,0},{1,8},{4,1},{5,9},{8,4},{9,12},{12,5},{13,13},{16,16},{17,24... | collective-permute-start | bytes 1769480 | tf_op jit(solution)/shard_map/ppermute | solution.py:721
  79.4 36.6 %collective-permute-start.14 = (bf16[96,3072]{1,0:T(8,128)(2,1)}, bf16[96,3072]{1,0:T(8,128)(2,1)}, u32[]{:S(2)}, u32[]{:S(2)}) collective-permute-start(bf16[96,3072]{1,0:T(8,128)(2,1)} %get-tuple-element.323), channel_id=1, source_target_pairs={{0,0},{1,8},{4,1},{5,9},{8,4},{9,12},{12,5},{13,13},{16,16},{17,24... | collective-permute-start | bytes 1769480 | tf_op jit(solution)/shard_map/ppermute | solution.py:721
  82.6 33.5 %collective-permute-start.15 = (bf16[96,3072]{1,0:T(8,128)(2,1)}, bf16[96,3072]{1,0:T(8,128)(2,1)}, u32[]{:S(2)}, u32[]{:S(2)}) collective-permute-start(bf16[96,3072]{1,0:T(8,128)(2,1)} %get-tuple-element.324), channel_id=1, source_target_pairs={{0,4},{1,12},{4,5},{5,13},{8,0},{9,8},{12,1},{13,9},{16,20},{17,28... | collective-permute-start | bytes 1769480 | tf_op jit(solution)/shard_map/ppermute | solution.py:721
  84.2 31.9 %collective-permute-start.17 = (bf16[96,3072]{1,0:T(8,128)(2,1)}, bf16[96,3072]{1,0:T(8,128)(2,1)}, u32[]{:S(2)}, u32[]{:S(2)}) collective-permute-start(bf16[96,3072]{1,0:T(8,128)(2,1)} %get-tuple-element.322), channel_id=1, source_target_pairs={{0,16},{1,24},{4,17},{5,25},{8,20},{9,28},{12,21},{13,29},{16,0},{... | collective-permute-start | bytes 1769480 | tf_op jit(solution)/shard_map/ppermute | solution.py:721
  112.4 89.5 %all-to-all-start = ((bf16[8,2,128,768]{3,2,1,0:T(8,128)(2,1)}), bf16[8,2,128,768]{3,2,1,0:T(8,128)(2,1)S(1)}, u32[]{:S(2)}, u32[]{:S(2)}) async-start(bf16[8,2,128,768]{3,2,1,0:T(8,128)(2,1)} %get-tuple-element.150), calls=%async_computation | async-start | bytes 6291456 | tf_op jit(solution)/shard_map/all_to_all | solution.py:898
  117.5 61.1 %collective-permute-start.20 = (bf16[96,3072]{1,0:T(8,128)(2,1)S(1)}, bf16[96,3072]{1,0:T(8,128)(2,1)S(1)}, u32[]{:S(2)}, u32[]{:S(2)}) collective-permute-start(bf16[96,3072]{1,0:T(8,128)(2,1)S(1)} %get-tuple-element.321), channel_id=1, source_target_pairs={{0,4},{1,12},{4,5},{5,13},{8,0},{9,8},{12,1},{13,9},{16,20},{17,28... | collective-permute-start | bytes 1769480 | tf_op jit(solution)/shard_map/ppermute | solution.py:721
  120.5 70.8 %collective-permute-start.22 = (bf16[96,3072]{1,0:T(8,128)(2,1)S(1)}, bf16[96,3072]{1,0:T(8,128)(2,1)S(1)}, u32[]{:S(2)}, u32[]{:S(2)}) collective-permute-start(bf16[96,3072]{1,0:T(8,128)(2,1)S(1)} %get-tuple-element.320), channel_id=1, source_target_pairs={{0,20},{1,28},{4,21},{5,29},{8,16},{9,24},{12,17},{13,25},{16,4},{... | collective-permute-start | bytes 1769480 | tf_op jit(solution)/shard_map/ppermute | solution.py:721
  121.1 79.0 %collective-permute-start.21 = (bf16[96,3072]{1,0:T(8,128)(2,1)S(1)}, bf16[96,3072]{1,0:T(8,128)(2,1)S(1)}, u32[]{:S(2)}, u32[]{:S(2)}) collective-permute-start(bf16[96,3072]{1,0:T(8,128)(2,1)S(1)} %dynamic-slice_bitcast_fusion.7), channel_id=1, source_target_pairs={{0,20},{1,28},{4,21},{5,29},{8,16},{9,24},{12,17},{13,25},{16,4},{... | collective-permute-start | bytes 1769480 | tf_op jit(solution)/shard_map/ppermute | solution.py:721
  125.3 74.8 %collective-permute-start.18 = (bf16[96,3072]{1,0:T(8,128)(2,1)}, bf16[96,3072]{1,0:T(8,128)(2,1)S(1)}, u32[]{:S(2)}, u32[]{:S(2)}) collective-permute-start(bf16[96,3072]{1,0:T(8,128)(2,1)} %collective-permute-done.13.refs_1_), channel_id=1, source_target_pairs={{0,1},{1,0},{2,3},{3,2},{4,5},{5,4},{6,7},{7,6},{8,9},{9,8},{10,11... | collective-permute-start | bytes 1769480 | tf_op jit(solution)/shard_map/ppermute | solution.py:688
  125.3 74.8 %collective-permute-start.19 = (bf16[96,3072]{1,0:T(8,128)(2,1)}, bf16[96,3072]{1,0:T(8,128)(2,1)S(1)}, u32[]{:S(2)}, u32[]{:S(2)}) collective-permute-start(bf16[96,3072]{1,0:T(8,128)(2,1)} %collective-permute-done.14.refs_2_), channel_id=1, source_target_pairs={{0,1},{1,0},{2,3},{3,2},{4,5},{5,4},{6,7},{7,6},{8,9},{9,8},{10,11... | collective-permute-start | bytes 1769480 | tf_op jit(solution)/shard_map/ppermute | solution.py:688
  203.6 48.5 %all-to-all-start.2 = ((bf16[8,2,128,768]{3,2,1,0:T(8,128)(2,1)}), bf16[8,2,128,768]{3,2,1,0:T(8,128)(2,1)}, u32[]{:S(2)}, u32[]{:S(2)}) async-start(bf16[8,2,128,768]{3,2,1,0:T(8,128)(2,1)} %get-tuple-element.179), calls=%async_computation.2 | async-start | bytes 6291456 | tf_op jit(solution)/shard_map/all_to_all | solution.py:898
  252.1 52.8 %all-to-all-start.1 = ((bf16[8,2,128,768]{3,2,1,0:T(8,128)(2,1)}), bf16[8,2,128,768]{3,2,1,0:T(8,128)(2,1)S(1)}, u32[]{:S(2)}, u32[]{:S(2)}) async-start(bf16[8,2,128,768]{3,2,1,0:T(8,128)(2,1)} %get-tuple-element.178), calls=%async_computation.1 | async-start | bytes 6291456 | tf_op jit(solution)/shard_map/all_to_all | solution.py:904
  306.5 76.0 %all-to-all-start.3 = ((bf16[8,2,128,768]{3,2,1,0:T(8,128)(2,1)}), bf16[8,2,128,768]{3,2,1,0:T(8,128)(2,1)}, u32[]{:S(2)}, u32[]{:S(2)}) async-start(bf16[8,2,128,768]{3,2,1,0:T(8,128)(2,1)} %get-tuple-element.196), calls=%async_computation.3 | async-start | bytes 6291456 | tf_op jit(solution)/shard_map/all_to_all | solution.py:904
  333.8 64.4 %collective-permute-start.33 = (bf16[4,256,768]{2,1,0:T(8,128)(2,1)}, bf16[4,256,768]{2,1,0:T(8,128)(2,1)}, u32[]{:S(2)}, u32[]{:S(2)}) collective-permute-start(bf16[4,256,768]{2,1,0:T(8,128)(2,1)} %dynamic-slice_bitcast_fusion.1), channel_id=1, source_target_pairs={{0,1},{1,0},{2,3},{3,2},{4,5},{5,4},{6,7},{7,6},{8,9},{9,8},{10,11... | collective-permute-start | bytes 4718600 | tf_op jit(solution)/shard_map/ppermute | solution.py:688
  336.7 68.9 %collective-permute-start.29 = (bf16[2,96,2048]{2,1,0:T(8,128)(2,1)}, bf16[2,96,2048]{2,1,0:T(8,128)(2,1)S(1)}, u32[]{:S(2)}, u32[]{:S(2)}) collective-permute-start(bf16[2,96,2048]{2,1,0:T(8,128)(2,1)} %get-tuple-element.311), channel_id=1, source_target_pairs={{0,0},{8,1},{1,4},{9,5},{4,8},{12,9},{5,12},{13,13},{16,16},{24,17... | collective-permute-start | bytes 2359304 | tf_op jit(solution)/shard_map/ppermute | solution.py:813
  340.2 65.3 %collective-permute-start.30 = (bf16[2,96,2048]{2,1,0:T(8,128)(2,1)}, bf16[2,96,2048]{2,1,0:T(8,128)(2,1)S(1)}, u32[]{:S(2)}, u32[]{:S(2)}) collective-permute-start(bf16[2,96,2048]{2,1,0:T(8,128)(2,1)} %get-tuple-element.310), channel_id=1, source_target_pairs={{4,0},{12,1},{5,4},{13,5},{0,8},{8,9},{1,12},{9,13},{20,16},{28,17... | collective-permute-start | bytes 2359304 | tf_op jit(solution)/shard_map/ppermute | solution.py:813
  341.9 63.7 %collective-permute-start.31 = (bf16[2,96,2048]{2,1,0:T(8,128)(2,1)}, bf16[2,96,2048]{2,1,0:T(8,128)(2,1)S(1)}, u32[]{:S(2)}, u32[]{:S(2)}) collective-permute-start(bf16[2,96,2048]{2,1,0:T(8,128)(2,1)} %get-tuple-element.309), channel_id=1, source_target_pairs={{16,0},{24,1},{17,4},{25,5},{20,8},{28,9},{21,12},{29,13},{0,16},{... | collective-permute-start | bytes 2359304 | tf_op jit(solution)/shard_map/ppermute | solution.py:813
  347.9 57.7 %collective-permute-start.32 = (bf16[2,96,2048]{2,1,0:T(8,128)(2,1)}, bf16[2,96,2048]{2,1,0:T(8,128)(2,1)S(1)}, u32[]{:S(2)}, u32[]{:S(2)}) collective-permute-start(bf16[2,96,2048]{2,1,0:T(8,128)(2,1)} %get-tuple-element.308), channel_id=1, source_target_pairs={{20,0},{28,1},{21,4},{29,5},{16,8},{24,9},{17,12},{25,13},{4,16},{... | collective-permute-start | bytes 2359304 | tf_op jit(solution)/shard_map/ppermute | solution.py:813
  407.0 48.9 %collective-permute-start.34 = (bf16[256,768]{1,0:T(8,128)(2,1)S(1)}, bf16[256,768]{1,0:T(8,128)(2,1)S(1)}, u32[]{:S(2)}, u32[]{:S(2)}) collective-permute-start(bf16[256,768]{1,0:T(8,128)(2,1)S(1)} %get-tuple-element.319), channel_id=1, source_target_pairs={{0,0},{8,1},{1,4},{9,5},{4,8},{12,9},{5,12},{13,13},{16,16},{24,17... | collective-permute-start | bytes 1179656 | tf_op jit(solution)/shard_map/ppermute | solution.py:813
  419.9 36.0 %collective-permute-start.35 = (bf16[256,768]{1,0:T(8,128)(2,1)S(1)}, bf16[256,768]{1,0:T(8,128)(2,1)S(1)}, u32[]{:S(2)}, u32[]{:S(2)}) collective-permute-start(bf16[256,768]{1,0:T(8,128)(2,1)S(1)} %get-tuple-element.318), channel_id=1, source_target_pairs={{4,0},{12,1},{5,4},{13,5},{0,8},{8,9},{1,12},{9,13},{20,16},{28,17... | collective-permute-start | bytes 1179656 | tf_op jit(solution)/shard_map/ppermute | solution.py:813
  420.6 35.3 %collective-permute-start.36 = (bf16[256,768]{1,0:T(8,128)(2,1)S(1)}, bf16[256,768]{1,0:T(8,128)(2,1)S(1)}, u32[]{:S(2)}, u32[]{:S(2)}) collective-permute-start(bf16[256,768]{1,0:T(8,128)(2,1)S(1)} %get-tuple-element.317), channel_id=1, source_target_pairs={{16,0},{24,1},{17,4},{25,5},{20,8},{28,9},{21,12},{29,13},{0,16},{... | collective-permute-start | bytes 1179656 | tf_op jit(solution)/shard_map/ppermute | solution.py:813
  420.6 35.3 %collective-permute-start.37 = (bf16[256,768]{1,0:T(8,128)(2,1)S(1)}, bf16[256,768]{1,0:T(8,128)(2,1)S(1)}, u32[]{:S(2)}, u32[]{:S(2)}) collective-permute-start(bf16[256,768]{1,0:T(8,128)(2,1)S(1)} %get-tuple-element.316), channel_id=1, source_target_pairs={{20,0},{28,1},{21,4},{29,5},{16,8},{24,9},{17,12},{25,13},{4,16},{... | collective-permute-start | bytes 1179656 | tf_op jit(solution)/shard_map/ppermute | solution.py:813
  (76 other events, 759.8 us)
